TPU v7x, 256 devices: a whole 4x4x8 slice. The times are simulated.
256 devices in a mesh: ctx: 64 (over x_lo, z, y), tp: 4 (over x_hi, core).
Axes of the slice: x: 4 (x_hi: 2, x_lo: 2; x = x_hi * 2 + x_lo), y: 4, z: 8, core: 2. Of those that a mesh axis runs over, the one named last changes fastest.
Arguments:
- queries: bfloat16 [8192, 4096], P('ctx', 'tp'), may hold values from -64 to 64
- keys: bfloat16 [8192, 1024], P('ctx', 'tp'), may hold values from -4 to 4
- values: bfloat16 [8192, 1024], P('ctx', 'tp'), may hold values from -6 to 6
- grad_out: bfloat16 [8192, 4096], P('ctx', 'tp'), may hold values from -6 to 6
- out_weight: bfloat16 [4096, 4096], P(None, 'tp'), may hold values from -0.09375 to 0.09375
- segments: int32 [8192], P('ctx'), may hold values from 0 to 1, as said below
Outputs:
- query_grad: bfloat16 [8192, 4096], P('ctx', 'tp')
- key_gradient: bfloat16 [8192, 1024], P('ctx', 'tp')
- value_gradient: bfloat16 [8192, 1024], P('ctx', 'tp')
Inputs may be any that keep to these rules, and one draw needn't show every extreme that they name: `segments`: document numbers never fall along the tokens, start at 0, and every document starts at a multiple of 8 tokens; there are exactly 2 documents.
All inputs are finite; a program needn't handle non-finite values.
Results may differ from a plain program's by a relative error of at most 0.015.
Values may be sent and summed in bfloat16 or wider, within the bound.
No kernel may reach another device: no remote copies, remote signals or barrier semaphores. Data moves between devices by JAX's collectives and lax.ppermute only.
A program may use at most 128 MiB of HBM per device.

v0:
```python
import functools
import math

import jax
import jax.numpy as jnp
from jax import lax
from jax.experimental import pallas as pl
from jax.experimental.pallas import tpu as pltpu
from jax.sharding import Mesh, PartitionSpec as P

HEAD = 128
RATIO = 4
CHUNK = 128
XL, NZ, NY = 2, 8, 4
PIECE = CHUNK + 16
KEYS = NZ * CHUNK
KT = 256
GROUP = RATIO * HEAD
DP = 4
ROWS = DP * GROUP
BLOCKS = 2 * NY // DP
SCALE = HEAD**-0.5
C2 = SCALE * math.log2(math.e)
NEG = -1e30
WIDE = jnp.float32
LOW = jnp.bfloat16
NT = (((1,), (1,)), ((), ()))
NN = (((1,), (0,)), ((), ()))
MIB = 1024 * 1024


def dot(a, b, dims=NN):
    return lax.dot_general(a, b, dims, preferred_element_type=WIDE)


def vspec():
    return pl.BlockSpec(memory_space=pltpu.VMEM)


def hspec():
    return pl.BlockSpec(memory_space=pltpu.HBM)


def in_hbm(x):
    return pltpu.with_memory_space_constraint(x, pltpu.HBM)


def sspec():
    return pl.BlockSpec(memory_space=pltpu.SMEM)


def params(mib):
    return pltpu.CompilerParams(vmem_limit_bytes=mib * MIB)


def prepare(scalars, queries, keys, values, segments):
    def kernel(sc, q_ref, k_ref, v_ref, seg_ref, q_own, q_oth, kv_own, kv_oth, seg, sems):
        xl = sc[0]
        top = pl.ds(0, CHUNK)
        copies = [pltpu.make_async_copy(seg_ref, seg, sems.at[0])]
        for i, (g, q, kv) in enumerate(((1 - xl, q_oth, kv_oth), (xl, q_own, kv_own))):
            at = pl.ds(pl.multiple_of(g * GROUP, GROUP), GROUP)
            copies.append(
                pltpu.make_async_copy(q_ref.at[:, at], q.at[top], sems.at[3 * i + 1])
            )
            at = pl.ds(pl.multiple_of(g * HEAD, HEAD), HEAD)
            for j, ref in enumerate((k_ref, v_ref)):
                copies.append(
                    pltpu.make_async_copy(
                        ref.at[:, at],
                        kv.at[top, pl.ds(j * HEAD, HEAD)],
                        sems.at[3 * i + 2 + j],
                    )
                )
        for copy in copies:
            copy.start()
        copies[0].wait()
        count = jnp.sum(jnp.where(seg[...] == 0, 1.0, 0.0), axis=1, keepdims=True)
        count = jnp.broadcast_to(count, (16, HEAD)).astype(LOW)
        for q, kv in ((q_own, kv_own), (q_oth, kv_oth)):
            q[CHUNK:PIECE, :] = jnp.concatenate([count] * RATIO, axis=1)
            kv[CHUNK:PIECE, :] = jnp.concatenate([count] * 2, axis=1)
        for copy in copies[1:]:
            copy.wait()

    return pl.pallas_call(
        kernel,
        in_specs=[sspec()] + [hspec()] * 4,
        out_specs=[vspec()] * 4,
        out_shape=[
            jax.ShapeDtypeStruct((2 * PIECE, GROUP), LOW),
            jax.ShapeDtypeStruct((PIECE, GROUP), LOW),
            jax.ShapeDtypeStruct((2 * PIECE, 2 * HEAD), LOW),
            jax.ShapeDtypeStruct((PIECE, 2 * HEAD), LOW),
        ],
        scratch_shapes=[pltpu.VMEM((1, CHUNK), jnp.int32), pltpu.SemaphoreType.DMA((7,))],
        compiler_params=params(8),
        name="prepare",
    )(scalars, *[in_hbm(x) for x in (queries, keys, values, segments.reshape(1, CHUNK))])


def stage(weight, grad):
    def kernel(w_hbm, g_hbm, w_ref, g_ref, sems):
        copies = [
            pltpu.make_async_copy(w_hbm, w_ref, sems.at[0]),
            pltpu.make_async_copy(g_hbm, g_ref, sems.at[1]),
        ]
        for copy in copies:
            copy.start()
        for copy in copies:
            copy.wait()

    return pl.pallas_call(
        kernel,
        in_specs=[hspec()] * 2,
        out_specs=[vspec()] * 2,
        out_shape=[jax.ShapeDtypeStruct(x.shape, x.dtype) for x in (weight, grad)],
        scratch_shapes=[pltpu.SemaphoreType.DMA((2,))],
        compiler_params=params(12),
        name="stage",
    )(in_hbm(weight), in_hbm(grad))


def upstream(scalars, grads, weight):
    rows, depth = grads[0].shape
    width = weight.shape[1]

    def kernel(sc, *refs):
        gs = refs[:4]
        w_ref, own_ref, oth_ref, acc = refs[4:]
        xl, tp = sc[0], sc[3]
        for i in range(4):
            start = pl.multiple_of(jnp.bitwise_xor(tp, i) * depth, depth)
            term = dot(gs[i][...], w_ref[pl.ds(start, depth), :])
            acc[...] = term if i == 0 else acc[...] + term
        for g, out in ((1 - xl, oth_ref), (xl, own_ref)):
            at = pl.ds(pl.multiple_of(g * GROUP, GROUP), GROUP)
            out[:rows, :] = acc[:, at].astype(LOW)

    return pl.pallas_call(
        kernel,
        in_specs=[sspec()] + [vspec()] * 5,
        out_specs=[vspec()] * 2,
        out_shape=[
            jax.ShapeDtypeStruct((2 * rows, GROUP), LOW),
            jax.ShapeDtypeStruct((rows, GROUP), LOW),
        ],
        scratch_shapes=[pltpu.VMEM((rows, width), WIDE)],
        compiler_params=params(16),
        name="upstream",
    )(scalars, *grads, weight)


def place(o, dy):
    return o * (NY // DP) + dy // DP, (dy % DP) * GROUP


def stack_rows(dst, blocks, step):
    for o in range(2):
        for dy in range(NY):
            block, first = place(o, dy)
            for h in range(RATIO):
                start = first + h * CHUNK
                dst[block, start : start + CHUNK, :] = blocks[dy][
                    o * step : o * step + CHUNK, h * HEAD : (h + 1) * HEAD
                ]


def key_chunk(xl, z, o, d):
    half = xl if o == 0 else 1 - xl
    return half * 4 + lax.rem(z + d, NZ) // 2


def count_row(ref, first):
    return ref[first + CHUNK : first + PIECE, :HEAD].astype(WIDE)[:1]


def fill_low(low_s, q, views):
    zeros = sum(count_row(ref, first + o * PIECE) for ref, first in views for o in range(2))
    tok = lax.broadcasted_iota(jnp.int32, (1, CHUNK), 1).astype(WIDE)
    for o in range(2):
        for dy in range(NY):
            low = jnp.where(tok >= count_row(q[dy], o * PIECE), zeros, 0.0)
            block, first = place(o, dy)
            for h in range(RATIO):
                start = first + h * CHUNK
                low_s[block : block + 1, start : start + CHUNK] = low


def limits(cls, block, xl, z, y, low_s):
    o = block // (NY // DP)
    h = jnp.where(o == 0, xl, 1 - xl)
    plane = z
    dy0 = lax.rem(block, NY // DP) * DP
    ys = [lax.rem(y + dy0 + i, NY) for i in range(DP)]
    parity = lax.rem(plane + cls, 2)
    full = h * (KEYS // 2) + ((plane + 1 - parity) // 2) * CHUNK
    if cls == 0:
        lane = lax.broadcasted_iota(jnp.int32, (1, ROWS), 1)
        yy = jnp.full((1, ROWS), ys[-1], jnp.int32)
        for i in reversed(range(DP - 1)):
            yy = jnp.where(lane < (i + 1) * GROUP, ys[i], yy)
        off = (yy - y) * CHUNK + jnp.bitwise_and(lane, CHUNK - 1)
        high = full + jnp.clip(off + 1, 0, CHUNK)
        top = full + jnp.where(functools.reduce(jnp.maximum, ys) >= y, CHUNK, 0)
    else:
        high = jnp.full((1, ROWS), full, jnp.int32)
        top = full
    low_f = low_s[pl.ds(block, 1), :]
    low = low_f.astype(jnp.int32)
    t_low = jnp.min(low_f).astype(jnp.int32) // KT
    t_high = (top + KT - 1) // KT
    return low, high, t_low, t_high, jnp.max(low_f).astype(jnp.int32), full


def over_tiles(lim, body):
    low, high, t_low, t_high, max_low, full = lim

    def mask(t, s):
        kk = t * KT + lax.broadcasted_iota(jnp.int32, (KT, ROWS), 0)
        return jnp.where((kk >= low) & (kk < high), s, NEG)

    def step(t, _):
        inside = (t * KT >= max_low) & ((t + 1) * KT <= full)

        @pl.when(inside)
        def _():
            body(t, lambda s: s)

        @pl.when(jnp.logical_not(inside))
        def _():
            body(t, functools.partial(mask, t))

        return 0

    lax.fori_loop(t_low, t_high, step, 0)


def forward(scalars, q_blocks, arrays, views):
    def kernel(sc, *refs):
        q = refs[0:4]
        kv = refs[4 : 4 + len(arrays)]
        o_ref, ml_ref, qs, kc, vt, low_s = refs[4 + len(arrays) :]
        xl, z, y = sc[0], sc[1], sc[2]
        stack_rows(qs, q, PIECE)
        for cls in range(2):
            here = [(kv[a], first) for a, first in views[cls]]
            fill_low(low_s.at[cls], q, here)
            for i, (ref, first) in enumerate(here):
                for o in range(2):
                    at = key_chunk(xl, z, o, 2 * i + cls)
                    rows = slice(first + o * PIECE, first + o * PIECE + CHUNK)
                    kc[cls, at] = ref[rows, :HEAD]
                    vt[cls, at, :HEAD, :] = ref[rows, HEAD:].T
                    vt[cls, at, HEAD:, :] = jnp.ones((16, CHUNK), LOW)

        def one_block(block, _):
            qp = qs[block]
            o_ref[block] = jnp.zeros((HEAD + 16, ROWS), WIDE)
            ml_ref[pl.ds(block, 1), :] = jnp.full((1, ROWS), NEG, WIDE)
            for cls in range(2):

                def tile(t, mask):
                    k = kc[cls, pl.ds(2 * t, 2)].reshape(KT, HEAD)
                    s = mask(dot(k, qp, NT) * C2)
                    old = ml_ref[pl.ds(block, 1), :]
                    new = jnp.maximum(old, jnp.max(s, axis=0, keepdims=True))
                    p = jnp.exp2(s - new).astype(LOW)
                    v = jnp.concatenate([vt[cls, 2 * t], vt[cls, 2 * t + 1]], axis=1)
                    o_ref[block] = o_ref[block] * jnp.exp2(old - new) + dot(v, p)
                    ml_ref[pl.ds(block, 1), :] = new

                over_tiles(limits(cls, block, xl, z, y, low_s.at[cls]), tile)
            return 0

        lax.fori_loop(0, BLOCKS, one_block, 0)
        for block in range(BLOCKS):
            ml_ref[BLOCKS + block : BLOCKS + block + 1, :] = o_ref[block, HEAD : HEAD + 1, :]

    return pl.pallas_call(
        kernel,
        in_specs=[sspec()] + [vspec()] * (4 + len(arrays)),
        out_specs=[vspec()] * 2,
        out_shape=[
            jax.ShapeDtypeStruct((BLOCKS, HEAD + 16, ROWS), WIDE),
            jax.ShapeDtypeStruct((2 * BLOCKS, ROWS), WIDE),
        ],
        scratch_shapes=[
            pltpu.VMEM((BLOCKS, ROWS, HEAD), LOW),
            pltpu.VMEM((2, NZ, CHUNK, HEAD), LOW),
            pltpu.VMEM((2, NZ, HEAD + 16, CHUNK), LOW),
            pltpu.VMEM((2, BLOCKS, ROWS), WIDE),
        ],
        compiler_params=params(32),
        cost_estimate=pl.CostEstimate(
            flops=8 * 10**9, bytes_accessed=4 * 2**20, transcendentals=2 * 2**20
        ),
        name="forward",
    )(scalars, *q_blocks, *arrays)


def weighted(o_part, ml, u_blocks):
    def kernel(o_ref, ml_ref, *refs):
        u = refs[0:4]
        out_ref = refs[4]
        out_ref[: 2 * BLOCKS, :] = ml_ref[...]
        for o in range(2):
            for dy in range(NY):
                block, first = place(o, dy)
                for h in range(RATIO):
                    at = slice(first + h * CHUNK, first + (h + 1) * CHUNK)
                    ut = u[dy][o * CHUNK : (o + 1) * CHUNK, h * HEAD : (h + 1) * HEAD]
                    out_ref[2 * BLOCKS + block : 2 * BLOCKS + block + 1, at] = jnp.sum(
                        ut.astype(WIDE).T * o_ref[block, :HEAD, at], axis=0, keepdims=True
                    )

    return pl.pallas_call(
        kernel,
        in_specs=[vspec()] * 6,
        out_specs=vspec(),
        out_shape=jax.ShapeDtypeStruct((3 * BLOCKS, ROWS), WIDE),
        compiler_params=params(16),
        name="weighted",
    )(o_part, ml, *u_blocks)


def backward(cls, scalars, stats, q_blocks, u_blocks, arrays, views, dq_before):
    last = dq_before is not None
    n = len(arrays)

    def kernel(sc, *refs):
        st = refs[0:4]
        q = refs[4:8]
        u = refs[8:12]
        kv = refs[12 : 12 + n]
        refs = refs[12 + n :]
        if last:
            before, refs = refs[0], refs[1:]
            dq_out, dkv_out, refs = refs[0:4], refs[4:8], refs[8:]
        else:
            dq_out, dkv_out, refs = refs[0:1], refs[1:3], refs[3:]
        qs, us, kc, vc, kt, dk, dv, al, lse_s, delta_s, low_s = refs[:11]
        dqt = refs[11] if last else dq_out[0]
        xl, z, y = sc[0], sc[1], sc[2]
        here = [(kv[a], first) for a, first in views]
        stack_rows(qs, q, PIECE)
        stack_rows(us, u, CHUNK)
        fill_low(low_s, q, here)
        for i, (ref, first) in enumerate(here):
            for o in range(2):
                at = key_chunk(xl, z, o, 2 * i + cls)
                rows = slice(first + o * PIECE, first + o * PIECE + CHUNK)
                key = ref[rows, :HEAD]
                kc[at] = key
                vc[at] = ref[rows, HEAD:]
                kt[at] = key.T
        dk[...] = jnp.zeros(dk.shape, WIDE)
        dv[...] = jnp.zeros(dv.shape, WIDE)
        dqt[...] = before[...] if last else jnp.zeros(dqt.shape, WIDE)

        for i in range(NY):
            for kind in range(3):
                for o in range(2):
                    for dy in range(NY):
                        b, to = place(o, dy)
                        c, frm = place(o, (dy - i) % NY)
                        b, c = kind * BLOCKS + b, kind * BLOCKS + c
                        al[i, b : b + 1, to : to + GROUP] = st[i][c : c + 1, frm : frm + GROUP]
        tops = [al[i, :BLOCKS] for i in range(NY)]
        top = functools.reduce(jnp.maximum, tops)
        factors = [jnp.exp2(t - top) for t in tops]
        mass = sum(f * al[i, BLOCKS : 2 * BLOCKS] for i, f in enumerate(factors))
        share = sum(f * al[i, 2 * BLOCKS :] for i, f in enumerate(factors))
        lse_s[...] = top + jnp.log2(mass)
        delta_s[...] = share / mass

        def one_block(block, _):
            lse = lse_s[pl.ds(block, 1), :]
            delta = delta_s[pl.ds(block, 1), :]
            qp = qs[block]
            up = us[block]

            def tile(t, mask):
                k = kc[pl.ds(2 * t, 2)].reshape(KT, HEAD)
                v = vc[pl.ds(2 * t, 2)].reshape(KT, HEAD)
                p = jnp.exp2(mask(dot(k, qp, NT) * C2) - lse)
                ds = (p * (dot(v, up, NT) - delta)).astype(LOW)
                p = p.astype(LOW)
                dv[pl.ds(2 * t, 2)] += dot(p, up).reshape(2, CHUNK, HEAD)
                dk[pl.ds(2 * t, 2)] += dot(ds, qp).reshape(2, CHUNK, HEAD)
                kt_tile = jnp.concatenate([kt[2 * t], kt[2 * t + 1]], axis=1)
                dqt[block] += dot(kt_tile, ds)

            over_tiles(limits(cls, block, xl, z, y, low_s), tile)
            return 0

        lax.fori_loop(0, BLOCKS, one_block, 0)

        def write(out, first, d):
            for o in range(2):
                at = key_chunk(xl, z, o, d)
                rows = slice(first + o * CHUNK, first + (o + 1) * CHUNK)
                out[rows, :HEAD] = (dk[at] * SCALE).astype(out.dtype)
                out[rows, HEAD:] = dv[at].astype(out.dtype)

        if last:
            for i in range(4):
                write(dkv_out[i], 0, 2 * i)
            for dy in range(NY):
                for o in range(2):
                    block, first = place(o, dy)
                    for h in range(RATIO):
                        start = first + h * CHUNK
                        part = dqt[block, :, start : start + CHUNK].T * SCALE
                        dq_out[dy][
                            o * CHUNK : (o + 1) * CHUNK, h * HEAD : (h + 1) * HEAD
                        ] = part.astype(dq_out[dy].dtype)
        else:
            write(dkv_out[0], 0, 1)
            write(dkv_out[0], 2 * CHUNK, 3)
            write(dkv_out[1], 0, 7)
            write(dkv_out[1], 2 * CHUNK, 5)

    dq_state = jax.ShapeDtypeStruct((BLOCKS, HEAD, ROWS), WIDE)
    if last:
        out_shape = [
            jax.ShapeDtypeStruct((2 * CHUNK, GROUP), WIDE if dy == 0 else LOW)
            for dy in range(NY)
        ] + [
            jax.ShapeDtypeStruct((2 * CHUNK, 2 * HEAD), LOW if i == 2 else WIDE)
            for i in range(4)
        ]
    else:
        out_shape = [dq_state] + [jax.ShapeDtypeStruct((4 * CHUNK, 2 * HEAD), LOW)] * 2
    state = [dq_before] if last else []
    return pl.pallas_call(
        kernel,
        in_specs=[sspec()] + [vspec()] * (12 + n + len(state)),
        out_specs=[vspec()] * len(out_shape),
        out_shape=out_shape,
        scratch_shapes=[
            pltpu.VMEM((BLOCKS, ROWS, HEAD), LOW),
            pltpu.VMEM((BLOCKS, ROWS, HEAD), LOW),
            pltpu.VMEM((NZ, CHUNK, HEAD), LOW),
            pltpu.VMEM((NZ, CHUNK, HEAD), LOW),
            pltpu.VMEM((NZ, HEAD, CHUNK), LOW),
            pltpu.VMEM((NZ, CHUNK, HEAD), WIDE),
            pltpu.VMEM((NZ, CHUNK, HEAD), WIDE),
            pltpu.VMEM((NY, 3 * BLOCKS, ROWS), WIDE),
            pltpu.VMEM((BLOCKS, ROWS), WIDE),
            pltpu.VMEM((BLOCKS, ROWS), WIDE),
            pltpu.VMEM((BLOCKS, ROWS), WIDE),
        ]
        + ([pltpu.VMEM((BLOCKS, HEAD, ROWS), WIDE)] if last else []),
        compiler_params=params(32),
        cost_estimate=pl.CostEstimate(
            flops=8 * 10**9, bytes_accessed=6 * 2**20, transcendentals=2 * 2**20
        ),
        name="backward%d" % cls,
    )(scalars, *stats, *q_blocks, *u_blocks, *arrays, *state)


def settle(dq, dq_got, dkv, dkv_got):
    def kernel(*refs):
        dq_ref, a, b, c, dkv_ref, d, e, f, keep, send = refs
        for out, first in ((keep, 0), (send, CHUNK)):
            rows = slice(first, first + CHUNK)
            total = dq_ref[rows, :]
            for g in (a, b, c):
                total += g[rows, :].astype(WIDE)
            out[:, :GROUP] = total.astype(LOW)
            total = dkv_ref[rows, :]
            for g in (d, e, f):
                total += g[rows, :].astype(WIDE)
            out[:, GROUP:] = total.astype(LOW)

    return pl.pallas_call(
        kernel,
        in_specs=[vspec()] * 8,
        out_specs=[vspec()] * 2,
        out_shape=[jax.ShapeDtypeStruct((CHUNK, GROUP + 2 * HEAD), LOW)] * 2,
        compiler_params=params(8),
        name="settle",
    )(dq, *dq_got, dkv, *dkv_got)


def join(scalars, keep, back):
    def kernel(sc, keep_ref, back_ref, q_ref, k_ref, v_ref):
        xl = sc[0]
        for g, ref in ((xl, keep_ref), (1 - xl, back_ref)):
            q_ref[:, pl.ds(pl.multiple_of(g * GROUP, GROUP), GROUP)] = ref[:, :GROUP]
            at = pl.ds(pl.multiple_of(g * HEAD, HEAD), HEAD)
            k_ref[:, at] = ref[:, GROUP : GROUP + HEAD]
            v_ref[:, at] = ref[:, GROUP + HEAD :]

    return pl.pallas_call(
        kernel,
        in_specs=[sspec(), vspec(), vspec()],
        out_specs=[vspec()] * 3,
        out_shape=[
            jax.ShapeDtypeStruct((CHUNK, 2 * GROUP), LOW),
            jax.ShapeDtypeStruct((CHUNK, 2 * HEAD), LOW),
            jax.ShapeDtypeStruct((CHUNK, 2 * HEAD), LOW),
        ],
        compiler_params=params(8),
        name="join",
    )(scalars, keep, back)


def shift(x, axis, size, d):
    return lax.ppermute(x, axis, [(i, (i - d) % size) for i in range(size)])


def swap(x):
    return shift(x, "xl", XL, 1)


def below(whole, x):
    return lax.dynamic_update_slice(whole, x, (whole.shape[0] - x.shape[0], 0))


def along_y(x):
    return [x] + [shift(x, "y", NY, d) for d in (1, 2, 3)]


def per_device(queries, keys, values, grad_out, out_weight, segments):
    xl, z, y = lax.axis_index("xl"), lax.axis_index("z"), lax.axis_index("y")
    tp = lax.axis_index("xh") * 2 + lax.axis_index("core")
    scalars = jnp.stack([xl, z, y, tp]).astype(jnp.int32)

    far = shift(grad_out, "xh", 2, 1)
    mate = shift(grad_out, "core", 2, 1)
    q_own, q_oth, kv_own, kv_oth = prepare(scalars, queries, keys, values, segments)
    kv_in = swap(kv_oth)
    q_in = swap(q_oth)

    kv = below(kv_own, kv_in)
    kv_up2 = shift(kv, "z", NZ, 2)
    kv_down2 = shift(kv, "z", NZ, -2)
    kv_4 = shift(kv, "z", NZ, 4)
    q_blocks = along_y(below(q_own, q_in))
    kv_up = shift(jnp.concatenate([kv, kv_up2], axis=0), "z", NZ, 1)
    kv_down = shift(jnp.concatenate([kv, kv_down2], axis=0), "z", NZ, -1)
    even = [kv, kv_up2, kv_4, kv_down2]
    odd = [kv_up, kv_down]
    second = 2 * PIECE
    even_views = [(i, 0) for i in range(4)]
    odd_views = [(0, 0), (0, second), (1, second), (1, 0)]

    relay, _ = lax.optimization_barrier((far, kv))
    far_mate = shift(relay, "core", 2, 1)
    weight, grad = stage(out_weight, grad_out)
    u_own, u_oth = upstream(scalars, [grad, mate, far, far_mate], weight)
    u_blocks = along_y(below(u_own, swap(u_oth)))

    o_part, ml = forward(
        scalars, q_blocks, even + odd, [even_views, [(4 + a, first) for a, first in odd_views]]
    )
    stats = along_y(weighted(o_part, ml, u_blocks))
    dq_state, bundle_up, bundle_down = backward(
        1, scalars, stats, q_blocks, u_blocks, odd, odd_views, None
    )
    got_up = shift(bundle_up, "z", NZ, -1)
    got_down = shift(bundle_down, "z", NZ, 1)
    *dq, dkv, dkv_up2, dkv_4, dkv_down2 = backward(
        0, scalars, stats, q_blocks, u_blocks, even, even_views, dq_state
    )

    near, further = slice(0, 2 * CHUNK), slice(2 * CHUNK, None)
    dkv = dkv + got_up[near].astype(WIDE) + got_down[near].astype(WIDE)
    up2 = (dkv_up2 + got_up[further].astype(WIDE)).astype(LOW)
    down2 = (dkv_down2 + got_down[further].astype(WIDE)).astype(LOW)
    dq, up2, down2 = lax.optimization_barrier((dq, up2, down2))
    dkv_got = [
        shift(dkv_4, "z", NZ, 4),
        shift(up2, "z", NZ, -2),
        shift(down2, "z", NZ, 2),
    ]
    dq_got = [shift(dq[d], "y", NY, -d) for d in (1, 2, 3)]
    keep, send = settle(dq[0], dq_got, dkv, dkv_got)
    return join(scalars, keep, swap(send))


def solution(mesh):
    fine = Mesh(mesh.devices.reshape(XL, NZ, NY, 2, 2), ("xl", "z", "y", "xh", "core"))
    ctx, tp = ("xl", "z", "y"), ("xh", "core")
    in_specs = (P(ctx, tp), P(ctx, tp), P(ctx, tp), P(ctx, tp), P(None, tp), P(ctx))
    out_specs = (P(ctx, tp), P(ctx, tp), P(ctx, tp))
    return jax.shard_map(
        per_device, mesh=fine, in_specs=in_specs, out_specs=out_specs, check_vma=False
    )
```

profile of v0, /device:TPU:2, one launch (start us, length us, event | category | flops | bytes accessed | tf_op | source)
XLA Modules:
  0.0 122.6 jit_solution(7555545085576037378)
XLA Ops:
  0.6 2.2 %collective-permute-start.11 = (bf16[128,1024]{1,0:T(8,128)(2,1)}, bf16[128,1024]{1,0:T(8,128)(2,1)S(1)}, u32[]{:S(2)}, u32[]{:S(2)}) collective-permute-start(bf16[128,1024]{1,0:T(8,128)(2,1)} %g_hbm.1), channel_id=1, source_target_pairs={{0,2},{2,0},{1,3},{3,1},{4,6},{6,4},{5,7},{7,5},{8,10},{10,8},{9,1... | collective-permute-start | bytes 786440 | tf_op jit(solution)/shard_map/ppermute | solution.py:511
  2.8 0.1 pad_add_fusion.sc
  2.9 1.6 %prepare.1 = (bf16[288,512]{1,0:T(8,128)(2,1)S(1)}, bf16[144,512]{1,0:T(8,128)(2,1)S(1)}, bf16[288,256]{1,0:T(8,128)(2,1)S(1)}, bf16[144,256]{1,0:T(8,128)(2,1)S(1)}) custom-call(s32[4]{0:T(128)S(1)} %pad_add_fusion.sc, bf16[128,1024]{1,0:T(8,128)(2,1)} %q_ref.1, bf16[128,256]{1,0:T(8,128)(2,1)} %k_ref.1, bf16[128,256]{1,0:T(8,128)(2,1)} %v_ref.1, ...), custom_call_target="tpu_custom_call" | custom-call | tf_op jit(solution)/shard_map/prepare/pallas_call | solution.py:86
  4.6 1.5 %collective-permute-start.4 = (bf16[144,256]{1,0:T(8,128)(2,1)S(1)}, bf16[144,256]{1,0:T(8,128)(2,1)S(1)}, u32[]{:S(2)}, u32[]{:S(2)}) collective-permute-start(bf16[144,256]{1,0:T(8,128)(2,1)S(1)} %get-tuple-element.36), channel_id=1, source_target_pairs={{0,128},{128,0},{1,129},{129,1},{2,130},{130,2},{3,131},{131,3},{4... | collective-permute-start | bytes 221192 | tf_op jit(solution)/shard_map/ppermute | solution.py:511
  6.1 0.0 collective-permute-start.10
  6.1 6.0 %collective-permute-done.4 = bf16[144,256]{1,0:T(8,128)(2,1)S(1)} collective-permute-done((bf16[144,256]{1,0:T(8,128)(2,1)S(1)}, bf16[144,256]{1,0:T(8,128)(2,1)S(1)}, u32[]{:S(2)}, u32[]{:S(2)}) %collective-permute-start.4) | collective-permute-done | bytes 73760 | tf_op jit(solution)/shard_map/ppermute | solution.py:511
  12.1 0.1 collective-permute-start.12
  12.2 0.7 collective-permute-start
  12.9 6.3 %collective-permute-start.5 = (bf16[288,256]{1,0:T(8,128)(2,1)S(1)}, bf16[288,256]{1,0:T(8,128)(2,1)S(1)}, u32[]{:S(2)}, u32[]{:S(2)}) collective-permute-start(bf16[288,256]{1,0:T(8,128)(2,1)S(1)} %constant_dynamic-update-slice_fusion.1.refs_4_.refs_12_), channel_id=1, source_target_pairs={{0,96},{16,112},{32,0},{48,16},{64,32},{80,48},{96,64},{112,80},{1... | collective-permute-start | bytes 442376 | tf_op jit(solution)/shard_map/ppermute | solution.py:511
  19.2 3.4 %stage.1 = (bf16[4096,1024]{1,0:T(8,128)(2,1)S(1)}, bf16[128,1024]{1,0:T(8,128)(2,1)S(1)}) custom-call(bf16[4096,1024]{1,0:T(8,128)(2,1)} %w_hbm.1, bf16[128,1024]{1,0:T(8,128)(2,1)} %g_hbm.1), custom_call_target="tpu_custom_call" | custom-call | tf_op jit(solution)/shard_map/stage/pallas_call | solution.py:113
  22.6 3.9 %collective-permute-start.6 = (bf16[288,256]{1,0:T(8,128)(2,1)S(1)}, bf16[288,256]{1,0:T(8,128)(2,1)S(1)}, u32[]{:S(2)}, u32[]{:S(2)}) collective-permute-start(bf16[288,256]{1,0:T(8,128)(2,1)S(1)} %constant_dynamic-update-slice_fusion.1.refs_4_.refs_12_), channel_id=1, source_target_pairs={{0,64},{16,80},{32,96},{48,112},{64,0},{80,16},{96,32},{112,48},{1... | collective-permute-start | bytes 442376 | tf_op jit(solution)/shard_map/ppermute | solution.py:511
  26.5 1.8 %upstream.1 = (bf16[256,512]{1,0:T(8,128)(2,1)S(1)}, bf16[128,512]{1,0:T(8,128)(2,1)S(1)}) custom-call(s32[4]{0:T(128)S(1)} %pad_add_fusion.sc, bf16[128,1024]{1,0:T(8,128)(2,1)S(1)} %get-tuple-element.39.refs_0_, bf16[128,1024]{1,0:T(8,128)(2,1)S(1)} %collective-permute-done.10.refs_1_, bf16[128,1024]{1,0:T(8,128)(2,1)S(1)} %collective-permute-done.11.refs_2_, ...), custom_call_target="tpu_custom_call" | custom-call | tf_op jit(solution)/shard_map/upstream/pallas_call | solution.py:140
  28.4 1.5 %collective-permute-start.13 = (bf16[128,512]{1,0:T(8,128)(2,1)S(1)}, bf16[128,512]{1,0:T(8,128)(2,1)S(1)}, u32[]{:S(2)}, u32[]{:S(2)}) collective-permute-start(bf16[128,512]{1,0:T(8,128)(2,1)S(1)} %get-tuple-element.43), channel_id=1, source_target_pairs={{0,128},{128,0},{1,129},{129,1},{2,130},{130,2},{3,131},{131,3},{4... | collective-permute-start | bytes 393224 | tf_op jit(solution)/shard_map/ppermute | solution.py:511
  29.9 3.1 %collective-permute-start.1 = (bf16[288,512]{1,0:T(8,128)(2,1)S(1)}, bf16[288,512]{1,0:T(8,128)(2,1)S(1)}, u32[]{:S(2)}, u32[]{:S(2)}) collective-permute-start(bf16[288,512]{1,0:T(8,128)(2,1)S(1)} %constant_dynamic-update-slice_fusion.2.refs_0_.refs_4_), channel_id=1, source_target_pairs={{0,12},{4,0},{8,4},{12,8},{1,13},{5,1},{9,5},{13,9},{2,14},{6,2},{... | collective-permute-start | bytes 884744 | tf_op jit(solution)/shard_map/ppermute | solution.py:511
  33.0 0.6 collective-permute-start.2
  33.6 1.0 collective-permute-start.3
  34.6 2.1 %collective-permute-done.6.refs_6_.refs_14_ = bf16[288,256]{1,0:T(8,128)(2,1)S(1)} collective-permute-done((bf16[288,256]{1,0:T(8,128)(2,1)S(1)}, bf16[288,256]{1,0:T(8,128)(2,1)S(1)}, u32[]{:S(2)}, u32[]{:S(2)}) %collective-permute-start.6) | collective-permute-done | bytes 147488 | tf_op jit(solution)/shard_map/ppermute | solution.py:511
  36.7 1.8 %collective-permute-start.8 = (bf16[576,256]{1,0:T(8,128)(2,1)S(1)}, bf16[576,256]{1,0:T(8,128)(2,1)S(1)}, u32[]{:S(2)}, u32[]{:S(2)}) collective-permute-start(bf16[576,256]{1,0:T(8,128)(2,1)S(1)} %get-tuple-element.67), channel_id=1, source_target_pairs={{0,112},{16,0},{32,16},{48,32},{64,48},{80,64},{96,80},{112,96},{1... | collective-permute-start | bytes 884744 | tf_op jit(solution)/shard_map/ppermute | solution.py:511
  38.5 0.2 collective-permute-start.9
  38.8 7.0 %collective-permute-done.1.refs_1_.refs_5_ = bf16[288,512]{1,0:T(8,128)(2,1)S(1)} collective-permute-done((bf16[288,512]{1,0:T(8,128)(2,1)S(1)}, bf16[288,512]{1,0:T(8,128)(2,1)S(1)}, u32[]{:S(2)}, u32[]{:S(2)}) %collective-permute-start.1) | collective-permute-done | bytes 294944 | tf_op jit(solution)/shard_map/ppermute | solution.py:511
  45.7 3.8 %collective-permute-start.14 = (bf16[256,512]{1,0:T(8,128)(2,1)S(1)}, bf16[256,512]{1,0:T(8,128)(2,1)S(1)}, u32[]{:S(2)}, u32[]{:S(2)}) collective-permute-start(bf16[256,512]{1,0:T(8,128)(2,1)S(1)} %constant_dynamic-update-slice_fusion.refs_0_.refs_8_), channel_id=1, source_target_pairs={{0,12},{4,0},{8,4},{12,8},{1,13},{5,1},{9,5},{13,9},{2,14},{6,2},{... | collective-permute-start | bytes 786440 | tf_op jit(solution)/shard_map/ppermute | solution.py:511
  49.6 1.1 collective-permute-done.3.refs_3_.refs_7_
  50.7 0.0 collective-permute-start.16
  50.7 7.3 %forward.1 = (f32[2,144,2048]{2,1,0:T(8,128)S(1)}, f32[4,2048]{1,0:T(4,128)S(1)}) custom-call(s32[4]{0:T(128)S(1)} %pad_add_fusion.sc, bf16[288,512]{1,0:T(8,128)(2,1)S(1)} %constant_dynamic-update-slice_fusion.2.refs_0_.refs_4_, bf16[288,512]{1,0:T(8,128)(2,1)S(1)} %collective-permute-done.1.refs_1_.refs_5_, ...), custom_call_target="tpu_custom_call" | custom-call | flops 8000000000 | bytes 4194304 | tf_op jit(solution)/shard_map/forward/pallas_call | solution.py:280
  58.1 4.8 %collective-permute-done.16.refs_3_.refs_11_ = bf16[256,512]{1,0:T(8,128)(2,1)S(1)} collective-permute-done((bf16[256,512]{1,0:T(8,128)(2,1)S(1)}, bf16[256,512]{1,0:T(8,128)(2,1)S(1)}, u32[]{:S(2)}, u32[]{:S(2)}) %collective-permute-start.16) | collective-permute-done | bytes 262176 | tf_op jit(solution)/shard_map/ppermute | solution.py:511
  62.8 0.4 weighted.1.refs_0_
  63.2 0.1 collective-permute-start.17
  63.3 0.8 collective-permute-start.18
  64.1 1.2 collective-permute-start.19
  65.3 2.2 %collective-permute-done.17.refs_1_ = f32[6,2048]{1,0:T(8,128)S(1)} collective-permute-done((f32[6,2048]{1,0:T(8,128)S(1)}, f32[6,2048]{1,0:T(8,128)S(1)}, u32[]{:S(2)}, u32[]{:S(2)}) %collective-permute-start.17) | collective-permute-done | bytes 49184 | tf_op jit(solution)/shard_map/ppermute | solution.py:511
  67.6 1.9 %collective-permute-done.18.refs_2_ = f32[6,2048]{1,0:T(8,128)S(1)} collective-permute-done((f32[6,2048]{1,0:T(8,128)S(1)}, f32[6,2048]{1,0:T(8,128)S(1)}, u32[]{:S(2)}, u32[]{:S(2)}) %collective-permute-start.18) | collective-permute-done | bytes 49184 | tf_op jit(solution)/shard_map/ppermute | solution.py:511
  69.5 0.8 collective-permute-done.19.refs_3_
  70.2 5.0 %backward1.1 = (f32[2,128,2048]{2,1,0:T(8,128)S(1)}, bf16[512,256]{1,0:T(8,128)(2,1)S(1)}, bf16[512,256]{1,0:T(8,128)(2,1)S(1)}) custom-call(s32[4]{0:T(128)S(1)} %pad_add_fusion.sc, f32[6,2048]{1,0:T(8,128)S(1)} %weighted.1.refs_0_, f32[6,2048]{1,0:T(8,128)S(1)} %collective-permute-done.17.refs_1_, f32[6,2048]{1,0:T(8,128)S(1)} %collective-permute-done.18.refs_2_, ...), custom_call_target="tpu_custom_call" | custom-call | flops 8000000000 | bytes 6291456 | tf_op jit(solution)/shard_map/backward1/pallas_call | solution.py:436
  75.3 4.1 %collective-permute-start.20 = (bf16[512,256]{1,0:T(8,128)(2,1)S(1)}, bf16[512,256]{1,0:T(8,128)(2,1)S(1)}, u32[]{:S(2)}, u32[]{:S(2)}) collective-permute-start(bf16[512,256]{1,0:T(8,128)(2,1)S(1)} %get-tuple-element.50), channel_id=1, source_target_pairs={{0,16},{16,32},{32,48},{48,64},{64,80},{80,96},{96,112},{112,0},{1... | collective-permute-start | bytes 786440 | tf_op jit(solution)/shard_map/ppermute | solution.py:511
  79.3 5.1 %collective-permute-start.21 = (bf16[512,256]{1,0:T(8,128)(2,1)S(1)}, bf16[512,256]{1,0:T(8,128)(2,1)S(1)}, u32[]{:S(2)}, u32[]{:S(2)}) collective-permute-start(bf16[512,256]{1,0:T(8,128)(2,1)S(1)} %get-tuple-element.52), channel_id=1, source_target_pairs={{0,112},{16,0},{32,16},{48,32},{64,48},{80,64},{96,80},{112,96},{1... | collective-permute-start | bytes 786440 | tf_op jit(solution)/shard_map/ppermute | solution.py:511
  84.4 7.3 %backward0.1 = (f32[256,512]{1,0:T(8,128)S(1)}, bf16[256,512]{1,0:T(8,128)(2,1)S(1)}, bf16[256,512]{1,0:T(8,128)(2,1)S(1)}, bf16[256,512]{1,0:T(8,128)(2,1)S(1)}...) custom-call(s32[4]{0:T(128)S(1)} %pad_add_fusion.sc, ...), custom_call_target="tpu_custom_call" | custom-call | flops 8000000000 | bytes 6291456 | tf_op jit(solution)/shard_map/backward0/pallas_call | solution.py:436
  91.7 4.4 %collective-permute-start.25 = (bf16[256,256]{1,0:T(8,128)(2,1)S(1)}, bf16[256,256]{1,0:T(8,128)(2,1)S(1)}, u32[]{:S(2)}, u32[]{:S(2)}) collective-permute-start(bf16[256,256]{1,0:T(8,128)(2,1)S(1)} %get-tuple-element.58), channel_id=1, source_target_pairs={{0,64},{16,80},{32,96},{48,112},{64,0},{80,16},{96,32},{112,48},{1... | collective-permute-start | bytes 393224 | tf_op jit(solution)/shard_map/ppermute | solution.py:511
  96.2 0.1 convert_add_fusion
  96.3 0.1 collective-permute-start.22
  96.4 9.2 %collective-permute-start.23 = (bf16[256,512]{1,0:T(8,128)(2,1)S(1)}, bf16[256,512]{1,0:T(8,128)(2,1)S(1)}, u32[]{:S(2)}, u32[]{:S(2)}) collective-permute-start(bf16[256,512]{1,0:T(8,128)(2,1)S(1)} %get-tuple-element.55), channel_id=1, source_target_pairs={{0,8},{4,12},{8,0},{12,4},{1,9},{5,13},{9,1},{13,5},{2,10},{6,14},... | collective-permute-start | bytes 786440 | tf_op jit(solution)/shard_map/ppermute | solution.py:511
  105.6 2.5 %collective-permute-start.26 = (bf16[256,256]{1,0:T(8,128)(2,1)S(1)}, bf16[256,256]{1,0:T(8,128)(2,1)S(1)}, u32[]{:S(2)}, u32[]{:S(2)}) collective-permute-start(bf16[256,256]{1,0:T(8,128)(2,1)S(1)} %get-tuple-element.59), channel_id=1, source_target_pairs={{0,32},{16,48},{32,64},{48,80},{64,96},{80,112},{96,0},{112,16},{1... | collective-permute-start | bytes 393224 | tf_op jit(solution)/shard_map/ppermute | solution.py:511
  108.0 1.7 %collective-permute-start.27 = (bf16[256,256]{1,0:T(8,128)(2,1)S(1)}, bf16[256,256]{1,0:T(8,128)(2,1)S(1)}, u32[]{:S(2)}, u32[]{:S(2)}) collective-permute-start(bf16[256,256]{1,0:T(8,128)(2,1)S(1)} %get-tuple-element.60), channel_id=1, source_target_pairs={{0,96},{16,112},{32,0},{48,16},{64,32},{80,48},{96,64},{112,80},{1... | collective-permute-start | bytes 393224 | tf_op jit(solution)/shard_map/ppermute | solution.py:511
  109.7 4.3 %collective-permute-done.26.refs_6_ = bf16[256,256]{1,0:T(8,128)(2,1)S(1)} collective-permute-done((bf16[256,256]{1,0:T(8,128)(2,1)S(1)}, bf16[256,256]{1,0:T(8,128)(2,1)S(1)}, u32[]{:S(2)}, u32[]{:S(2)}) %collective-permute-start.26) | collective-permute-done | bytes 131104 | tf_op jit(solution)/shard_map/ppermute | solution.py:511
  114.0 1.3 %collective-permute-done.23.refs_2_ = bf16[256,512]{1,0:T(8,128)(2,1)S(1)} collective-permute-done((bf16[256,512]{1,0:T(8,128)(2,1)S(1)}, bf16[256,512]{1,0:T(8,128)(2,1)S(1)}, u32[]{:S(2)}, u32[]{:S(2)}) %collective-permute-start.23) | collective-permute-done | bytes 262176 | tf_op jit(solution)/shard_map/ppermute | solution.py:511
  115.3 0.2 settle.1
  115.5 0.2 collective-permute-start.28
  115.7 5.6 %collective-permute-done.28.back_ref = bf16[128,768]{1,0:T(8,128)(2,1)S(1)} collective-permute-done((bf16[128,768]{1,0:T(8,128)(2,1)S(1)}, bf16[128,768]{1,0:T(8,128)(2,1)S(1)}, u32[]{:S(2)}, u32[]{:S(2)}) %collective-permute-start.28) | collective-permute-done | bytes 196640 | tf_op jit(solution)/shard_map/ppermute | solution.py:511
  121.3 1.3 %join.1 = (bf16[128,1024]{1,0:T(8,128)(2,1)}, bf16[128,256]{1,0:T(8,128)(2,1)}, bf16[128,256]{1,0:T(8,128)(2,1)}) custom-call(s32[4]{0:T(128)S(1)} %pad_add_fusion.sc, bf16[128,768]{1,0:T(8,128)(2,1)S(1)} %get-tuple-element.61.keep_ref, bf16[128,768]{1,0:T(8,128)(2,1)S(1)} %collective-permute-done.28.back_ref), custom_call_target="tpu_custom_call" | custom-call | tf_op jit(solution)/shard_map/join/pallas_call | solution.py:496
  (25 shorter events, 0.1 us)
Async XLA Ops:
  0.6 11.5 %collective-permute-start.11 = (bf16[128,1024]{1,0:T(8,128)(2,1)}, bf16[128,1024]{1,0:T(8,128)(2,1)S(1)}, u32[]{:S(2)}, u32[]{:S(2)}) collective-permute-start(bf16[128,1024]{1,0:T(8,128)(2,1)} %g_hbm.1), channel_id=1, source_target_pairs={{0,2},{2,0},{1,3},{3,1},{4,6},{6,4},{5,7},{7,5},{8,10},{10,8},{9,1... | collective-permute-start | bytes 786440 | tf_op jit(solution)/shard_map/ppermute | solution.py:511
  4.6 7.5 %collective-permute-start.4 = (bf16[144,256]{1,0:T(8,128)(2,1)S(1)}, bf16[144,256]{1,0:T(8,128)(2,1)S(1)}, u32[]{:S(2)}, u32[]{:S(2)}) collective-permute-start(bf16[144,256]{1,0:T(8,128)(2,1)S(1)} %get-tuple-element.36), channel_id=1, source_target_pairs={{0,128},{128,0},{1,129},{129,1},{2,130},{130,2},{3,131},{131,3},{4... | collective-permute-start | bytes 221192 | tf_op jit(solution)/shard_map/ppermute | solution.py:511
  6.1 16.5 %collective-permute-start.10 = (bf16[128,1024]{1,0:T(8,128)(2,1)}, bf16[128,1024]{1,0:T(8,128)(2,1)S(1)}, u32[]{:S(2)}, u32[]{:S(2)}) collective-permute-start(bf16[128,1024]{1,0:T(8,128)(2,1)} %g_hbm.1), channel_id=1, source_target_pairs={{0,1},{1,0},{2,3},{3,2},{4,5},{5,4},{6,7},{7,6},{8,9},{9,8},{10,11... | collective-permute-start | bytes 786440 | tf_op jit(solution)/shard_map/ppermute | solution.py:511
  12.1 14.4 %collective-permute-start.12 = (bf16[128,1024]{1,0:T(8,128)(2,1)S(1)}, bf16[128,1024]{1,0:T(8,128)(2,1)S(1)}, u32[]{:S(2)}, u32[]{:S(2)}) collective-permute-start(bf16[128,1024]{1,0:T(8,128)(2,1)S(1)} %collective-permute-done.11.refs_2_), channel_id=1, source_target_pairs={{0,1},{1,0},{2,3},{3,2},{4,5},{5,4},{6,7},{7,6},{8,9},{9,8},{10,11... | collective-permute-start | bytes 786440 | tf_op jit(solution)/shard_map/ppermute | solution.py:511
  12.2 17.7 %collective-permute-start = (bf16[144,512]{1,0:T(8,128)(2,1)S(1)}, bf16[144,512]{1,0:T(8,128)(2,1)S(1)}, u32[]{:S(2)}, u32[]{:S(2)}) collective-permute-start(bf16[144,512]{1,0:T(8,128)(2,1)S(1)} %get-tuple-element.34), channel_id=1, source_target_pairs={{0,128},{128,0},{1,129},{129,1},{2,130},{130,2},{3,131},{131,3},{4... | collective-permute-start | bytes 442376 | tf_op jit(solution)/shard_map/ppermute | solution.py:511
  12.9 20.1 %collective-permute-start.5 = (bf16[288,256]{1,0:T(8,128)(2,1)S(1)}, bf16[288,256]{1,0:T(8,128)(2,1)S(1)}, u32[]{:S(2)}, u32[]{:S(2)}) collective-permute-start(bf16[288,256]{1,0:T(8,128)(2,1)S(1)} %constant_dynamic-update-slice_fusion.1.refs_4_.refs_12_), channel_id=1, source_target_pairs={{0,96},{16,112},{32,0},{48,16},{64,32},{80,48},{96,64},{112,80},{1... | collective-permute-start | bytes 442376 | tf_op jit(solution)/shard_map/ppermute | solution.py:511
  19.2 14.4 %collective-permute-start.7 = (bf16[288,256]{1,0:T(8,128)(2,1)S(1)}, bf16[288,256]{1,0:T(8,128)(2,1)S(1)}, u32[]{:S(2)}, u32[]{:S(2)}) collective-permute-start(bf16[288,256]{1,0:T(8,128)(2,1)S(1)} %constant_dynamic-update-slice_fusion.1.refs_4_.refs_12_), channel_id=1, source_target_pairs={{0,32},{16,48},{32,64},{48,80},{64,96},{80,112},{96,0},{112,16},{1... | collective-permute-start | bytes 442376 | tf_op jit(solution)/shard_map/ppermute | solution.py:511
  22.6 14.1 %collective-permute-start.6 = (bf16[288,256]{1,0:T(8,128)(2,1)S(1)}, bf16[288,256]{1,0:T(8,128)(2,1)S(1)}, u32[]{:S(2)}, u32[]{:S(2)}) collective-permute-start(bf16[288,256]{1,0:T(8,128)(2,1)S(1)} %constant_dynamic-update-slice_fusion.1.refs_4_.refs_12_), channel_id=1, source_target_pairs={{0,64},{16,80},{32,96},{48,112},{64,0},{80,16},{96,32},{112,48},{1... | collective-permute-start | bytes 442376 | tf_op jit(solution)/shard_map/ppermute | solution.py:511
  28.4 10.1 %collective-permute-start.13 = (bf16[128,512]{1,0:T(8,128)(2,1)S(1)}, bf16[128,512]{1,0:T(8,128)(2,1)S(1)}, u32[]{:S(2)}, u32[]{:S(2)}) collective-permute-start(bf16[128,512]{1,0:T(8,128)(2,1)S(1)} %get-tuple-element.43), channel_id=1, source_target_pairs={{0,128},{128,0},{1,129},{129,1},{2,130},{130,2},{3,131},{131,3},{4... | collective-permute-start | bytes 393224 | tf_op jit(solution)/shard_map/ppermute | solution.py:511
  29.9 15.8 %collective-permute-start.1 = (bf16[288,512]{1,0:T(8,128)(2,1)S(1)}, bf16[288,512]{1,0:T(8,128)(2,1)S(1)}, u32[]{:S(2)}, u32[]{:S(2)}) collective-permute-start(bf16[288,512]{1,0:T(8,128)(2,1)S(1)} %constant_dynamic-update-slice_fusion.2.refs_0_.refs_4_), channel_id=1, source_target_pairs={{0,12},{4,0},{8,4},{12,8},{1,13},{5,1},{9,5},{13,9},{2,14},{6,2},{... | collective-permute-start | bytes 884744 | tf_op jit(solution)/shard_map/ppermute | solution.py:511
  33.0 16.6 %collective-permute-start.2 = (bf16[288,512]{1,0:T(8,128)(2,1)S(1)}, bf16[288,512]{1,0:T(8,128)(2,1)S(1)}, u32[]{:S(2)}, u32[]{:S(2)}) collective-permute-start(bf16[288,512]{1,0:T(8,128)(2,1)S(1)} %constant_dynamic-update-slice_fusion.2.refs_0_.refs_4_), channel_id=1, source_target_pairs={{0,8},{4,12},{8,0},{12,4},{1,9},{5,13},{9,1},{13,5},{2,10},{6,14},... | collective-permute-start | bytes 884744 | tf_op jit(solution)/shard_map/ppermute | solution.py:511
  33.6 17.1 %collective-permute-start.3 = (bf16[288,512]{1,0:T(8,128)(2,1)S(1)}, bf16[288,512]{1,0:T(8,128)(2,1)S(1)}, u32[]{:S(2)}, u32[]{:S(2)}) collective-permute-start(bf16[288,512]{1,0:T(8,128)(2,1)S(1)} %constant_dynamic-update-slice_fusion.2.refs_0_.refs_4_), channel_id=1, source_target_pairs={{0,4},{4,8},{8,12},{12,0},{1,5},{5,9},{9,13},{13,1},{2,6},{6,10},{... | collective-permute-start | bytes 884744 | tf_op jit(solution)/shard_map/ppermute | solution.py:511
  36.7 14.0 %collective-permute-start.8 = (bf16[576,256]{1,0:T(8,128)(2,1)S(1)}, bf16[576,256]{1,0:T(8,128)(2,1)S(1)}, u32[]{:S(2)}, u32[]{:S(2)}) collective-permute-start(bf16[576,256]{1,0:T(8,128)(2,1)S(1)} %get-tuple-element.67), channel_id=1, source_target_pairs={{0,112},{16,0},{32,16},{48,32},{64,48},{80,64},{96,80},{112,96},{1... | collective-permute-start | bytes 884744 | tf_op jit(solution)/shard_map/ppermute | solution.py:511
  38.5 12.2 %collective-permute-start.9 = (bf16[576,256]{1,0:T(8,128)(2,1)S(1)}, bf16[576,256]{1,0:T(8,128)(2,1)S(1)}, u32[]{:S(2)}, u32[]{:S(2)}) collective-permute-start(bf16[576,256]{1,0:T(8,128)(2,1)S(1)} %get-tuple-element.66), channel_id=1, source_target_pairs={{0,16},{16,32},{32,48},{48,64},{64,80},{80,96},{96,112},{112,0},{1... | collective-permute-start | bytes 884744 | tf_op jit(solution)/shard_map/ppermute | solution.py:511
  45.7 12.3 %collective-permute-start.14 = (bf16[256,512]{1,0:T(8,128)(2,1)S(1)}, bf16[256,512]{1,0:T(8,128)(2,1)S(1)}, u32[]{:S(2)}, u32[]{:S(2)}) collective-permute-start(bf16[256,512]{1,0:T(8,128)(2,1)S(1)} %constant_dynamic-update-slice_fusion.refs_0_.refs_8_), channel_id=1, source_target_pairs={{0,12},{4,0},{8,4},{12,8},{1,13},{5,1},{9,5},{13,9},{2,14},{6,2},{... | collective-permute-start | bytes 786440 | tf_op jit(solution)/shard_map/ppermute | solution.py:511
  49.6 8.5 %collective-permute-start.15 = (bf16[256,512]{1,0:T(8,128)(2,1)S(1)}, bf16[256,512]{1,0:T(8,128)(2,1)S(1)}, u32[]{:S(2)}, u32[]{:S(2)}) collective-permute-start(bf16[256,512]{1,0:T(8,128)(2,1)S(1)} %constant_dynamic-update-slice_fusion.refs_0_.refs_8_), channel_id=1, source_target_pairs={{0,8},{4,12},{8,0},{12,4},{1,9},{5,13},{9,1},{13,5},{2,10},{6,14},... | collective-permute-start | bytes 786440 | tf_op jit(solution)/shard_map/ppermute | solution.py:511
  50.7 12.1 %collective-permute-start.16 = (bf16[256,512]{1,0:T(8,128)(2,1)S(1)}, bf16[256,512]{1,0:T(8,128)(2,1)S(1)}, u32[]{:S(2)}, u32[]{:S(2)}) collective-permute-start(bf16[256,512]{1,0:T(8,128)(2,1)S(1)} %constant_dynamic-update-slice_fusion.refs_0_.refs_8_), channel_id=1, source_target_pairs={{0,4},{4,8},{8,12},{12,0},{1,5},{5,9},{9,13},{13,1},{2,6},{6,10},{... | collective-permute-start | bytes 786440 | tf_op jit(solution)/shard_map/ppermute | solution.py:511
  63.2 4.3 %collective-permute-start.17 = (f32[6,2048]{1,0:T(8,128)S(1)}, f32[6,2048]{1,0:T(8,128)S(1)}, u32[]{:S(2)}, u32[]{:S(2)}) collective-permute-start(f32[6,2048]{1,0:T(8,128)S(1)} %weighted.1.refs_0_), channel_id=1, source_target_pairs={{0,12},{4,0},{8,4},{12,8},{1,13},{5,1},{9,5},{13,9},{2,14},{6,2},{... | collective-permute-start | bytes 147464 | tf_op jit(solution)/shard_map/ppermute | solution.py:511
  63.3 6.1 %collective-permute-start.18 = (f32[6,2048]{1,0:T(8,128)S(1)}, f32[6,2048]{1,0:T(8,128)S(1)}, u32[]{:S(2)}, u32[]{:S(2)}) collective-permute-start(f32[6,2048]{1,0:T(8,128)S(1)} %weighted.1.refs_0_), channel_id=1, source_target_pairs={{0,8},{4,12},{8,0},{12,4},{1,9},{5,13},{9,1},{13,5},{2,10},{6,14},... | collective-permute-start | bytes 147464 | tf_op jit(solution)/shard_map/ppermute | solution.py:511
  64.1 6.1 %collective-permute-start.19 = (f32[6,2048]{1,0:T(8,128)S(1)}, f32[6,2048]{1,0:T(8,128)S(1)}, u32[]{:S(2)}, u32[]{:S(2)}) collective-permute-start(f32[6,2048]{1,0:T(8,128)S(1)} %weighted.1.refs_0_), channel_id=1, source_target_pairs={{0,4},{4,8},{8,12},{12,0},{1,5},{5,9},{9,13},{13,1},{2,6},{6,10},{... | collective-permute-start | bytes 147464 | tf_op jit(solution)/shard_map/ppermute | solution.py:511
  75.3 20.9 %collective-permute-start.20 = (bf16[512,256]{1,0:T(8,128)(2,1)S(1)}, bf16[512,256]{1,0:T(8,128)(2,1)S(1)}, u32[]{:S(2)}, u32[]{:S(2)}) collective-permute-start(bf16[512,256]{1,0:T(8,128)(2,1)S(1)} %get-tuple-element.50), channel_id=1, source_target_pairs={{0,16},{16,32},{32,48},{48,64},{64,80},{80,96},{96,112},{112,0},{1... | collective-permute-start | bytes 786440 | tf_op jit(solution)/shard_map/ppermute | solution.py:511
  79.3 16.8 %collective-permute-start.21 = (bf16[512,256]{1,0:T(8,128)(2,1)S(1)}, bf16[512,256]{1,0:T(8,128)(2,1)S(1)}, u32[]{:S(2)}, u32[]{:S(2)}) collective-permute-start(bf16[512,256]{1,0:T(8,128)(2,1)S(1)} %get-tuple-element.52), channel_id=1, source_target_pairs={{0,112},{16,0},{32,16},{48,32},{64,48},{80,64},{96,80},{112,96},{1... | collective-permute-start | bytes 786440 | tf_op jit(solution)/shard_map/ppermute | solution.py:511
  91.7 16.3 %collective-permute-start.25 = (bf16[256,256]{1,0:T(8,128)(2,1)S(1)}, bf16[256,256]{1,0:T(8,128)(2,1)S(1)}, u32[]{:S(2)}, u32[]{:S(2)}) collective-permute-start(bf16[256,256]{1,0:T(8,128)(2,1)S(1)} %get-tuple-element.58), channel_id=1, source_target_pairs={{0,64},{16,80},{32,96},{48,112},{64,0},{80,16},{96,32},{112,48},{1... | collective-permute-start | bytes 393224 | tf_op jit(solution)/shard_map/ppermute | solution.py:511
  96.3 17.8 %collective-permute-start.22 = (bf16[256,512]{1,0:T(8,128)(2,1)S(1)}, bf16[256,512]{1,0:T(8,128)(2,1)S(1)}, u32[]{:S(2)}, u32[]{:S(2)}) collective-permute-start(bf16[256,512]{1,0:T(8,128)(2,1)S(1)} %get-tuple-element.54), channel_id=1, source_target_pairs={{0,4},{4,8},{8,12},{12,0},{1,5},{5,9},{9,13},{13,1},{2,6},{6,10},{... | collective-permute-start | bytes 786440 | tf_op jit(solution)/shard_map/ppermute | solution.py:511
  96.4 19.0 %collective-permute-start.23 = (bf16[256,512]{1,0:T(8,128)(2,1)S(1)}, bf16[256,512]{1,0:T(8,128)(2,1)S(1)}, u32[]{:S(2)}, u32[]{:S(2)}) collective-permute-start(bf16[256,512]{1,0:T(8,128)(2,1)S(1)} %get-tuple-element.55), channel_id=1, source_target_pairs={{0,8},{4,12},{8,0},{12,4},{1,9},{5,13},{9,1},{13,5},{2,10},{6,14},... | collective-permute-start | bytes 786440 | tf_op jit(solution)/shard_map/ppermute | solution.py:511
  105.6 9.7 %collective-permute-start.24 = (bf16[256,512]{1,0:T(8,128)(2,1)S(1)}, bf16[256,512]{1,0:T(8,128)(2,1)S(1)}, u32[]{:S(2)}, u32[]{:S(2)}) collective-permute-start(bf16[256,512]{1,0:T(8,128)(2,1)S(1)} %get-tuple-element.56), channel_id=1, source_target_pairs={{0,12},{4,0},{8,4},{12,8},{1,13},{5,1},{9,5},{13,9},{2,14},{6,2},{... | collective-permute-start | bytes 786440 | tf_op jit(solution)/shard_map/ppermute | solution.py:511
  105.6 8.4 %collective-permute-start.26 = (bf16[256,256]{1,0:T(8,128)(2,1)S(1)}, bf16[256,256]{1,0:T(8,128)(2,1)S(1)}, u32[]{:S(2)}, u32[]{:S(2)}) collective-permute-start(bf16[256,256]{1,0:T(8,128)(2,1)S(1)} %get-tuple-element.59), channel_id=1, source_target_pairs={{0,32},{16,48},{32,64},{48,80},{64,96},{80,112},{96,0},{112,16},{1... | collective-permute-start | bytes 393224 | tf_op jit(solution)/shard_map/ppermute | solution.py:511
  108.0 6.0 %collective-permute-start.27 = (bf16[256,256]{1,0:T(8,128)(2,1)S(1)}, bf16[256,256]{1,0:T(8,128)(2,1)S(1)}, u32[]{:S(2)}, u32[]{:S(2)}) collective-permute-start(bf16[256,256]{1,0:T(8,128)(2,1)S(1)} %get-tuple-element.60), channel_id=1, source_target_pairs={{0,96},{16,112},{32,0},{48,16},{64,32},{80,48},{96,64},{112,80},{1... | collective-permute-start | bytes 393224 | tf_op jit(solution)/shard_map/ppermute | solution.py:511
  115.5 5.8 %collective-permute-start.28 = (bf16[128,768]{1,0:T(8,128)(2,1)S(1)}, bf16[128,768]{1,0:T(8,128)(2,1)S(1)}, u32[]{:S(2)}, u32[]{:S(2)}) collective-permute-start(bf16[128,768]{1,0:T(8,128)(2,1)S(1)} %get-tuple-element.62), channel_id=1, source_target_pairs={{0,128},{128,0},{1,129},{129,1},{2,130},{130,2},{3,131},{131,3},{4... | collective-permute-start | bytes 589832 | tf_op jit(solution)/shard_map/ppermute | solution.py:511
where the time goes:
time: 122 us; the launch traced here: 123 us
  starting transfers between devices  56.1 us (46%)
  waiting for transfers between devices  37.1 us (30%)
  Pallas kernels  28.4 us (23%)
    ppermute x29, starting transfers between devices, shift(): return lax.ppermute(x, axis, [(i, (i - d) % size) for i in range(size)])  56.1 us
    ppermute x29, waiting for transfers between devices, shift(): return lax.ppermute(x, axis, [(i, (i - d) % size) for i in range(size)])  37.1 us
    pallas_call x2, Pallas kernels, backward(): pl.pallas_call(kernel, in_specs=[sspec()] + [vspec()] * (12 + n + len(sta...  12.3 us
    pallas_call x1, Pallas kernels, forward(): pl.pallas_call(kernel, in_specs=[sspec()] + [vspec()] * (4 + len(arrays))...  7.33 us
    pallas_call x1, Pallas kernels, stage(): pl.pallas_call(kernel, in_specs=[hspec()] * 2, out_specs=[vspec()] * 2, o...  3.4 us
  transfers between devices with their start and end apart: 29, of which 11 were waited for; matrix products, arithmetic and copies ran while one was open for 0% of the time, Pallas kernels for 18%

commit v1 on v0

--- a/solution.py
+++ b/solution.py
@@ -117,6 +117,9 @@
         out_shape=[jax.ShapeDtypeStruct(x.shape, x.dtype) for x in (weight, grad)],
         scratch_shapes=[pltpu.SemaphoreType.DMA((2,))],
         compiler_params=params(12),
+        cost_estimate=pl.CostEstimate(
+            flops=0, bytes_accessed=4 * weight.size, transcendentals=0
+        ),
         name="stage",
     )(in_hbm(weight), in_hbm(grad))
 
@@ -151,6 +154,9 @@
     )(scalars, *grads, weight)
 
 
+DISTANCES = {None: tuple(range(NZ)), 0: (0, 2, 6), 1: (1, 3, 5, 7, 4)}
+
+
 def place(o, dy):
     return o * (NY // DP) + dy // DP, (dy % DP) * GROUP
 
@@ -166,9 +172,17 @@
                 ]
 
 
-def key_chunk(xl, z, o, d):
+def rank(cls, plane, z):
+    if cls is None:
+        return plane
+    odd = (plane + 1 - lax.rem(z + 1, 2)) // 2
+    fourth = jnp.where(lax.rem(z + 4, NZ) < plane, 1, 0)
+    return odd + fourth if cls == 1 else plane - odd - fourth
+
+
+def key_chunk(cls, xl, z, o, d):
     half = xl if o == 0 else 1 - xl
-    return half * 4 + lax.rem(z + d, NZ) // 2
+    return half * len(DISTANCES[cls]) + rank(cls, lax.rem(z + d, NZ), z)
 
 
 def count_row(ref, first):
@@ -193,9 +207,8 @@
     plane = z
     dy0 = lax.rem(block, NY // DP) * DP
     ys = [lax.rem(y + dy0 + i, NY) for i in range(DP)]
-    parity = lax.rem(plane + cls, 2)
-    full = h * (KEYS // 2) + ((plane + 1 - parity) // 2) * CHUNK
-    if cls == 0:
+    full = (h * len(DISTANCES[cls]) + rank(cls, plane, z)) * CHUNK
+    if cls != 1:
         lane = lax.broadcasted_iota(jnp.int32, (1, ROWS), 1)
         yy = jnp.full((1, ROWS), ys[-1], jnp.int32)
         for i in reversed(range(DP - 1)):
@@ -243,34 +256,32 @@
         o_ref, ml_ref, qs, kc, vt, low_s = refs[4 + len(arrays) :]
         xl, z, y = sc[0], sc[1], sc[2]
         stack_rows(qs, q, PIECE)
-        for cls in range(2):
-            here = [(kv[a], first) for a, first in views[cls]]
-            fill_low(low_s.at[cls], q, here)
-            for i, (ref, first) in enumerate(here):
-                for o in range(2):
-                    at = key_chunk(xl, z, o, 2 * i + cls)
-                    rows = slice(first + o * PIECE, first + o * PIECE + CHUNK)
-                    kc[cls, at] = ref[rows, :HEAD]
-                    vt[cls, at, :HEAD, :] = ref[rows, HEAD:].T
-                    vt[cls, at, HEAD:, :] = jnp.ones((16, CHUNK), LOW)
+        here = [(kv[a], first) for a, first, _ in views]
+        fill_low(low_s, q, here)
+        for (ref, first), (_, _, d) in zip(here, views):
+            for o in range(2):
+                at = key_chunk(None, xl, z, o, d)
+                rows = slice(first + o * PIECE, first + o * PIECE + CHUNK)
+                kc[at] = ref[rows, :HEAD]
+                vt[at, :HEAD, :] = ref[rows, HEAD:].T
+                vt[at, HEAD:, :] = jnp.ones((16, CHUNK), LOW)
 
         def one_block(block, _):
             qp = qs[block]
             o_ref[block] = jnp.zeros((HEAD + 16, ROWS), WIDE)
             ml_ref[pl.ds(block, 1), :] = jnp.full((1, ROWS), NEG, WIDE)
-            for cls in range(2):
-
-                def tile(t, mask):
-                    k = kc[cls, pl.ds(2 * t, 2)].reshape(KT, HEAD)
-                    s = mask(dot(k, qp, NT) * C2)
-                    old = ml_ref[pl.ds(block, 1), :]
-                    new = jnp.maximum(old, jnp.max(s, axis=0, keepdims=True))
-                    p = jnp.exp2(s - new).astype(LOW)
-                    v = jnp.concatenate([vt[cls, 2 * t], vt[cls, 2 * t + 1]], axis=1)
-                    o_ref[block] = o_ref[block] * jnp.exp2(old - new) + dot(v, p)
-                    ml_ref[pl.ds(block, 1), :] = new
-
-                over_tiles(limits(cls, block, xl, z, y, low_s.at[cls]), tile)
+
+            def tile(t, mask):
+                k = kc[pl.ds(2 * t, 2)].reshape(KT, HEAD)
+                s = mask(dot(k, qp, NT) * C2)
+                old = ml_ref[pl.ds(block, 1), :]
+                new = jnp.maximum(old, jnp.max(s, axis=0, keepdims=True))
+                p = jnp.exp2(s - new).astype(LOW)
+                v = jnp.concatenate([vt[2 * t], vt[2 * t + 1]], axis=1)
+                o_ref[block] = o_ref[block] * jnp.exp2(old - new) + dot(v, p)
+                ml_ref[pl.ds(block, 1), :] = new
+
+            over_tiles(limits(None, block, xl, z, y, low_s), tile)
             return 0
 
         lax.fori_loop(0, BLOCKS, one_block, 0)
@@ -287,9 +298,9 @@
         ],
         scratch_shapes=[
             pltpu.VMEM((BLOCKS, ROWS, HEAD), LOW),
-            pltpu.VMEM((2, NZ, CHUNK, HEAD), LOW),
-            pltpu.VMEM((2, NZ, HEAD + 16, CHUNK), LOW),
-            pltpu.VMEM((2, BLOCKS, ROWS), WIDE),
+            pltpu.VMEM((2 * NZ, CHUNK, HEAD), LOW),
+            pltpu.VMEM((2 * NZ, HEAD + 16, CHUNK), LOW),
+            pltpu.VMEM((BLOCKS, ROWS), WIDE),
         ],
         compiler_params=params(32),
         cost_estimate=pl.CostEstimate(
@@ -327,6 +338,7 @@
 def backward(cls, scalars, stats, q_blocks, u_blocks, arrays, views, dq_before):
     last = dq_before is not None
     n = len(arrays)
+    chunks = 2 * len(DISTANCES[cls])
 
     def kernel(sc, *refs):
         st = refs[0:4]
@@ -336,19 +348,19 @@
         refs = refs[12 + n :]
         if last:
             before, refs = refs[0], refs[1:]
-            dq_out, dkv_out, refs = refs[0:4], refs[4:8], refs[8:]
+            dq_out, dkv_out, refs = refs[0:4], refs[4:7], refs[7:]
         else:
-            dq_out, dkv_out, refs = refs[0:1], refs[1:3], refs[3:]
+            dq_out, dkv_out, refs = refs[0:1], refs[1:4], refs[4:]
         qs, us, kc, vc, kt, dk, dv, al, lse_s, delta_s, low_s = refs[:11]
         dqt = refs[11] if last else dq_out[0]
         xl, z, y = sc[0], sc[1], sc[2]
-        here = [(kv[a], first) for a, first in views]
+        here = [(kv[a], first) for a, first, _ in views]
         stack_rows(qs, q, PIECE)
         stack_rows(us, u, CHUNK)
         fill_low(low_s, q, here)
-        for i, (ref, first) in enumerate(here):
+        for (ref, first), (_, _, d) in zip(here, views):
             for o in range(2):
-                at = key_chunk(xl, z, o, 2 * i + cls)
+                at = key_chunk(cls, xl, z, o, d)
                 rows = slice(first + o * PIECE, first + o * PIECE + CHUNK)
                 key = ref[rows, :HEAD]
                 kc[at] = key
@@ -398,14 +410,14 @@
 
         def write(out, first, d):
             for o in range(2):
-                at = key_chunk(xl, z, o, d)
+                at = key_chunk(cls, xl, z, o, d)
                 rows = slice(first + o * CHUNK, first + (o + 1) * CHUNK)
                 out[rows, :HEAD] = (dk[at] * SCALE).astype(out.dtype)
                 out[rows, HEAD:] = dv[at].astype(out.dtype)
 
         if last:
-            for i in range(4):
-                write(dkv_out[i], 0, 2 * i)
+            for out, d in zip(dkv_out, DISTANCES[cls]):
+                write(out, 0, d)
             for dy in range(NY):
                 for o in range(2):
                     block, first = place(o, dy)
@@ -420,6 +432,7 @@
             write(dkv_out[0], 2 * CHUNK, 3)
             write(dkv_out[1], 0, 7)
             write(dkv_out[1], 2 * CHUNK, 5)
+            write(dkv_out[2], 0, 4)
 
     dq_state = jax.ShapeDtypeStruct((BLOCKS, HEAD, ROWS), WIDE)
     if last:
@@ -427,11 +440,12 @@
             jax.ShapeDtypeStruct((2 * CHUNK, GROUP), WIDE if dy == 0 else LOW)
             for dy in range(NY)
         ] + [
-            jax.ShapeDtypeStruct((2 * CHUNK, 2 * HEAD), LOW if i == 2 else WIDE)
-            for i in range(4)
+            jax.ShapeDtypeStruct((2 * CHUNK, 2 * HEAD), WIDE) for d in DISTANCES[cls]
         ]
     else:
-        out_shape = [dq_state] + [jax.ShapeDtypeStruct((4 * CHUNK, 2 * HEAD), LOW)] * 2
+        out_shape = [dq_state] + [
+            jax.ShapeDtypeStruct((n * CHUNK, 2 * HEAD), LOW) for n in (4, 4, 2)
+        ]
     state = [dq_before] if last else []
     return pl.pallas_call(
         kernel,
@@ -441,11 +455,11 @@
         scratch_shapes=[
             pltpu.VMEM((BLOCKS, ROWS, HEAD), LOW),
             pltpu.VMEM((BLOCKS, ROWS, HEAD), LOW),
-            pltpu.VMEM((NZ, CHUNK, HEAD), LOW),
-            pltpu.VMEM((NZ, CHUNK, HEAD), LOW),
-            pltpu.VMEM((NZ, HEAD, CHUNK), LOW),
-            pltpu.VMEM((NZ, CHUNK, HEAD), WIDE),
-            pltpu.VMEM((NZ, CHUNK, HEAD), WIDE),
+            pltpu.VMEM((chunks, CHUNK, HEAD), LOW),
+            pltpu.VMEM((chunks, CHUNK, HEAD), LOW),
+            pltpu.VMEM((chunks, HEAD, CHUNK), LOW),
+            pltpu.VMEM((chunks, CHUNK, HEAD), WIDE),
+            pltpu.VMEM((chunks, CHUNK, HEAD), WIDE),
             pltpu.VMEM((NY, 3 * BLOCKS, ROWS), WIDE),
             pltpu.VMEM((BLOCKS, ROWS), WIDE),
             pltpu.VMEM((BLOCKS, ROWS), WIDE),
@@ -534,6 +548,8 @@
     kv_in = swap(kv_oth)
     q_in = swap(q_oth)
 
+    weight, grad = stage(out_weight, grad_out)
+    kv_in, _ = lax.optimization_barrier((kv_in, grad))
     kv = below(kv_own, kv_in)
     kv_up2 = shift(kv, "z", NZ, 2)
     kv_down2 = shift(kv, "z", NZ, -2)
@@ -541,28 +557,28 @@
     q_blocks = along_y(below(q_own, q_in))
     kv_up = shift(jnp.concatenate([kv, kv_up2], axis=0), "z", NZ, 1)
     kv_down = shift(jnp.concatenate([kv, kv_down2], axis=0), "z", NZ, -1)
-    even = [kv, kv_up2, kv_4, kv_down2]
-    odd = [kv_up, kv_down]
     second = 2 * PIECE
-    even_views = [(i, 0) for i in range(4)]
-    odd_views = [(0, 0), (0, second), (1, second), (1, 0)]
+    odd = [kv_up, kv_down, kv_4]
+    odd_views = [(0, 0, 1), (0, second, 3), (1, second, 5), (1, 0, 7), (2, 0, 4)]
+    even = [kv, kv_up2, kv_down2]
+    even_views = [(0, 0, 0), (1, 0, 2), (2, 0, 6)]
 
     relay, _ = lax.optimization_barrier((far, kv))
     far_mate = shift(relay, "core", 2, 1)
-    weight, grad = stage(out_weight, grad_out)
     u_own, u_oth = upstream(scalars, [grad, mate, far, far_mate], weight)
     u_blocks = along_y(below(u_own, swap(u_oth)))
 
     o_part, ml = forward(
-        scalars, q_blocks, even + odd, [even_views, [(4 + a, first) for a, first in odd_views]]
+        scalars, q_blocks, even + odd, even_views + [(3 + a, f, d) for a, f, d in odd_views]
     )
     stats = along_y(weighted(o_part, ml, u_blocks))
-    dq_state, bundle_up, bundle_down = backward(
+    dq_state, bundle_up, bundle_down, dkv_4 = backward(
         1, scalars, stats, q_blocks, u_blocks, odd, odd_views, None
     )
     got_up = shift(bundle_up, "z", NZ, -1)
     got_down = shift(bundle_down, "z", NZ, 1)
-    *dq, dkv, dkv_up2, dkv_4, dkv_down2 = backward(
+    got_4 = shift(dkv_4, "z", NZ, 4)
+    *dq, dkv, dkv_up2, dkv_down2 = backward(
         0, scalars, stats, q_blocks, u_blocks, even, even_views, dq_state
     )
 
@@ -572,7 +588,7 @@
     down2 = (dkv_down2 + got_down[further].astype(WIDE)).astype(LOW)
     dq, up2, down2 = lax.optimization_barrier((dq, up2, down2))
     dkv_got = [
-        shift(dkv_4, "z", NZ, 4),
+        got_4,
         shift(up2, "z", NZ, -2),
         shift(down2, "z", NZ, 2),
     ]

time: 122 us -> 114 us (0.934); the launches traced: 123 us -> 112 us
  waiting for transfers between devices: 37.1 us -> 26.2 us
  starting transfers between devices: 56.1 us -> 53.8 us
  Pallas kernels: 28.4 us -> 30.5 us
    ppermute x29, waiting for transfers between devices: 37.1 us -> 26.2 us  [shift(): return lax.ppermute(x, axis, [(i, (i - d) % size) for i in range(size)])]
    ppermute x29, starting transfers between devices: 56.1 us -> 53.8 us  [shift(): return lax.ppermute(x, axis, [(i, (i - d) % size) for i in range(size)])]
    pallas_call x2, Pallas kernels: 12.3 us -> 13.8 us  [backward(): pl.pallas_call(kernel, in_specs=[sspec()] + [vspec()] * (12 + n + len(sta...]
  transfers between devices with their start and end apart: 29 -> 29, of which waited for: 11 -> 11; matrix products, arithmetic and copies ran while one was open for 0% -> 0% of each run, Pallas kernels for 18% -> 20%
where the time goes in v1:
time: 114 us; the launch traced here: 112 us
  starting transfers between devices  53.8 us (47%)
  Pallas kernels  30.5 us (27%)
  waiting for transfers between devices  26.2 us (23%)
    ppermute x29, starting transfers between devices, shift(): return lax.ppermute(x, axis, [(i, (i - d) % size) for i in range(size)])  53.8 us
    ppermute x29, waiting for transfers between devices, shift(): return lax.ppermute(x, axis, [(i, (i - d) % size) for i in range(size)])  26.2 us
    pallas_call x2, Pallas kernels, backward(): pl.pallas_call(kernel, in_specs=[sspec()] + [vspec()] * (12 + n + len(sta...  13.8 us
    pallas_call x1, Pallas kernels, forward(): pl.pallas_call(kernel, in_specs=[sspec()] + [vspec()] * (4 + len(arrays))...  7.96 us
    pallas_call x1, Pallas kernels, stage(): pl.pallas_call(kernel, in_specs=[hspec()] * 2, out_specs=[vspec()] * 2, o...  3.4 us
  transfers between devices with their start and end apart: 29, of which 11 were waited for; matrix products, arithmetic and copies ran while one was open for 0% of the time, Pallas kernels for 20%

profile of v1, /device:TPU:2, one launch (start us, length us, event | category | flops | bytes accessed | tf_op | source)
XLA Modules:
  0.0 111.7 jit_solution(5580293780816977357)
XLA Ops:
  0.6 2.2 %collective-permute-start.11 = (bf16[128,1024]{1,0:T(8,128)(2,1)}, bf16[128,1024]{1,0:T(8,128)(2,1)S(1)}, u32[]{:S(2)}, u32[]{:S(2)}) collective-permute-start(bf16[128,1024]{1,0:T(8,128)(2,1)} %g_hbm.1), channel_id=1, source_target_pairs={{0,2},{2,0},{1,3},{3,1},{4,6},{6,4},{5,7},{7,5},{8,10},{10,8},{9,1... | collective-permute-start | bytes 786440 | tf_op jit(solution)/shard_map/ppermute | solution.py:525
  2.8 0.1 pad_add_fusion.sc
  2.9 1.6 %prepare.1 = (bf16[288,512]{1,0:T(8,128)(2,1)S(1)}, bf16[144,512]{1,0:T(8,128)(2,1)S(1)}, bf16[288,256]{1,0:T(8,128)(2,1)S(1)}, bf16[144,256]{1,0:T(8,128)(2,1)S(1)}) custom-call(s32[4]{0:T(128)S(1)} %pad_add_fusion.sc, bf16[128,1024]{1,0:T(8,128)(2,1)} %q_ref.1, bf16[128,256]{1,0:T(8,128)(2,1)} %k_ref.1, bf16[128,256]{1,0:T(8,128)(2,1)} %v_ref.1, ...), custom_call_target="tpu_custom_call" | custom-call | tf_op jit(solution)/shard_map/prepare/pallas_call | solution.py:86
  4.6 1.5 %collective-permute-start.4 = (bf16[144,256]{1,0:T(8,128)(2,1)S(1)}, bf16[144,256]{1,0:T(8,128)(2,1)S(1)}, u32[]{:S(2)}, u32[]{:S(2)}) collective-permute-start(bf16[144,256]{1,0:T(8,128)(2,1)S(1)} %get-tuple-element.37), channel_id=1, source_target_pairs={{0,128},{128,0},{1,129},{129,1},{2,130},{130,2},{3,131},{131,3},{4... | collective-permute-start | bytes 221192 | tf_op jit(solution)/shard_map/ppermute | solution.py:525
  6.1 3.4 %stage.1 = (bf16[4096,1024]{1,0:T(8,128)(2,1)S(1)}, bf16[128,1024]{1,0:T(8,128)(2,1)S(1)}) custom-call(bf16[4096,1024]{1,0:T(8,128)(2,1)} %w_hbm.1, bf16[128,1024]{1,0:T(8,128)(2,1)} %g_hbm.1), custom_call_target="tpu_custom_call" | custom-call | bytes 16777216 | tf_op jit(solution)/shard_map/stage/pallas_call | solution.py:113
  9.5 2.6 %collective-permute-done.4 = bf16[144,256]{1,0:T(8,128)(2,1)S(1)} collective-permute-done((bf16[144,256]{1,0:T(8,128)(2,1)S(1)}, bf16[144,256]{1,0:T(8,128)(2,1)S(1)}, u32[]{:S(2)}, u32[]{:S(2)}) %collective-permute-start.4) | collective-permute-done | bytes 73760 | tf_op jit(solution)/shard_map/ppermute | solution.py:525
  12.1 0.1 collective-permute-start.12
  12.2 0.7 collective-permute-start
  12.9 6.3 %collective-permute-start.5 = (bf16[288,256]{1,0:T(8,128)(2,1)S(1)}, bf16[288,256]{1,0:T(8,128)(2,1)S(1)}, u32[]{:S(2)}, u32[]{:S(2)}) collective-permute-start(bf16[288,256]{1,0:T(8,128)(2,1)S(1)} %constant_dynamic-update-slice_fusion.1.refs_4_.refs_12_), channel_id=1, source_target_pairs={{0,96},{16,112},{32,0},{48,16},{64,32},{80,48},{96,64},{112,80},{1... | collective-permute-start | bytes 442376 | tf_op jit(solution)/shard_map/ppermute | solution.py:525
  19.2 3.8 %collective-permute-start.9 = (bf16[288,256]{1,0:T(8,128)(2,1)S(1)}, bf16[288,256]{1,0:T(8,128)(2,1)S(1)}, u32[]{:S(2)}, u32[]{:S(2)}) collective-permute-start(bf16[288,256]{1,0:T(8,128)(2,1)S(1)} %constant_dynamic-update-slice_fusion.1.refs_4_.refs_12_), channel_id=1, source_target_pairs={{0,64},{16,80},{32,96},{48,112},{64,0},{80,16},{96,32},{112,48},{1... | collective-permute-start | bytes 442376 | tf_op jit(solution)/shard_map/ppermute | solution.py:525
  23.0 1.9 %upstream.1 = (bf16[256,512]{1,0:T(8,128)(2,1)S(1)}, bf16[128,512]{1,0:T(8,128)(2,1)S(1)}) custom-call(s32[4]{0:T(128)S(1)} %pad_add_fusion.sc, bf16[128,1024]{1,0:T(8,128)(2,1)S(1)} %get-tuple-element.38.refs_0_, bf16[128,1024]{1,0:T(8,128)(2,1)S(1)} %collective-permute-done.10.refs_1_, bf16[128,1024]{1,0:T(8,128)(2,1)S(1)} %collective-permute-done.11.refs_2_, ...), custom_call_target="tpu_custom_call" | custom-call | tf_op jit(solution)/shard_map/upstream/pallas_call | solution.py:143
  24.9 1.5 %collective-permute-start.13 = (bf16[128,512]{1,0:T(8,128)(2,1)S(1)}, bf16[128,512]{1,0:T(8,128)(2,1)S(1)}, u32[]{:S(2)}, u32[]{:S(2)}) collective-permute-start(bf16[128,512]{1,0:T(8,128)(2,1)S(1)} %get-tuple-element.45), channel_id=1, source_target_pairs={{0,128},{128,0},{1,129},{129,1},{2,130},{130,2},{3,131},{131,3},{4... | collective-permute-start | bytes 393224 | tf_op jit(solution)/shard_map/ppermute | solution.py:525
  26.4 3.1 %collective-permute-start.1 = (bf16[288,512]{1,0:T(8,128)(2,1)S(1)}, bf16[288,512]{1,0:T(8,128)(2,1)S(1)}, u32[]{:S(2)}, u32[]{:S(2)}) collective-permute-start(bf16[288,512]{1,0:T(8,128)(2,1)S(1)} %constant_dynamic-update-slice_fusion.2.refs_0_.refs_4_), channel_id=1, source_target_pairs={{0,12},{4,0},{8,4},{12,8},{1,13},{5,1},{9,5},{13,9},{2,14},{6,2},{... | collective-permute-start | bytes 884744 | tf_op jit(solution)/shard_map/ppermute | solution.py:525
  29.5 1.5 %collective-permute-done.5.refs_5_.refs_13_ = bf16[288,256]{1,0:T(8,128)(2,1)S(1)} collective-permute-done((bf16[288,256]{1,0:T(8,128)(2,1)S(1)}, bf16[288,256]{1,0:T(8,128)(2,1)S(1)}, u32[]{:S(2)}, u32[]{:S(2)}) %collective-permute-start.5) | collective-permute-done | bytes 147488 | tf_op jit(solution)/shard_map/ppermute | solution.py:525
  31.0 3.2 %collective-permute-start.2 = (bf16[288,512]{1,0:T(8,128)(2,1)S(1)}, bf16[288,512]{1,0:T(8,128)(2,1)S(1)}, u32[]{:S(2)}, u32[]{:S(2)}) collective-permute-start(bf16[288,512]{1,0:T(8,128)(2,1)S(1)} %constant_dynamic-update-slice_fusion.2.refs_0_.refs_4_), channel_id=1, source_target_pairs={{0,8},{4,12},{8,0},{12,4},{1,9},{5,13},{9,1},{13,5},{2,10},{6,14},... | collective-permute-start | bytes 884744 | tf_op jit(solution)/shard_map/ppermute | solution.py:525
  34.2 1.0 collective-permute-start.3
  35.2 1.1 %collective-permute-start.7 = (bf16[576,256]{1,0:T(8,128)(2,1)S(1)}, bf16[576,256]{1,0:T(8,128)(2,1)S(1)}, u32[]{:S(2)}, u32[]{:S(2)}) collective-permute-start(bf16[576,256]{1,0:T(8,128)(2,1)S(1)} %get-tuple-element.69), channel_id=1, source_target_pairs={{0,112},{16,0},{32,16},{48,32},{64,48},{80,64},{96,80},{112,96},{1... | collective-permute-start | bytes 884744 | tf_op jit(solution)/shard_map/ppermute | solution.py:525
  36.4 2.8 %collective-permute-start.8 = (bf16[576,256]{1,0:T(8,128)(2,1)S(1)}, bf16[576,256]{1,0:T(8,128)(2,1)S(1)}, u32[]{:S(2)}, u32[]{:S(2)}) collective-permute-start(bf16[576,256]{1,0:T(8,128)(2,1)S(1)} %get-tuple-element.68), channel_id=1, source_target_pairs={{0,16},{16,32},{32,48},{48,64},{64,80},{80,96},{96,112},{112,0},{1... | collective-permute-start | bytes 884744 | tf_op jit(solution)/shard_map/ppermute | solution.py:525
  39.2 2.3 %collective-permute-done.1.refs_1_.refs_5_ = bf16[288,512]{1,0:T(8,128)(2,1)S(1)} collective-permute-done((bf16[288,512]{1,0:T(8,128)(2,1)S(1)}, bf16[288,512]{1,0:T(8,128)(2,1)S(1)}, u32[]{:S(2)}, u32[]{:S(2)}) %collective-permute-start.1) | collective-permute-done | bytes 294944 | tf_op jit(solution)/shard_map/ppermute | solution.py:525
  41.5 4.1 %collective-permute-start.14 = (bf16[256,512]{1,0:T(8,128)(2,1)S(1)}, bf16[256,512]{1,0:T(8,128)(2,1)S(1)}, u32[]{:S(2)}, u32[]{:S(2)}) collective-permute-start(bf16[256,512]{1,0:T(8,128)(2,1)S(1)} %constant_dynamic-update-slice_fusion.refs_0_.refs_8_), channel_id=1, source_target_pairs={{0,12},{4,0},{8,4},{12,8},{1,13},{5,1},{9,5},{13,9},{2,14},{6,2},{... | collective-permute-start | bytes 786440 | tf_op jit(solution)/shard_map/ppermute | solution.py:525
  45.6 0.0 collective-permute-start.15
  45.6 3.1 %collective-permute-done.3.refs_3_.refs_7_ = bf16[288,512]{1,0:T(8,128)(2,1)S(1)} collective-permute-done((bf16[288,512]{1,0:T(8,128)(2,1)S(1)}, bf16[288,512]{1,0:T(8,128)(2,1)S(1)}, u32[]{:S(2)}, u32[]{:S(2)}) %collective-permute-start.3) | collective-permute-done | bytes 294944 | tf_op jit(solution)/shard_map/ppermute | solution.py:525
  48.7 1.7 %collective-permute-start.16 = (bf16[256,512]{1,0:T(8,128)(2,1)S(1)}, bf16[256,512]{1,0:T(8,128)(2,1)S(1)}, u32[]{:S(2)}, u32[]{:S(2)}) collective-permute-start(bf16[256,512]{1,0:T(8,128)(2,1)S(1)} %constant_dynamic-update-slice_fusion.refs_0_.refs_8_), channel_id=1, source_target_pairs={{0,4},{4,8},{8,12},{12,0},{1,5},{5,9},{9,13},{13,1},{2,6},{6,10},{... | collective-permute-start | bytes 786440 | tf_op jit(solution)/shard_map/ppermute | solution.py:525
  50.5 8.0 %forward.1 = (f32[2,144,2048]{2,1,0:T(8,128)S(1)}, f32[4,2048]{1,0:T(4,128)S(1)}) custom-call(s32[4]{0:T(128)S(1)} %pad_add_fusion.sc, bf16[288,512]{1,0:T(8,128)(2,1)S(1)} %constant_dynamic-update-slice_fusion.2.refs_0_.refs_4_, bf16[288,512]{1,0:T(8,128)(2,1)S(1)} %collective-permute-done.1.refs_1_.refs_5_, ...), custom_call_target="tpu_custom_call" | custom-call | flops 8000000000 | bytes 4194304 | tf_op jit(solution)/shard_map/forward/pallas_call | solution.py:291
  58.5 1.6 %collective-permute-done.16.refs_3_.refs_11_ = bf16[256,512]{1,0:T(8,128)(2,1)S(1)} collective-permute-done((bf16[256,512]{1,0:T(8,128)(2,1)S(1)}, bf16[256,512]{1,0:T(8,128)(2,1)S(1)}, u32[]{:S(2)}, u32[]{:S(2)}) %collective-permute-start.16) | collective-permute-done | bytes 262176 | tf_op jit(solution)/shard_map/ppermute | solution.py:525
  60.0 0.4 weighted.1.refs_0_
  60.4 0.1 collective-permute-start.17
  60.5 2.1 %collective-permute-start.18 = (f32[6,2048]{1,0:T(8,128)S(1)}, f32[6,2048]{1,0:T(8,128)S(1)}, u32[]{:S(2)}, u32[]{:S(2)}) collective-permute-start(f32[6,2048]{1,0:T(8,128)S(1)} %weighted.1.refs_0_), channel_id=1, source_target_pairs={{0,8},{4,12},{8,0},{12,4},{1,9},{5,13},{9,1},{13,5},{2,10},{6,14},... | collective-permute-start | bytes 147464 | tf_op jit(solution)/shard_map/ppermute | solution.py:525
  62.6 0.4 collective-permute-start.19
  63.0 1.8 %collective-permute-done.17.refs_1_ = f32[6,2048]{1,0:T(8,128)S(1)} collective-permute-done((f32[6,2048]{1,0:T(8,128)S(1)}, f32[6,2048]{1,0:T(8,128)S(1)}, u32[]{:S(2)}, u32[]{:S(2)}) %collective-permute-start.17) | collective-permute-done | bytes 49184 | tf_op jit(solution)/shard_map/ppermute | solution.py:525
  64.8 1.8 %collective-permute-done.18.refs_2_ = f32[6,2048]{1,0:T(8,128)S(1)} collective-permute-done((f32[6,2048]{1,0:T(8,128)S(1)}, f32[6,2048]{1,0:T(8,128)S(1)}, u32[]{:S(2)}, u32[]{:S(2)}) %collective-permute-start.18) | collective-permute-done | bytes 49184 | tf_op jit(solution)/shard_map/ppermute | solution.py:525
  66.5 1.5 %collective-permute-done.19.refs_3_ = f32[6,2048]{1,0:T(8,128)S(1)} collective-permute-done((f32[6,2048]{1,0:T(8,128)S(1)}, f32[6,2048]{1,0:T(8,128)S(1)}, u32[]{:S(2)}, u32[]{:S(2)}) %collective-permute-start.19) | collective-permute-done | bytes 49184 | tf_op jit(solution)/shard_map/ppermute | solution.py:525
  68.0 6.6 %backward1.1 = (f32[2,128,2048]{2,1,0:T(8,128)S(1)}, bf16[512,256]{1,0:T(8,128)(2,1)S(1)}, bf16[512,256]{1,0:T(8,128)(2,1)S(1)}, bf16[256,256]{1,0:T(8,128)(2,1)S(1)}) custom-call(s32[4]{0:T(128)S(1)} %pad_add_fusion.sc, f32[6,2048]{1,0:T(8,128)S(1)} %weighted.1.refs_0_, f32[6,2048]{1,0:T(8,128)S(1)} %collective-permute-done.17.refs_1_, ...), custom_call_target="tpu_custom_call" | custom-call | flops 8000000000 | bytes 6291456 | tf_op jit(solution)/shard_map/backward1/pallas_call | solution.py:450
  74.6 1.0 collective-permute-start.20
  75.7 2.3 %collective-permute-start.21 = (bf16[512,256]{1,0:T(8,128)(2,1)S(1)}, bf16[512,256]{1,0:T(8,128)(2,1)S(1)}, u32[]{:S(2)}, u32[]{:S(2)}) collective-permute-start(bf16[512,256]{1,0:T(8,128)(2,1)S(1)} %get-tuple-element.54), channel_id=1, source_target_pairs={{0,112},{16,0},{32,16},{48,32},{64,48},{80,64},{96,80},{112,96},{1... | collective-permute-start | bytes 786440 | tf_op jit(solution)/shard_map/ppermute | solution.py:525
  78.0 3.0 %collective-permute-start.25 = (bf16[256,256]{1,0:T(8,128)(2,1)S(1)}, bf16[256,256]{1,0:T(8,128)(2,1)S(1)}, u32[]{:S(2)}, u32[]{:S(2)}) collective-permute-start(bf16[256,256]{1,0:T(8,128)(2,1)S(1)} %get-tuple-element.60), channel_id=1, source_target_pairs={{0,64},{16,80},{32,96},{48,112},{64,0},{80,16},{96,32},{112,48},{1... | collective-permute-start | bytes 393224 | tf_op jit(solution)/shard_map/ppermute | solution.py:525
  81.0 7.2 %backward0.1 = (f32[256,512]{1,0:T(8,128)S(1)}, bf16[256,512]{1,0:T(8,128)(2,1)S(1)}, bf16[256,512]{1,0:T(8,128)(2,1)S(1)}, bf16[256,512]{1,0:T(8,128)(2,1)S(1)}...) custom-call(s32[4]{0:T(128)S(1)} %pad_add_fusion.sc, f32[6,2048]{1,0:T(8,128)S(1)} %weighted.1.refs_0_, ...), custom_call_target="tpu_custom_call" | custom-call | flops 8000000000 | bytes 6291456 | tf_op jit(solution)/shard_map/backward0/pallas_call | solution.py:450
  88.2 0.1 convert_add_fusion
  88.3 0.1 collective-permute-start.22
  88.4 2.6 %collective-permute-start.23 = (bf16[256,512]{1,0:T(8,128)(2,1)S(1)}, bf16[256,512]{1,0:T(8,128)(2,1)S(1)}, u32[]{:S(2)}, u32[]{:S(2)}) collective-permute-start(bf16[256,512]{1,0:T(8,128)(2,1)S(1)} %get-tuple-element.57), channel_id=1, source_target_pairs={{0,8},{4,12},{8,0},{12,4},{1,9},{5,13},{9,1},{13,5},{2,10},{6,14},... | collective-permute-start | bytes 786440 | tf_op jit(solution)/shard_map/ppermute | solution.py:525
  91.1 1.2 %collective-permute-start.24 = (bf16[256,512]{1,0:T(8,128)(2,1)S(1)}, bf16[256,512]{1,0:T(8,128)(2,1)S(1)}, u32[]{:S(2)}, u32[]{:S(2)}) collective-permute-start(bf16[256,512]{1,0:T(8,128)(2,1)S(1)} %get-tuple-element.58), channel_id=1, source_target_pairs={{0,12},{4,0},{8,4},{12,8},{1,13},{5,1},{9,5},{13,9},{2,14},{6,2},{... | collective-permute-start | bytes 786440 | tf_op jit(solution)/shard_map/ppermute | solution.py:525
  92.3 6.2 %collective-permute-start.26 = (bf16[256,256]{1,0:T(8,128)(2,1)S(1)}, bf16[256,256]{1,0:T(8,128)(2,1)S(1)}, u32[]{:S(2)}, u32[]{:S(2)}) collective-permute-start(bf16[256,256]{1,0:T(8,128)(2,1)S(1)} %get-tuple-element.61), channel_id=1, source_target_pairs={{0,32},{16,48},{32,64},{48,80},{64,96},{80,112},{96,0},{112,16},{1... | collective-permute-start | bytes 393224 | tf_op jit(solution)/shard_map/ppermute | solution.py:525
  98.5 2.6 %collective-permute-done.26.refs_6_ = bf16[256,256]{1,0:T(8,128)(2,1)S(1)} collective-permute-done((bf16[256,256]{1,0:T(8,128)(2,1)S(1)}, bf16[256,256]{1,0:T(8,128)(2,1)S(1)}, u32[]{:S(2)}, u32[]{:S(2)}) %collective-permute-start.26) | collective-permute-done | bytes 131104 | tf_op jit(solution)/shard_map/ppermute | solution.py:525
  101.1 3.2 %collective-permute-done.27.refs_7_ = bf16[256,256]{1,0:T(8,128)(2,1)S(1)} collective-permute-done((bf16[256,256]{1,0:T(8,128)(2,1)S(1)}, bf16[256,256]{1,0:T(8,128)(2,1)S(1)}, u32[]{:S(2)}, u32[]{:S(2)}) %collective-permute-start.27) | collective-permute-done | bytes 131104 | tf_op jit(solution)/shard_map/ppermute | solution.py:525
  104.4 0.2 settle.1
  104.6 1.5 %collective-permute-start.28 = (bf16[128,768]{1,0:T(8,128)(2,1)S(1)}, bf16[128,768]{1,0:T(8,128)(2,1)S(1)}, u32[]{:S(2)}, u32[]{:S(2)}) collective-permute-start(bf16[128,768]{1,0:T(8,128)(2,1)S(1)} %get-tuple-element.64), channel_id=1, source_target_pairs={{0,128},{128,0},{1,129},{129,1},{2,130},{130,2},{3,131},{131,3},{4... | collective-permute-start | bytes 589832 | tf_op jit(solution)/shard_map/ppermute | solution.py:525
  106.1 4.2 %collective-permute-done.28.back_ref = bf16[128,768]{1,0:T(8,128)(2,1)S(1)} collective-permute-done((bf16[128,768]{1,0:T(8,128)(2,1)S(1)}, bf16[128,768]{1,0:T(8,128)(2,1)S(1)}, u32[]{:S(2)}, u32[]{:S(2)}) %collective-permute-start.28) | collective-permute-done | bytes 196640 | tf_op jit(solution)/shard_map/ppermute | solution.py:525
  110.3 1.3 %join.1 = (bf16[128,1024]{1,0:T(8,128)(2,1)}, bf16[128,256]{1,0:T(8,128)(2,1)}, bf16[128,256]{1,0:T(8,128)(2,1)}) custom-call(s32[4]{0:T(128)S(1)} %pad_add_fusion.sc, bf16[128,768]{1,0:T(8,128)(2,1)S(1)} %get-tuple-element.63.keep_ref, bf16[128,768]{1,0:T(8,128)(2,1)S(1)} %collective-permute-done.28.back_ref), custom_call_target="tpu_custom_call" | custom-call | tf_op jit(solution)/shard_map/join/pallas_call | solution.py:510
  (25 shorter events, 0.1 us)
Async XLA Ops:
  0.6 11.5 %collective-permute-start.11 = (bf16[128,1024]{1,0:T(8,128)(2,1)}, bf16[128,1024]{1,0:T(8,128)(2,1)S(1)}, u32[]{:S(2)}, u32[]{:S(2)}) collective-permute-start(bf16[128,1024]{1,0:T(8,128)(2,1)} %g_hbm.1), channel_id=1, source_target_pairs={{0,2},{2,0},{1,3},{3,1},{4,6},{6,4},{5,7},{7,5},{8,10},{10,8},{9,1... | collective-permute-start | bytes 786440 | tf_op jit(solution)/shard_map/ppermute | solution.py:525
  4.6 7.5 %collective-permute-start.4 = (bf16[144,256]{1,0:T(8,128)(2,1)S(1)}, bf16[144,256]{1,0:T(8,128)(2,1)S(1)}, u32[]{:S(2)}, u32[]{:S(2)}) collective-permute-start(bf16[144,256]{1,0:T(8,128)(2,1)S(1)} %get-tuple-element.37), channel_id=1, source_target_pairs={{0,128},{128,0},{1,129},{129,1},{2,130},{130,2},{3,131},{131,3},{4... | collective-permute-start | bytes 221192 | tf_op jit(solution)/shard_map/ppermute | solution.py:525
  6.1 13.1 %collective-permute-start.10 = (bf16[128,1024]{1,0:T(8,128)(2,1)}, bf16[128,1024]{1,0:T(8,128)(2,1)S(1)}, u32[]{:S(2)}, u32[]{:S(2)}) collective-permute-start(bf16[128,1024]{1,0:T(8,128)(2,1)} %g_hbm.1), channel_id=1, source_target_pairs={{0,1},{1,0},{2,3},{3,2},{4,5},{5,4},{6,7},{7,6},{8,9},{9,8},{10,11... | collective-permute-start | bytes 786440 | tf_op jit(solution)/shard_map/ppermute | solution.py:525
  12.1 10.9 %collective-permute-start.12 = (bf16[128,1024]{1,0:T(8,128)(2,1)S(1)}, bf16[128,1024]{1,0:T(8,128)(2,1)S(1)}, u32[]{:S(2)}, u32[]{:S(2)}) collective-permute-start(bf16[128,1024]{1,0:T(8,128)(2,1)S(1)} %collective-permute-done.11.refs_2_), channel_id=1, source_target_pairs={{0,1},{1,0},{2,3},{3,2},{4,5},{5,4},{6,7},{7,6},{8,9},{9,8},{10,11... | collective-permute-start | bytes 786440 | tf_op jit(solution)/shard_map/ppermute | solution.py:525
  12.2 14.2 %collective-permute-start = (bf16[144,512]{1,0:T(8,128)(2,1)S(1)}, bf16[144,512]{1,0:T(8,128)(2,1)S(1)}, u32[]{:S(2)}, u32[]{:S(2)}) collective-permute-start(bf16[144,512]{1,0:T(8,128)(2,1)S(1)} %get-tuple-element.35), channel_id=1, source_target_pairs={{0,128},{128,0},{1,129},{129,1},{2,130},{130,2},{3,131},{131,3},{4... | collective-permute-start | bytes 442376 | tf_op jit(solution)/shard_map/ppermute | solution.py:525
  12.9 18.1 %collective-permute-start.5 = (bf16[288,256]{1,0:T(8,128)(2,1)S(1)}, bf16[288,256]{1,0:T(8,128)(2,1)S(1)}, u32[]{:S(2)}, u32[]{:S(2)}) collective-permute-start(bf16[288,256]{1,0:T(8,128)(2,1)S(1)} %constant_dynamic-update-slice_fusion.1.refs_4_.refs_12_), channel_id=1, source_target_pairs={{0,96},{16,112},{32,0},{48,16},{64,32},{80,48},{96,64},{112,80},{1... | collective-permute-start | bytes 442376 | tf_op jit(solution)/shard_map/ppermute | solution.py:525
  19.2 15.0 %collective-permute-start.6 = (bf16[288,256]{1,0:T(8,128)(2,1)S(1)}, bf16[288,256]{1,0:T(8,128)(2,1)S(1)}, u32[]{:S(2)}, u32[]{:S(2)}) collective-permute-start(bf16[288,256]{1,0:T(8,128)(2,1)S(1)} %constant_dynamic-update-slice_fusion.1.refs_4_.refs_12_), channel_id=1, source_target_pairs={{0,32},{16,48},{32,64},{48,80},{64,96},{80,112},{96,0},{112,16},{1... | collective-permute-start | bytes 442376 | tf_op jit(solution)/shard_map/ppermute | solution.py:525
  19.2 16.1 %collective-permute-start.9 = (bf16[288,256]{1,0:T(8,128)(2,1)S(1)}, bf16[288,256]{1,0:T(8,128)(2,1)S(1)}, u32[]{:S(2)}, u32[]{:S(2)}) collective-permute-start(bf16[288,256]{1,0:T(8,128)(2,1)S(1)} %constant_dynamic-update-slice_fusion.1.refs_4_.refs_12_), channel_id=1, source_target_pairs={{0,64},{16,80},{32,96},{48,112},{64,0},{80,16},{96,32},{112,48},{1... | collective-permute-start | bytes 442376 | tf_op jit(solution)/shard_map/ppermute | solution.py:525
  24.9 11.5 %collective-permute-start.13 = (bf16[128,512]{1,0:T(8,128)(2,1)S(1)}, bf16[128,512]{1,0:T(8,128)(2,1)S(1)}, u32[]{:S(2)}, u32[]{:S(2)}) collective-permute-start(bf16[128,512]{1,0:T(8,128)(2,1)S(1)} %get-tuple-element.45), channel_id=1, source_target_pairs={{0,128},{128,0},{1,129},{129,1},{2,130},{130,2},{3,131},{131,3},{4... | collective-permute-start | bytes 393224 | tf_op jit(solution)/shard_map/ppermute | solution.py:525
  26.4 15.1 %collective-permute-start.1 = (bf16[288,512]{1,0:T(8,128)(2,1)S(1)}, bf16[288,512]{1,0:T(8,128)(2,1)S(1)}, u32[]{:S(2)}, u32[]{:S(2)}) collective-permute-start(bf16[288,512]{1,0:T(8,128)(2,1)S(1)} %constant_dynamic-update-slice_fusion.2.refs_0_.refs_4_), channel_id=1, source_target_pairs={{0,12},{4,0},{8,4},{12,8},{1,13},{5,1},{9,5},{13,9},{2,14},{6,2},{... | collective-permute-start | bytes 884744 | tf_op jit(solution)/shard_map/ppermute | solution.py:525
  31.0 14.6 %collective-permute-start.2 = (bf16[288,512]{1,0:T(8,128)(2,1)S(1)}, bf16[288,512]{1,0:T(8,128)(2,1)S(1)}, u32[]{:S(2)}, u32[]{:S(2)}) collective-permute-start(bf16[288,512]{1,0:T(8,128)(2,1)S(1)} %constant_dynamic-update-slice_fusion.2.refs_0_.refs_4_), channel_id=1, source_target_pairs={{0,8},{4,12},{8,0},{12,4},{1,9},{5,13},{9,1},{13,5},{2,10},{6,14},... | collective-permute-start | bytes 884744 | tf_op jit(solution)/shard_map/ppermute | solution.py:525
  34.2 14.5 %collective-permute-start.3 = (bf16[288,512]{1,0:T(8,128)(2,1)S(1)}, bf16[288,512]{1,0:T(8,128)(2,1)S(1)}, u32[]{:S(2)}, u32[]{:S(2)}) collective-permute-start(bf16[288,512]{1,0:T(8,128)(2,1)S(1)} %constant_dynamic-update-slice_fusion.2.refs_0_.refs_4_), channel_id=1, source_target_pairs={{0,4},{4,8},{8,12},{12,0},{1,5},{5,9},{9,13},{13,1},{2,6},{6,10},{... | collective-permute-start | bytes 884744 | tf_op jit(solution)/shard_map/ppermute | solution.py:525
  35.2 15.2 %collective-permute-start.7 = (bf16[576,256]{1,0:T(8,128)(2,1)S(1)}, bf16[576,256]{1,0:T(8,128)(2,1)S(1)}, u32[]{:S(2)}, u32[]{:S(2)}) collective-permute-start(bf16[576,256]{1,0:T(8,128)(2,1)S(1)} %get-tuple-element.69), channel_id=1, source_target_pairs={{0,112},{16,0},{32,16},{48,32},{64,48},{80,64},{96,80},{112,96},{1... | collective-permute-start | bytes 884744 | tf_op jit(solution)/shard_map/ppermute | solution.py:525
  36.4 14.1 %collective-permute-start.8 = (bf16[576,256]{1,0:T(8,128)(2,1)S(1)}, bf16[576,256]{1,0:T(8,128)(2,1)S(1)}, u32[]{:S(2)}, u32[]{:S(2)}) collective-permute-start(bf16[576,256]{1,0:T(8,128)(2,1)S(1)} %get-tuple-element.68), channel_id=1, source_target_pairs={{0,16},{16,32},{32,48},{48,64},{64,80},{80,96},{96,112},{112,0},{1... | collective-permute-start | bytes 884744 | tf_op jit(solution)/shard_map/ppermute | solution.py:525
  41.5 16.9 %collective-permute-start.14 = (bf16[256,512]{1,0:T(8,128)(2,1)S(1)}, bf16[256,512]{1,0:T(8,128)(2,1)S(1)}, u32[]{:S(2)}, u32[]{:S(2)}) collective-permute-start(bf16[256,512]{1,0:T(8,128)(2,1)S(1)} %constant_dynamic-update-slice_fusion.refs_0_.refs_8_), channel_id=1, source_target_pairs={{0,12},{4,0},{8,4},{12,8},{1,13},{5,1},{9,5},{13,9},{2,14},{6,2},{... | collective-permute-start | bytes 786440 | tf_op jit(solution)/shard_map/ppermute | solution.py:525
  45.6 12.8 %collective-permute-start.15 = (bf16[256,512]{1,0:T(8,128)(2,1)S(1)}, bf16[256,512]{1,0:T(8,128)(2,1)S(1)}, u32[]{:S(2)}, u32[]{:S(2)}) collective-permute-start(bf16[256,512]{1,0:T(8,128)(2,1)S(1)} %constant_dynamic-update-slice_fusion.refs_0_.refs_8_), channel_id=1, source_target_pairs={{0,8},{4,12},{8,0},{12,4},{1,9},{5,13},{9,1},{13,5},{2,10},{6,14},... | collective-permute-start | bytes 786440 | tf_op jit(solution)/shard_map/ppermute | solution.py:525
  48.7 11.3 %collective-permute-start.16 = (bf16[256,512]{1,0:T(8,128)(2,1)S(1)}, bf16[256,512]{1,0:T(8,128)(2,1)S(1)}, u32[]{:S(2)}, u32[]{:S(2)}) collective-permute-start(bf16[256,512]{1,0:T(8,128)(2,1)S(1)} %constant_dynamic-update-slice_fusion.refs_0_.refs_8_), channel_id=1, source_target_pairs={{0,4},{4,8},{8,12},{12,0},{1,5},{5,9},{9,13},{13,1},{2,6},{6,10},{... | collective-permute-start | bytes 786440 | tf_op jit(solution)/shard_map/ppermute | solution.py:525
  60.4 4.4 %collective-permute-start.17 = (f32[6,2048]{1,0:T(8,128)S(1)}, f32[6,2048]{1,0:T(8,128)S(1)}, u32[]{:S(2)}, u32[]{:S(2)}) collective-permute-start(f32[6,2048]{1,0:T(8,128)S(1)} %weighted.1.refs_0_), channel_id=1, source_target_pairs={{0,12},{4,0},{8,4},{12,8},{1,13},{5,1},{9,5},{13,9},{2,14},{6,2},{... | collective-permute-start | bytes 147464 | tf_op jit(solution)/shard_map/ppermute | solution.py:525
  60.5 6.0 %collective-permute-start.18 = (f32[6,2048]{1,0:T(8,128)S(1)}, f32[6,2048]{1,0:T(8,128)S(1)}, u32[]{:S(2)}, u32[]{:S(2)}) collective-permute-start(f32[6,2048]{1,0:T(8,128)S(1)} %weighted.1.refs_0_), channel_id=1, source_target_pairs={{0,8},{4,12},{8,0},{12,4},{1,9},{5,13},{9,1},{13,5},{2,10},{6,14},... | collective-permute-start | bytes 147464 | tf_op jit(solution)/shard_map/ppermute | solution.py:525
  62.6 5.5 %collective-permute-start.19 = (f32[6,2048]{1,0:T(8,128)S(1)}, f32[6,2048]{1,0:T(8,128)S(1)}, u32[]{:S(2)}, u32[]{:S(2)}) collective-permute-start(f32[6,2048]{1,0:T(8,128)S(1)} %weighted.1.refs_0_), channel_id=1, source_target_pairs={{0,4},{4,8},{8,12},{12,0},{1,5},{5,9},{9,13},{13,1},{2,6},{6,10},{... | collective-permute-start | bytes 147464 | tf_op jit(solution)/shard_map/ppermute | solution.py:525
  74.6 13.6 %collective-permute-start.20 = (bf16[512,256]{1,0:T(8,128)(2,1)S(1)}, bf16[512,256]{1,0:T(8,128)(2,1)S(1)}, u32[]{:S(2)}, u32[]{:S(2)}) collective-permute-start(bf16[512,256]{1,0:T(8,128)(2,1)S(1)} %get-tuple-element.52), channel_id=1, source_target_pairs={{0,16},{16,32},{32,48},{48,64},{64,80},{80,96},{96,112},{112,0},{1... | collective-permute-start | bytes 786440 | tf_op jit(solution)/shard_map/ppermute | solution.py:525
  75.7 12.6 %collective-permute-start.21 = (bf16[512,256]{1,0:T(8,128)(2,1)S(1)}, bf16[512,256]{1,0:T(8,128)(2,1)S(1)}, u32[]{:S(2)}, u32[]{:S(2)}) collective-permute-start(bf16[512,256]{1,0:T(8,128)(2,1)S(1)} %get-tuple-element.54), channel_id=1, source_target_pairs={{0,112},{16,0},{32,16},{48,32},{64,48},{80,64},{96,80},{112,96},{1... | collective-permute-start | bytes 786440 | tf_op jit(solution)/shard_map/ppermute | solution.py:525
  78.0 20.6 %collective-permute-start.25 = (bf16[256,256]{1,0:T(8,128)(2,1)S(1)}, bf16[256,256]{1,0:T(8,128)(2,1)S(1)}, u32[]{:S(2)}, u32[]{:S(2)}) collective-permute-start(bf16[256,256]{1,0:T(8,128)(2,1)S(1)} %get-tuple-element.60), channel_id=1, source_target_pairs={{0,64},{16,80},{32,96},{48,112},{64,0},{80,16},{96,32},{112,48},{1... | collective-permute-start | bytes 393224 | tf_op jit(solution)/shard_map/ppermute | solution.py:525
  88.3 16.0 %collective-permute-start.22 = (bf16[256,512]{1,0:T(8,128)(2,1)S(1)}, bf16[256,512]{1,0:T(8,128)(2,1)S(1)}, u32[]{:S(2)}, u32[]{:S(2)}) collective-permute-start(bf16[256,512]{1,0:T(8,128)(2,1)S(1)} %get-tuple-element.56), channel_id=1, source_target_pairs={{0,4},{4,8},{8,12},{12,0},{1,5},{5,9},{9,13},{13,1},{2,6},{6,10},{... | collective-permute-start | bytes 786440 | tf_op jit(solution)/shard_map/ppermute | solution.py:525
  88.4 15.9 %collective-permute-start.23 = (bf16[256,512]{1,0:T(8,128)(2,1)S(1)}, bf16[256,512]{1,0:T(8,128)(2,1)S(1)}, u32[]{:S(2)}, u32[]{:S(2)}) collective-permute-start(bf16[256,512]{1,0:T(8,128)(2,1)S(1)} %get-tuple-element.57), channel_id=1, source_target_pairs={{0,8},{4,12},{8,0},{12,4},{1,9},{5,13},{9,1},{13,5},{2,10},{6,14},... | collective-permute-start | bytes 786440 | tf_op jit(solution)/shard_map/ppermute | solution.py:525
  91.1 13.3 %collective-permute-start.24 = (bf16[256,512]{1,0:T(8,128)(2,1)S(1)}, bf16[256,512]{1,0:T(8,128)(2,1)S(1)}, u32[]{:S(2)}, u32[]{:S(2)}) collective-permute-start(bf16[256,512]{1,0:T(8,128)(2,1)S(1)} %get-tuple-element.58), channel_id=1, source_target_pairs={{0,12},{4,0},{8,4},{12,8},{1,13},{5,1},{9,5},{13,9},{2,14},{6,2},{... | collective-permute-start | bytes 786440 | tf_op jit(solution)/shard_map/ppermute | solution.py:525
  92.3 8.8 %collective-permute-start.26 = (bf16[256,256]{1,0:T(8,128)(2,1)S(1)}, bf16[256,256]{1,0:T(8,128)(2,1)S(1)}, u32[]{:S(2)}, u32[]{:S(2)}) collective-permute-start(bf16[256,256]{1,0:T(8,128)(2,1)S(1)} %get-tuple-element.61), channel_id=1, source_target_pairs={{0,32},{16,48},{32,64},{48,80},{64,96},{80,112},{96,0},{112,16},{1... | collective-permute-start | bytes 393224 | tf_op jit(solution)/shard_map/ppermute | solution.py:525
  98.5 5.9 %collective-permute-start.27 = (bf16[256,256]{1,0:T(8,128)(2,1)S(1)}, bf16[256,256]{1,0:T(8,128)(2,1)S(1)}, u32[]{:S(2)}, u32[]{:S(2)}) collective-permute-start(bf16[256,256]{1,0:T(8,128)(2,1)S(1)} %get-tuple-element.62), channel_id=1, source_target_pairs={{0,96},{16,112},{32,0},{48,16},{64,32},{80,48},{96,64},{112,80},{1... | collective-permute-start | bytes 393224 | tf_op jit(solution)/shard_map/ppermute | solution.py:525
  104.6 5.8 %collective-permute-start.28 = (bf16[128,768]{1,0:T(8,128)(2,1)S(1)}, bf16[128,768]{1,0:T(8,128)(2,1)S(1)}, u32[]{:S(2)}, u32[]{:S(2)}) collective-permute-start(bf16[128,768]{1,0:T(8,128)(2,1)S(1)} %get-tuple-element.64), channel_id=1, source_target_pairs={{0,128},{128,0},{1,129},{129,1},{2,130},{130,2},{3,131},{131,3},{4... | collective-permute-start | bytes 589832 | tf_op jit(solution)/shard_map/ppermute | solution.py:525

commit v2 on v1

--- a/solution.py
+++ b/solution.py
@@ -14,7 +14,6 @@
 XL, NZ, NY = 2, 8, 4
 PIECE = CHUNK + 16
 KEYS = NZ * CHUNK
-KT = 256
 GROUP = RATIO * HEAD
 DP = 4
 ROWS = DP * GROUP
@@ -221,32 +220,37 @@
         top = full
     low_f = low_s[pl.ds(block, 1), :]
     low = low_f.astype(jnp.int32)
-    t_low = jnp.min(low_f).astype(jnp.int32) // KT
-    t_high = (top + KT - 1) // KT
-    return low, high, t_low, t_high, jnp.max(low_f).astype(jnp.int32), full
+    c_low = jnp.min(low_f).astype(jnp.int32) // CHUNK
+    return low, high, c_low, top // CHUNK, jnp.max(low_f).astype(jnp.int32), full
 
 
 def over_tiles(lim, body):
-    low, high, t_low, t_high, max_low, full = lim
-
-    def mask(t, s):
-        kk = t * KT + lax.broadcasted_iota(jnp.int32, (KT, ROWS), 0)
+    low, high, c_low, c_high, max_low, full = lim
+
+    def mask(c, s):
+        kk = c * CHUNK + lax.broadcasted_iota(jnp.int32, s.shape, 0)
         return jnp.where((kk >= low) & (kk < high), s, NEG)
 
-    def step(t, _):
-        inside = (t * KT >= max_low) & ((t + 1) * KT <= full)
+    def step(i, _):
+        c = c_low + 2 * i
+        inside = (c * CHUNK >= max_low) & ((c + 2) * CHUNK <= full)
 
         @pl.when(inside)
         def _():
-            body(t, lambda s: s)
+            body(c, 2, lambda s: s)
 
         @pl.when(jnp.logical_not(inside))
         def _():
-            body(t, functools.partial(mask, t))
+            body(c, 2, functools.partial(mask, c))
 
         return 0
 
-    lax.fori_loop(t_low, t_high, step, 0)
+    count = jnp.maximum(c_high - c_low, 0)
+    lax.fori_loop(0, count // 2, step, 0)
+
+    @pl.when(lax.rem(count, 2) == 1)
+    def _():
+        body(c_high - 1, 1, functools.partial(mask, c_high - 1))
 
 
 def forward(scalars, q_blocks, arrays, views):
@@ -271,13 +275,13 @@
             o_ref[block] = jnp.zeros((HEAD + 16, ROWS), WIDE)
             ml_ref[pl.ds(block, 1), :] = jnp.full((1, ROWS), NEG, WIDE)
 
-            def tile(t, mask):
-                k = kc[pl.ds(2 * t, 2)].reshape(KT, HEAD)
+            def tile(c, n, mask):
+                k = kc[pl.ds(c, n)].reshape(n * CHUNK, HEAD)
                 s = mask(dot(k, qp, NT) * C2)
                 old = ml_ref[pl.ds(block, 1), :]
                 new = jnp.maximum(old, jnp.max(s, axis=0, keepdims=True))
                 p = jnp.exp2(s - new).astype(LOW)
-                v = jnp.concatenate([vt[2 * t], vt[2 * t + 1]], axis=1)
+                v = jnp.concatenate([vt[c + i] for i in range(n)], axis=1)
                 o_ref[block] = o_ref[block] * jnp.exp2(old - new) + dot(v, p)
                 ml_ref[pl.ds(block, 1), :] = new
 
@@ -392,15 +396,15 @@
             qp = qs[block]
             up = us[block]
 
-            def tile(t, mask):
-                k = kc[pl.ds(2 * t, 2)].reshape(KT, HEAD)
-                v = vc[pl.ds(2 * t, 2)].reshape(KT, HEAD)
+            def tile(c, n, mask):
+                k = kc[pl.ds(c, n)].reshape(n * CHUNK, HEAD)
+                v = vc[pl.ds(c, n)].reshape(n * CHUNK, HEAD)
                 p = jnp.exp2(mask(dot(k, qp, NT) * C2) - lse)
                 ds = (p * (dot(v, up, NT) - delta)).astype(LOW)
                 p = p.astype(LOW)
-                dv[pl.ds(2 * t, 2)] += dot(p, up).reshape(2, CHUNK, HEAD)
-                dk[pl.ds(2 * t, 2)] += dot(ds, qp).reshape(2, CHUNK, HEAD)
-                kt_tile = jnp.concatenate([kt[2 * t], kt[2 * t + 1]], axis=1)
+                dv[pl.ds(c, n)] += dot(p, up).reshape(n, CHUNK, HEAD)
+                dk[pl.ds(c, n)] += dot(ds, qp).reshape(n, CHUNK, HEAD)
+                kt_tile = jnp.concatenate([kt[c + i] for i in range(n)], axis=1)
                 dqt[block] += dot(kt_tile, ds)
 
             over_tiles(limits(cls, block, xl, z, y, low_s), tile)
@@ -553,8 +557,9 @@
     kv = below(kv_own, kv_in)
     kv_up2 = shift(kv, "z", NZ, 2)
     kv_down2 = shift(kv, "z", NZ, -2)
-    kv_4 = shift(kv, "z", NZ, 4)
     q_blocks = along_y(below(q_own, q_in))
+    kv_late, _ = lax.optimization_barrier((kv, q_blocks[0]))
+    kv_4 = shift(kv_late, "z", NZ, 4)
     kv_up = shift(jnp.concatenate([kv, kv_up2], axis=0), "z", NZ, 1)
     kv_down = shift(jnp.concatenate([kv, kv_down2], axis=0), "z", NZ, -1)
     second = 2 * PIECE

time: 114 us -> 113 us (level); the launches traced: 112 us -> 113 us
  Pallas kernels: 30.5 us -> 19.7 us
  starting transfers between devices: 53.8 us -> 62.3 us
  waiting for transfers between devices: 26.2 us -> 29.8 us
    ppermute x29, starting transfers between devices: 53.8 us -> 62.3 us  [shift(): return lax.ppermute(x, axis, [(i, (i - d) % size) for i in range(size)])]
    pallas_call x2, Pallas kernels: 13.8 us -> 7.57 us  [backward(): pl.pallas_call(kernel, in_specs=[sspec()] + [vspec()] * (12 + n + len(sta...]
    pallas_call x1, Pallas kernels: 7.96 us -> 3.36 us  [forward(): pl.pallas_call(kernel, in_specs=[sspec()] + [vspec()] * (4 + len(arrays))...]
    ppermute x29, waiting for transfers between devices: 26.2 us -> 29.8 us  [shift(): return lax.ppermute(x, axis, [(i, (i - d) % size) for i in range(size)])]
  transfers between devices with their start and end apart: 29 -> 29, of which waited for: 11 -> 11; matrix products, arithmetic and copies ran while one was open for 0% -> 0% of each run, Pallas kernels for 20% -> 13%
where the time goes in v2:
time: 113 us
  starting transfers between devices  62.3 us (55%)
  waiting for transfers between devices  29.8 us (26%)
  Pallas kernels  19.7 us (17%)
    ppermute x29, starting transfers between devices, shift(): return lax.ppermute(x, axis, [(i, (i - d) % size) for i in range(size)])  62.3 us
    ppermute x29, waiting for transfers between devices, shift(): return lax.ppermute(x, axis, [(i, (i - d) % size) for i in range(size)])  29.8 us
    pallas_call x2, Pallas kernels, backward(): pl.pallas_call(kernel, in_specs=[sspec()] + [vspec()] * (12 + n + len(sta...  7.57 us
    pallas_call x1, Pallas kernels, stage(): pl.pallas_call(kernel, in_specs=[hspec()] * 2, out_specs=[vspec()] * 2, o...  3.4 us
    pallas_call x1, Pallas kernels, forward(): pl.pallas_call(kernel, in_specs=[sspec()] + [vspec()] * (4 + len(arrays))...  3.36 us
  transfers between devices with their start and end apart: 29, of which 11 were waited for; matrix products, arithmetic and copies ran while one was open for 0% of the time, Pallas kernels for 13%

profile of v2, /device:TPU:2, one launch (start us, length us, event | category | flops | bytes accessed | tf_op | source)
XLA Modules:
  0.0 112.8 jit_solution(55733951499216124)
XLA Ops:
  0.6 2.2 %collective-permute-start.11 = (bf16[128,1024]{1,0:T(8,128)(2,1)}, bf16[128,1024]{1,0:T(8,128)(2,1)S(1)}, u32[]{:S(2)}, u32[]{:S(2)}) collective-permute-start(bf16[128,1024]{1,0:T(8,128)(2,1)} %g_hbm.1), channel_id=1, source_target_pairs={{0,2},{2,0},{1,3},{3,1},{4,6},{6,4},{5,7},{7,5},{8,10},{10,8},{9,1... | collective-permute-start | bytes 786440 | tf_op jit(solution)/shard_map/ppermute | solution.py:529
  2.9 1.6 %prepare.1 = (bf16[288,512]{1,0:T(8,128)(2,1)S(1)}, bf16[144,512]{1,0:T(8,128)(2,1)S(1)}, bf16[288,256]{1,0:T(8,128)(2,1)S(1)}, bf16[144,256]{1,0:T(8,128)(2,1)S(1)}) custom-call(s32[4]{0:T(128)S(1)} %pad_add_fusion.sc, bf16[128,1024]{1,0:T(8,128)(2,1)} %q_ref.1, bf16[128,256]{1,0:T(8,128)(2,1)} %k_ref.1, bf16[128,256]{1,0:T(8,128)(2,1)} %v_ref.1, ...), custom_call_target="tpu_custom_call" | custom-call | tf_op jit(solution)/shard_map/prepare/pallas_call | solution.py:85
  4.6 1.5 %collective-permute-start.4 = (bf16[144,256]{1,0:T(8,128)(2,1)S(1)}, bf16[144,256]{1,0:T(8,128)(2,1)S(1)}, u32[]{:S(2)}, u32[]{:S(2)}) collective-permute-start(bf16[144,256]{1,0:T(8,128)(2,1)S(1)} %get-tuple-element.38), channel_id=1, source_target_pairs={{0,128},{128,0},{1,129},{129,1},{2,130},{130,2},{3,131},{131,3},{4... | collective-permute-start | bytes 221192 | tf_op jit(solution)/shard_map/ppermute | solution.py:529
  6.1 0.6 collective-permute-start
  6.7 3.4 %stage.1 = (bf16[4096,1024]{1,0:T(8,128)(2,1)S(1)}, bf16[128,1024]{1,0:T(8,128)(2,1)S(1)}) custom-call(bf16[4096,1024]{1,0:T(8,128)(2,1)} %w_hbm.1, bf16[128,1024]{1,0:T(8,128)(2,1)} %g_hbm.1), custom_call_target="tpu_custom_call" | custom-call | bytes 16777216 | tf_op jit(solution)/shard_map/stage/pallas_call | solution.py:112
  10.1 3.2 %collective-permute-done.4 = bf16[144,256]{1,0:T(8,128)(2,1)S(1)} collective-permute-done((bf16[144,256]{1,0:T(8,128)(2,1)S(1)}, bf16[144,256]{1,0:T(8,128)(2,1)S(1)}, u32[]{:S(2)}, u32[]{:S(2)}) %collective-permute-start.4) | collective-permute-done | bytes 73760 | tf_op jit(solution)/shard_map/ppermute | solution.py:529
  13.2 0.1 collective-permute-start.12
  13.3 6.4 %collective-permute-start.5 = (bf16[288,256]{1,0:T(8,128)(2,1)S(1)}, bf16[288,256]{1,0:T(8,128)(2,1)S(1)}, u32[]{:S(2)}, u32[]{:S(2)}) collective-permute-start(bf16[288,256]{1,0:T(8,128)(2,1)S(1)} %constant_dynamic-update-slice_fusion.1.refs_4_.refs_12_), channel_id=1, source_target_pairs={{0,96},{16,112},{32,0},{48,16},{64,32},{80,48},{96,64},{112,80},{1... | collective-permute-start | bytes 442376 | tf_op jit(solution)/shard_map/ppermute | solution.py:529
  19.7 3.9 %collective-permute-start.9 = (bf16[288,256]{1,0:T(8,128)(2,1)S(1)}, bf16[288,256]{1,0:T(8,128)(2,1)S(1)}, u32[]{:S(2)}, u32[]{:S(2)}) collective-permute-start(bf16[288,256]{1,0:T(8,128)(2,1)S(1)} %constant_dynamic-update-slice_fusion.1.refs_4_.refs_12_), channel_id=1, source_target_pairs={{0,64},{16,80},{32,96},{48,112},{64,0},{80,16},{96,32},{112,48},{1... | collective-permute-start | bytes 442376 | tf_op jit(solution)/shard_map/ppermute | solution.py:529
  23.7 1.8 %upstream.1 = (bf16[256,512]{1,0:T(8,128)(2,1)S(1)}, bf16[128,512]{1,0:T(8,128)(2,1)S(1)}) custom-call(s32[4]{0:T(128)S(1)} %pad_add_fusion.sc, bf16[128,1024]{1,0:T(8,128)(2,1)S(1)} %get-tuple-element.39.refs_0_, bf16[128,1024]{1,0:T(8,128)(2,1)S(1)} %collective-permute-done.10.refs_1_, bf16[128,1024]{1,0:T(8,128)(2,1)S(1)} %collective-permute-done.11.refs_2_, ...), custom_call_target="tpu_custom_call" | custom-call | tf_op jit(solution)/shard_map/upstream/pallas_call | solution.py:142
  25.5 0.7 collective-permute-start.13
  26.2 3.0 %collective-permute-start.1 = (bf16[288,512]{1,0:T(8,128)(2,1)S(1)}, bf16[288,512]{1,0:T(8,128)(2,1)S(1)}, u32[]{:S(2)}, u32[]{:S(2)}) collective-permute-start(bf16[288,512]{1,0:T(8,128)(2,1)S(1)} %constant_dynamic-update-slice_fusion.2.refs_0_.refs_4_), channel_id=1, source_target_pairs={{0,12},{4,0},{8,4},{12,8},{1,13},{5,1},{9,5},{13,9},{2,14},{6,2},{... | collective-permute-start | bytes 884744 | tf_op jit(solution)/shard_map/ppermute | solution.py:529
  29.2 2.6 %collective-permute-done.5.refs_5_.refs_13_ = bf16[288,256]{1,0:T(8,128)(2,1)S(1)} collective-permute-done((bf16[288,256]{1,0:T(8,128)(2,1)S(1)}, bf16[288,256]{1,0:T(8,128)(2,1)S(1)}, u32[]{:S(2)}, u32[]{:S(2)}) %collective-permute-start.5) | collective-permute-done | bytes 147488 | tf_op jit(solution)/shard_map/ppermute | solution.py:529
  31.8 3.2 %collective-permute-start.2 = (bf16[288,512]{1,0:T(8,128)(2,1)S(1)}, bf16[288,512]{1,0:T(8,128)(2,1)S(1)}, u32[]{:S(2)}, u32[]{:S(2)}) collective-permute-start(bf16[288,512]{1,0:T(8,128)(2,1)S(1)} %constant_dynamic-update-slice_fusion.2.refs_0_.refs_4_), channel_id=1, source_target_pairs={{0,8},{4,12},{8,0},{12,4},{1,9},{5,13},{9,1},{13,5},{2,10},{6,14},... | collective-permute-start | bytes 884744 | tf_op jit(solution)/shard_map/ppermute | solution.py:529
  35.0 0.8 collective-permute-start.3
  35.9 1.3 %collective-permute-start.7 = (bf16[576,256]{1,0:T(8,128)(2,1)S(1)}, bf16[576,256]{1,0:T(8,128)(2,1)S(1)}, u32[]{:S(2)}, u32[]{:S(2)}) collective-permute-start(bf16[576,256]{1,0:T(8,128)(2,1)S(1)} %get-tuple-element.71), channel_id=1, source_target_pairs={{0,112},{16,0},{32,16},{48,32},{64,48},{80,64},{96,80},{112,96},{1... | collective-permute-start | bytes 884744 | tf_op jit(solution)/shard_map/ppermute | solution.py:529
  37.2 2.8 %collective-permute-start.8 = (bf16[576,256]{1,0:T(8,128)(2,1)S(1)}, bf16[576,256]{1,0:T(8,128)(2,1)S(1)}, u32[]{:S(2)}, u32[]{:S(2)}) collective-permute-start(bf16[576,256]{1,0:T(8,128)(2,1)S(1)} %get-tuple-element.70), channel_id=1, source_target_pairs={{0,16},{16,32},{32,48},{48,64},{64,80},{80,96},{96,112},{112,0},{1... | collective-permute-start | bytes 884744 | tf_op jit(solution)/shard_map/ppermute | solution.py:529
  40.1 3.5 %collective-permute-start.14 = (bf16[256,512]{1,0:T(8,128)(2,1)S(1)}, bf16[256,512]{1,0:T(8,128)(2,1)S(1)}, u32[]{:S(2)}, u32[]{:S(2)}) collective-permute-start(bf16[256,512]{1,0:T(8,128)(2,1)S(1)} %constant_dynamic-update-slice_fusion.refs_0_.refs_8_), channel_id=1, source_target_pairs={{0,12},{4,0},{8,4},{12,8},{1,13},{5,1},{9,5},{13,9},{2,14},{6,2},{... | collective-permute-start | bytes 786440 | tf_op jit(solution)/shard_map/ppermute | solution.py:529
  43.6 2.9 %collective-permute-start.15 = (bf16[256,512]{1,0:T(8,128)(2,1)S(1)}, bf16[256,512]{1,0:T(8,128)(2,1)S(1)}, u32[]{:S(2)}, u32[]{:S(2)}) collective-permute-start(bf16[256,512]{1,0:T(8,128)(2,1)S(1)} %constant_dynamic-update-slice_fusion.refs_0_.refs_8_), channel_id=1, source_target_pairs={{0,8},{4,12},{8,0},{12,4},{1,9},{5,13},{9,1},{13,5},{2,10},{6,14},... | collective-permute-start | bytes 786440 | tf_op jit(solution)/shard_map/ppermute | solution.py:529
  46.5 3.1 %collective-permute-done.3.refs_3_.refs_7_ = bf16[288,512]{1,0:T(8,128)(2,1)S(1)} collective-permute-done((bf16[288,512]{1,0:T(8,128)(2,1)S(1)}, bf16[288,512]{1,0:T(8,128)(2,1)S(1)}, u32[]{:S(2)}, u32[]{:S(2)}) %collective-permute-start.3) | collective-permute-done | bytes 294944 | tf_op jit(solution)/shard_map/ppermute | solution.py:529
  49.6 1.7 %collective-permute-start.16 = (bf16[256,512]{1,0:T(8,128)(2,1)S(1)}, bf16[256,512]{1,0:T(8,128)(2,1)S(1)}, u32[]{:S(2)}, u32[]{:S(2)}) collective-permute-start(bf16[256,512]{1,0:T(8,128)(2,1)S(1)} %constant_dynamic-update-slice_fusion.refs_0_.refs_8_), channel_id=1, source_target_pairs={{0,4},{4,8},{8,12},{12,0},{1,5},{5,9},{9,13},{13,1},{2,6},{6,10},{... | collective-permute-start | bytes 786440 | tf_op jit(solution)/shard_map/ppermute | solution.py:529
  51.3 3.4 %forward.1 = (f32[2,144,2048]{2,1,0:T(8,128)S(1)}, f32[4,2048]{1,0:T(4,128)S(1)}) custom-call(s32[4]{0:T(128)S(1)} %pad_add_fusion.sc, bf16[288,512]{1,0:T(8,128)(2,1)S(1)} %constant_dynamic-update-slice_fusion.2.refs_0_.refs_4_, bf16[288,512]{1,0:T(8,128)(2,1)S(1)} %collective-permute-done.1.refs_1_.refs_5_, ...), custom_call_target="tpu_custom_call" | custom-call | flops 8000000000 | bytes 4194304 | tf_op jit(solution)/shard_map/forward/pallas_call | solution.py:295
  54.7 0.6 collective-permute-done.15.refs_2_.refs_10_
  55.3 4.6 %collective-permute-done.16.refs_3_.refs_11_ = bf16[256,512]{1,0:T(8,128)(2,1)S(1)} collective-permute-done((bf16[256,512]{1,0:T(8,128)(2,1)S(1)}, bf16[256,512]{1,0:T(8,128)(2,1)S(1)}, u32[]{:S(2)}, u32[]{:S(2)}) %collective-permute-start.16) | collective-permute-done | bytes 262176 | tf_op jit(solution)/shard_map/ppermute | solution.py:529
  59.9 0.4 weighted.1.refs_0_
  60.3 0.1 collective-permute-start.17
  60.4 3.2 %collective-permute-start.18 = (f32[6,2048]{1,0:T(8,128)S(1)}, f32[6,2048]{1,0:T(8,128)S(1)}, u32[]{:S(2)}, u32[]{:S(2)}) collective-permute-start(f32[6,2048]{1,0:T(8,128)S(1)} %weighted.1.refs_0_), channel_id=1, source_target_pairs={{0,8},{4,12},{8,0},{12,4},{1,9},{5,13},{9,1},{13,5},{2,10},{6,14},... | collective-permute-start | bytes 147464 | tf_op jit(solution)/shard_map/ppermute | solution.py:529
  63.6 0.5 collective-permute-start.19
  64.1 1.0 collective-permute-done.17.refs_1_
  65.2 1.2 %collective-permute-done.18.refs_2_ = f32[6,2048]{1,0:T(8,128)S(1)} collective-permute-done((f32[6,2048]{1,0:T(8,128)S(1)}, f32[6,2048]{1,0:T(8,128)S(1)}, u32[]{:S(2)}, u32[]{:S(2)}) %collective-permute-start.18) | collective-permute-done | bytes 49184 | tf_op jit(solution)/shard_map/ppermute | solution.py:529
  66.4 2.7 %collective-permute-done.19.refs_3_ = f32[6,2048]{1,0:T(8,128)S(1)} collective-permute-done((f32[6,2048]{1,0:T(8,128)S(1)}, f32[6,2048]{1,0:T(8,128)S(1)}, u32[]{:S(2)}, u32[]{:S(2)}) %collective-permute-start.19) | collective-permute-done | bytes 49184 | tf_op jit(solution)/shard_map/ppermute | solution.py:529
  69.1 3.0 %backward1.1 = (f32[2,128,2048]{2,1,0:T(8,128)S(1)}, bf16[512,256]{1,0:T(8,128)(2,1)S(1)}, bf16[512,256]{1,0:T(8,128)(2,1)S(1)}, bf16[256,256]{1,0:T(8,128)(2,1)S(1)}) custom-call(s32[4]{0:T(128)S(1)} %pad_add_fusion.sc, f32[6,2048]{1,0:T(8,128)S(1)} %weighted.1.refs_0_, f32[6,2048]{1,0:T(8,128)S(1)} %collective-permute-done.17.refs_1_, ...), custom_call_target="tpu_custom_call" | custom-call | flops 8000000000 | bytes 6291456 | tf_op jit(solution)/shard_map/backward1/pallas_call | solution.py:454
  72.1 0.1 collective-permute-start.20
  72.2 3.2 %collective-permute-start.21 = (bf16[512,256]{1,0:T(8,128)(2,1)S(1)}, bf16[512,256]{1,0:T(8,128)(2,1)S(1)}, u32[]{:S(2)}, u32[]{:S(2)}) collective-permute-start(bf16[512,256]{1,0:T(8,128)(2,1)S(1)} %get-tuple-element.56), channel_id=1, source_target_pairs={{0,112},{16,0},{32,16},{48,32},{64,48},{80,64},{96,80},{112,96},{1... | collective-permute-start | bytes 786440 | tf_op jit(solution)/shard_map/ppermute | solution.py:529
  75.4 7.8 %collective-permute-start.25 = (bf16[256,256]{1,0:T(8,128)(2,1)S(1)}, bf16[256,256]{1,0:T(8,128)(2,1)S(1)}, u32[]{:S(2)}, u32[]{:S(2)}) collective-permute-start(bf16[256,256]{1,0:T(8,128)(2,1)S(1)} %get-tuple-element.62), channel_id=1, source_target_pairs={{0,64},{16,80},{32,96},{48,112},{64,0},{80,16},{96,32},{112,48},{1... | collective-permute-start | bytes 393224 | tf_op jit(solution)/shard_map/ppermute | solution.py:529
  83.3 4.6 %backward0.1 = (f32[256,512]{1,0:T(8,128)S(1)}, bf16[256,512]{1,0:T(8,128)(2,1)S(1)}, bf16[256,512]{1,0:T(8,128)(2,1)S(1)}, bf16[256,512]{1,0:T(8,128)(2,1)S(1)}...) custom-call(s32[4]{0:T(128)S(1)} %pad_add_fusion.sc, f32[6,2048]{1,0:T(8,128)S(1)} %weighted.1.refs_0_, ...), custom_call_target="tpu_custom_call" | custom-call | flops 8000000000 | bytes 6291456 | tf_op jit(solution)/shard_map/backward0/pallas_call | solution.py:454
  87.8 0.1 convert_add_fusion
  87.9 0.1 collective-permute-start.22
  88.0 3.0 %collective-permute-start.23 = (bf16[256,512]{1,0:T(8,128)(2,1)S(1)}, bf16[256,512]{1,0:T(8,128)(2,1)S(1)}, u32[]{:S(2)}, u32[]{:S(2)}) collective-permute-start(bf16[256,512]{1,0:T(8,128)(2,1)S(1)} %get-tuple-element.59), channel_id=1, source_target_pairs={{0,8},{4,12},{8,0},{12,4},{1,9},{5,13},{9,1},{13,5},{2,10},{6,14},... | collective-permute-start | bytes 786440 | tf_op jit(solution)/shard_map/ppermute | solution.py:529
  91.0 1.9 %collective-permute-start.24 = (bf16[256,512]{1,0:T(8,128)(2,1)S(1)}, bf16[256,512]{1,0:T(8,128)(2,1)S(1)}, u32[]{:S(2)}, u32[]{:S(2)}) collective-permute-start(bf16[256,512]{1,0:T(8,128)(2,1)S(1)} %get-tuple-element.60), channel_id=1, source_target_pairs={{0,12},{4,0},{8,4},{12,8},{1,13},{5,1},{9,5},{13,9},{2,14},{6,2},{... | collective-permute-start | bytes 786440 | tf_op jit(solution)/shard_map/ppermute | solution.py:529
  92.9 5.9 %collective-permute-start.26 = (bf16[256,256]{1,0:T(8,128)(2,1)S(1)}, bf16[256,256]{1,0:T(8,128)(2,1)S(1)}, u32[]{:S(2)}, u32[]{:S(2)}) collective-permute-start(bf16[256,256]{1,0:T(8,128)(2,1)S(1)} %get-tuple-element.63), channel_id=1, source_target_pairs={{0,32},{16,48},{32,64},{48,80},{64,96},{80,112},{96,0},{112,16},{1... | collective-permute-start | bytes 393224 | tf_op jit(solution)/shard_map/ppermute | solution.py:529
  98.9 1.0 collective-permute-start.27
  99.9 4.3 %collective-permute-done.26.refs_6_ = bf16[256,256]{1,0:T(8,128)(2,1)S(1)} collective-permute-done((bf16[256,256]{1,0:T(8,128)(2,1)S(1)}, bf16[256,256]{1,0:T(8,128)(2,1)S(1)}, u32[]{:S(2)}, u32[]{:S(2)}) %collective-permute-start.26) | collective-permute-done | bytes 131104 | tf_op jit(solution)/shard_map/ppermute | solution.py:529
  104.2 1.3 %collective-permute-done.27.refs_7_ = bf16[256,256]{1,0:T(8,128)(2,1)S(1)} collective-permute-done((bf16[256,256]{1,0:T(8,128)(2,1)S(1)}, bf16[256,256]{1,0:T(8,128)(2,1)S(1)}, u32[]{:S(2)}, u32[]{:S(2)}) %collective-permute-start.27) | collective-permute-done | bytes 131104 | tf_op jit(solution)/shard_map/ppermute | solution.py:529
  105.5 0.2 settle.1
  105.7 0.7 collective-permute-start.28
  106.4 5.1 %collective-permute-done.28.back_ref = bf16[128,768]{1,0:T(8,128)(2,1)S(1)} collective-permute-done((bf16[128,768]{1,0:T(8,128)(2,1)S(1)}, bf16[128,768]{1,0:T(8,128)(2,1)S(1)}, u32[]{:S(2)}, u32[]{:S(2)}) %collective-permute-start.28) | collective-permute-done | bytes 196640 | tf_op jit(solution)/shard_map/ppermute | solution.py:529
  111.5 1.3 %join.1 = (bf16[128,1024]{1,0:T(8,128)(2,1)}, bf16[128,256]{1,0:T(8,128)(2,1)}, bf16[128,256]{1,0:T(8,128)(2,1)}) custom-call(s32[4]{0:T(128)S(1)} %pad_add_fusion.sc, bf16[128,768]{1,0:T(8,128)(2,1)S(1)} %get-tuple-element.65.keep_ref, bf16[128,768]{1,0:T(8,128)(2,1)S(1)} %collective-permute-done.28.back_ref), custom_call_target="tpu_custom_call" | custom-call | tf_op jit(solution)/shard_map/join/pallas_call | solution.py:514
  (25 shorter events, 0.2 us)
Async XLA Ops:
  0.6 12.6 %collective-permute-start.11 = (bf16[128,1024]{1,0:T(8,128)(2,1)}, bf16[128,1024]{1,0:T(8,128)(2,1)S(1)}, u32[]{:S(2)}, u32[]{:S(2)}) collective-permute-start(bf16[128,1024]{1,0:T(8,128)(2,1)} %g_hbm.1), channel_id=1, source_target_pairs={{0,2},{2,0},{1,3},{3,1},{4,6},{6,4},{5,7},{7,5},{8,10},{10,8},{9,1... | collective-permute-start | bytes 786440 | tf_op jit(solution)/shard_map/ppermute | solution.py:529
  4.6 8.7 %collective-permute-start.4 = (bf16[144,256]{1,0:T(8,128)(2,1)S(1)}, bf16[144,256]{1,0:T(8,128)(2,1)S(1)}, u32[]{:S(2)}, u32[]{:S(2)}) collective-permute-start(bf16[144,256]{1,0:T(8,128)(2,1)S(1)} %get-tuple-element.38), channel_id=1, source_target_pairs={{0,128},{128,0},{1,129},{129,1},{2,130},{130,2},{3,131},{131,3},{4... | collective-permute-start | bytes 221192 | tf_op jit(solution)/shard_map/ppermute | solution.py:529
  6.1 17.6 %collective-permute-start.10 = (bf16[128,1024]{1,0:T(8,128)(2,1)}, bf16[128,1024]{1,0:T(8,128)(2,1)S(1)}, u32[]{:S(2)}, u32[]{:S(2)}) collective-permute-start(bf16[128,1024]{1,0:T(8,128)(2,1)} %g_hbm.1), channel_id=1, source_target_pairs={{0,1},{1,0},{2,3},{3,2},{4,5},{5,4},{6,7},{7,6},{8,9},{9,8},{10,11... | collective-permute-start | bytes 786440 | tf_op jit(solution)/shard_map/ppermute | solution.py:529
  6.1 13.7 %collective-permute-start = (bf16[144,512]{1,0:T(8,128)(2,1)S(1)}, bf16[144,512]{1,0:T(8,128)(2,1)S(1)}, u32[]{:S(2)}, u32[]{:S(2)}) collective-permute-start(bf16[144,512]{1,0:T(8,128)(2,1)S(1)} %get-tuple-element.36), channel_id=1, source_target_pairs={{0,128},{128,0},{1,129},{129,1},{2,130},{130,2},{3,131},{131,3},{4... | collective-permute-start | bytes 442376 | tf_op jit(solution)/shard_map/ppermute | solution.py:529
  13.2 10.4 %collective-permute-start.12 = (bf16[128,1024]{1,0:T(8,128)(2,1)S(1)}, bf16[128,1024]{1,0:T(8,128)(2,1)S(1)}, u32[]{:S(2)}, u32[]{:S(2)}) collective-permute-start(bf16[128,1024]{1,0:T(8,128)(2,1)S(1)} %collective-permute-done.11.refs_2_), channel_id=1, source_target_pairs={{0,1},{1,0},{2,3},{3,2},{4,5},{5,4},{6,7},{7,6},{8,9},{9,8},{10,11... | collective-permute-start | bytes 786440 | tf_op jit(solution)/shard_map/ppermute | solution.py:529
  13.3 18.5 %collective-permute-start.5 = (bf16[288,256]{1,0:T(8,128)(2,1)S(1)}, bf16[288,256]{1,0:T(8,128)(2,1)S(1)}, u32[]{:S(2)}, u32[]{:S(2)}) collective-permute-start(bf16[288,256]{1,0:T(8,128)(2,1)S(1)} %constant_dynamic-update-slice_fusion.1.refs_4_.refs_12_), channel_id=1, source_target_pairs={{0,96},{16,112},{32,0},{48,16},{64,32},{80,48},{96,64},{112,80},{1... | collective-permute-start | bytes 442376 | tf_op jit(solution)/shard_map/ppermute | solution.py:529
  19.7 15.3 %collective-permute-start.6 = (bf16[288,256]{1,0:T(8,128)(2,1)S(1)}, bf16[288,256]{1,0:T(8,128)(2,1)S(1)}, u32[]{:S(2)}, u32[]{:S(2)}) collective-permute-start(bf16[288,256]{1,0:T(8,128)(2,1)S(1)} %constant_dynamic-update-slice_fusion.1.refs_4_.refs_12_), channel_id=1, source_target_pairs={{0,32},{16,48},{32,64},{48,80},{64,96},{80,112},{96,0},{112,16},{1... | collective-permute-start | bytes 442376 | tf_op jit(solution)/shard_map/ppermute | solution.py:529
  19.7 16.1 %collective-permute-start.9 = (bf16[288,256]{1,0:T(8,128)(2,1)S(1)}, bf16[288,256]{1,0:T(8,128)(2,1)S(1)}, u32[]{:S(2)}, u32[]{:S(2)}) collective-permute-start(bf16[288,256]{1,0:T(8,128)(2,1)S(1)} %constant_dynamic-update-slice_fusion.1.refs_4_.refs_12_), channel_id=1, source_target_pairs={{0,64},{16,80},{32,96},{48,112},{64,0},{80,16},{96,32},{112,48},{1... | collective-permute-start | bytes 442376 | tf_op jit(solution)/shard_map/ppermute | solution.py:529
  25.5 11.7 %collective-permute-start.13 = (bf16[128,512]{1,0:T(8,128)(2,1)S(1)}, bf16[128,512]{1,0:T(8,128)(2,1)S(1)}, u32[]{:S(2)}, u32[]{:S(2)}) collective-permute-start(bf16[128,512]{1,0:T(8,128)(2,1)S(1)} %get-tuple-element.47), channel_id=1, source_target_pairs={{0,128},{128,0},{1,129},{129,1},{2,130},{130,2},{3,131},{131,3},{4... | collective-permute-start | bytes 393224 | tf_op jit(solution)/shard_map/ppermute | solution.py:529
  26.2 13.9 %collective-permute-start.1 = (bf16[288,512]{1,0:T(8,128)(2,1)S(1)}, bf16[288,512]{1,0:T(8,128)(2,1)S(1)}, u32[]{:S(2)}, u32[]{:S(2)}) collective-permute-start(bf16[288,512]{1,0:T(8,128)(2,1)S(1)} %constant_dynamic-update-slice_fusion.2.refs_0_.refs_4_), channel_id=1, source_target_pairs={{0,12},{4,0},{8,4},{12,8},{1,13},{5,1},{9,5},{13,9},{2,14},{6,2},{... | collective-permute-start | bytes 884744 | tf_op jit(solution)/shard_map/ppermute | solution.py:529
  31.8 11.8 %collective-permute-start.2 = (bf16[288,512]{1,0:T(8,128)(2,1)S(1)}, bf16[288,512]{1,0:T(8,128)(2,1)S(1)}, u32[]{:S(2)}, u32[]{:S(2)}) collective-permute-start(bf16[288,512]{1,0:T(8,128)(2,1)S(1)} %constant_dynamic-update-slice_fusion.2.refs_0_.refs_4_), channel_id=1, source_target_pairs={{0,8},{4,12},{8,0},{12,4},{1,9},{5,13},{9,1},{13,5},{2,10},{6,14},... | collective-permute-start | bytes 884744 | tf_op jit(solution)/shard_map/ppermute | solution.py:529
  35.0 14.5 %collective-permute-start.3 = (bf16[288,512]{1,0:T(8,128)(2,1)S(1)}, bf16[288,512]{1,0:T(8,128)(2,1)S(1)}, u32[]{:S(2)}, u32[]{:S(2)}) collective-permute-start(bf16[288,512]{1,0:T(8,128)(2,1)S(1)} %constant_dynamic-update-slice_fusion.2.refs_0_.refs_4_), channel_id=1, source_target_pairs={{0,4},{4,8},{8,12},{12,0},{1,5},{5,9},{9,13},{13,1},{2,6},{6,10},{... | collective-permute-start | bytes 884744 | tf_op jit(solution)/shard_map/ppermute | solution.py:529
  35.9 15.5 %collective-permute-start.7 = (bf16[576,256]{1,0:T(8,128)(2,1)S(1)}, bf16[576,256]{1,0:T(8,128)(2,1)S(1)}, u32[]{:S(2)}, u32[]{:S(2)}) collective-permute-start(bf16[576,256]{1,0:T(8,128)(2,1)S(1)} %get-tuple-element.71), channel_id=1, source_target_pairs={{0,112},{16,0},{32,16},{48,32},{64,48},{80,64},{96,80},{112,96},{1... | collective-permute-start | bytes 884744 | tf_op jit(solution)/shard_map/ppermute | solution.py:529
  37.2 14.1 %collective-permute-start.8 = (bf16[576,256]{1,0:T(8,128)(2,1)S(1)}, bf16[576,256]{1,0:T(8,128)(2,1)S(1)}, u32[]{:S(2)}, u32[]{:S(2)}) collective-permute-start(bf16[576,256]{1,0:T(8,128)(2,1)S(1)} %get-tuple-element.70), channel_id=1, source_target_pairs={{0,16},{16,32},{32,48},{48,64},{64,80},{80,96},{96,112},{112,0},{1... | collective-permute-start | bytes 884744 | tf_op jit(solution)/shard_map/ppermute | solution.py:529
  40.1 14.6 %collective-permute-start.14 = (bf16[256,512]{1,0:T(8,128)(2,1)S(1)}, bf16[256,512]{1,0:T(8,128)(2,1)S(1)}, u32[]{:S(2)}, u32[]{:S(2)}) collective-permute-start(bf16[256,512]{1,0:T(8,128)(2,1)S(1)} %constant_dynamic-update-slice_fusion.refs_0_.refs_8_), channel_id=1, source_target_pairs={{0,12},{4,0},{8,4},{12,8},{1,13},{5,1},{9,5},{13,9},{2,14},{6,2},{... | collective-permute-start | bytes 786440 | tf_op jit(solution)/shard_map/ppermute | solution.py:529
  43.6 11.7 %collective-permute-start.15 = (bf16[256,512]{1,0:T(8,128)(2,1)S(1)}, bf16[256,512]{1,0:T(8,128)(2,1)S(1)}, u32[]{:S(2)}, u32[]{:S(2)}) collective-permute-start(bf16[256,512]{1,0:T(8,128)(2,1)S(1)} %constant_dynamic-update-slice_fusion.refs_0_.refs_8_), channel_id=1, source_target_pairs={{0,8},{4,12},{8,0},{12,4},{1,9},{5,13},{9,1},{13,5},{2,10},{6,14},... | collective-permute-start | bytes 786440 | tf_op jit(solution)/shard_map/ppermute | solution.py:529
  49.6 10.3 %collective-permute-start.16 = (bf16[256,512]{1,0:T(8,128)(2,1)S(1)}, bf16[256,512]{1,0:T(8,128)(2,1)S(1)}, u32[]{:S(2)}, u32[]{:S(2)}) collective-permute-start(bf16[256,512]{1,0:T(8,128)(2,1)S(1)} %constant_dynamic-update-slice_fusion.refs_0_.refs_8_), channel_id=1, source_target_pairs={{0,4},{4,8},{8,12},{12,0},{1,5},{5,9},{9,13},{13,1},{2,6},{6,10},{... | collective-permute-start | bytes 786440 | tf_op jit(solution)/shard_map/ppermute | solution.py:529
  60.3 4.9 %collective-permute-start.17 = (f32[6,2048]{1,0:T(8,128)S(1)}, f32[6,2048]{1,0:T(8,128)S(1)}, u32[]{:S(2)}, u32[]{:S(2)}) collective-permute-start(f32[6,2048]{1,0:T(8,128)S(1)} %weighted.1.refs_0_), channel_id=1, source_target_pairs={{0,12},{4,0},{8,4},{12,8},{1,13},{5,1},{9,5},{13,9},{2,14},{6,2},{... | collective-permute-start | bytes 147464 | tf_op jit(solution)/shard_map/ppermute | solution.py:529
  60.4 6.0 %collective-permute-start.18 = (f32[6,2048]{1,0:T(8,128)S(1)}, f32[6,2048]{1,0:T(8,128)S(1)}, u32[]{:S(2)}, u32[]{:S(2)}) collective-permute-start(f32[6,2048]{1,0:T(8,128)S(1)} %weighted.1.refs_0_), channel_id=1, source_target_pairs={{0,8},{4,12},{8,0},{12,4},{1,9},{5,13},{9,1},{13,5},{2,10},{6,14},... | collective-permute-start | bytes 147464 | tf_op jit(solution)/shard_map/ppermute | solution.py:529
  63.6 5.5 %collective-permute-start.19 = (f32[6,2048]{1,0:T(8,128)S(1)}, f32[6,2048]{1,0:T(8,128)S(1)}, u32[]{:S(2)}, u32[]{:S(2)}) collective-permute-start(f32[6,2048]{1,0:T(8,128)S(1)} %weighted.1.refs_0_), channel_id=1, source_target_pairs={{0,4},{4,8},{8,12},{12,0},{1,5},{5,9},{9,13},{13,1},{2,6},{6,10},{... | collective-permute-start | bytes 147464 | tf_op jit(solution)/shard_map/ppermute | solution.py:529
  72.1 15.7 %collective-permute-start.20 = (bf16[512,256]{1,0:T(8,128)(2,1)S(1)}, bf16[512,256]{1,0:T(8,128)(2,1)S(1)}, u32[]{:S(2)}, u32[]{:S(2)}) collective-permute-start(bf16[512,256]{1,0:T(8,128)(2,1)S(1)} %get-tuple-element.54), channel_id=1, source_target_pairs={{0,16},{16,32},{32,48},{48,64},{64,80},{80,96},{96,112},{112,0},{1... | collective-permute-start | bytes 786440 | tf_op jit(solution)/shard_map/ppermute | solution.py:529
  72.2 15.6 %collective-permute-start.21 = (bf16[512,256]{1,0:T(8,128)(2,1)S(1)}, bf16[512,256]{1,0:T(8,128)(2,1)S(1)}, u32[]{:S(2)}, u32[]{:S(2)}) collective-permute-start(bf16[512,256]{1,0:T(8,128)(2,1)S(1)} %get-tuple-element.56), channel_id=1, source_target_pairs={{0,112},{16,0},{32,16},{48,32},{64,48},{80,64},{96,80},{112,96},{1... | collective-permute-start | bytes 786440 | tf_op jit(solution)/shard_map/ppermute | solution.py:529
  75.4 23.4 %collective-permute-start.25 = (bf16[256,256]{1,0:T(8,128)(2,1)S(1)}, bf16[256,256]{1,0:T(8,128)(2,1)S(1)}, u32[]{:S(2)}, u32[]{:S(2)}) collective-permute-start(bf16[256,256]{1,0:T(8,128)(2,1)S(1)} %get-tuple-element.62), channel_id=1, source_target_pairs={{0,64},{16,80},{32,96},{48,112},{64,0},{80,16},{96,32},{112,48},{1... | collective-permute-start | bytes 393224 | tf_op jit(solution)/shard_map/ppermute | solution.py:529
  87.9 17.6 %collective-permute-start.22 = (bf16[256,512]{1,0:T(8,128)(2,1)S(1)}, bf16[256,512]{1,0:T(8,128)(2,1)S(1)}, u32[]{:S(2)}, u32[]{:S(2)}) collective-permute-start(bf16[256,512]{1,0:T(8,128)(2,1)S(1)} %get-tuple-element.58), channel_id=1, source_target_pairs={{0,4},{4,8},{8,12},{12,0},{1,5},{5,9},{9,13},{13,1},{2,6},{6,10},{... | collective-permute-start | bytes 786440 | tf_op jit(solution)/shard_map/ppermute | solution.py:529
  88.0 17.5 %collective-permute-start.23 = (bf16[256,512]{1,0:T(8,128)(2,1)S(1)}, bf16[256,512]{1,0:T(8,128)(2,1)S(1)}, u32[]{:S(2)}, u32[]{:S(2)}) collective-permute-start(bf16[256,512]{1,0:T(8,128)(2,1)S(1)} %get-tuple-element.59), channel_id=1, source_target_pairs={{0,8},{4,12},{8,0},{12,4},{1,9},{5,13},{9,1},{13,5},{2,10},{6,14},... | collective-permute-start | bytes 786440 | tf_op jit(solution)/shard_map/ppermute | solution.py:529
  91.0 14.5 %collective-permute-start.24 = (bf16[256,512]{1,0:T(8,128)(2,1)S(1)}, bf16[256,512]{1,0:T(8,128)(2,1)S(1)}, u32[]{:S(2)}, u32[]{:S(2)}) collective-permute-start(bf16[256,512]{1,0:T(8,128)(2,1)S(1)} %get-tuple-element.60), channel_id=1, source_target_pairs={{0,12},{4,0},{8,4},{12,8},{1,13},{5,1},{9,5},{13,9},{2,14},{6,2},{... | collective-permute-start | bytes 786440 | tf_op jit(solution)/shard_map/ppermute | solution.py:529
  92.9 11.3 %collective-permute-start.26 = (bf16[256,256]{1,0:T(8,128)(2,1)S(1)}, bf16[256,256]{1,0:T(8,128)(2,1)S(1)}, u32[]{:S(2)}, u32[]{:S(2)}) collective-permute-start(bf16[256,256]{1,0:T(8,128)(2,1)S(1)} %get-tuple-element.63), channel_id=1, source_target_pairs={{0,32},{16,48},{32,64},{48,80},{64,96},{80,112},{96,0},{112,16},{1... | collective-permute-start | bytes 393224 | tf_op jit(solution)/shard_map/ppermute | solution.py:529
  98.9 6.7 %collective-permute-start.27 = (bf16[256,256]{1,0:T(8,128)(2,1)S(1)}, bf16[256,256]{1,0:T(8,128)(2,1)S(1)}, u32[]{:S(2)}, u32[]{:S(2)}) collective-permute-start(bf16[256,256]{1,0:T(8,128)(2,1)S(1)} %get-tuple-element.64), channel_id=1, source_target_pairs={{0,96},{16,112},{32,0},{48,16},{64,32},{80,48},{96,64},{112,80},{1... | collective-permute-start | bytes 393224 | tf_op jit(solution)/shard_map/ppermute | solution.py:529
  105.7 5.8 %collective-permute-start.28 = (bf16[128,768]{1,0:T(8,128)(2,1)S(1)}, bf16[128,768]{1,0:T(8,128)(2,1)S(1)}, u32[]{:S(2)}, u32[]{:S(2)}) collective-permute-start(bf16[128,768]{1,0:T(8,128)(2,1)S(1)} %get-tuple-element.66), channel_id=1, source_target_pairs={{0,128},{128,0},{1,129},{129,1},{2,130},{130,2},{3,131},{131,3},{4... | collective-permute-start | bytes 589832 | tf_op jit(solution)/shard_map/ppermute | solution.py:529

commit v3 on v2

--- a/solution.py
+++ b/solution.py
@@ -582,10 +582,12 @@
     )
     got_up = shift(bundle_up, "z", NZ, -1)
     got_down = shift(bundle_down, "z", NZ, 1)
-    got_4 = shift(dkv_4, "z", NZ, 4)
     *dq, dkv, dkv_up2, dkv_down2 = backward(
         0, scalars, stats, q_blocks, u_blocks, even, even_views, dq_state
     )
+
+    dkv_4, _ = lax.optimization_barrier((dkv_4, dkv))
+    got_4 = shift(dkv_4, "z", NZ, 4)
 
     near, further = slice(0, 2 * CHUNK), slice(2 * CHUNK, None)
     dkv = dkv + got_up[near].astype(WIDE) + got_down[near].astype(WIDE)

time: 113 us -> 113 us (level)
  Pallas kernels: 19.7 us -> 23.4 us
  waiting for transfers between devices: 29.8 us -> 26.7 us
    ppermute x29, waiting for transfers between devices: 29.8 us -> 26.7 us  [shift(): return lax.ppermute(x, axis, [(i, (i - d) % size) for i in range(size)])]
    pallas_call x2, Pallas kernels: 7.57 us -> 9.68 us  [backward(): pl.pallas_call(kernel, in_specs=[sspec()] + [vspec()] * (12 + n + len(sta...]
    pallas_call x1, Pallas kernels: 3.36 us -> 4.97 us  [forward(): pl.pallas_call(kernel, in_specs=[sspec()] + [vspec()] * (4 + len(arrays))...]
  transfers between devices with their start and end apart: 29 -> 29, of which waited for: 11 -> 10; matrix products, arithmetic and copies ran while one was open for 0% -> 0% of each run, Pallas kernels for 13% -> 15%
where the time goes in v3:
time: 113 us
  starting transfers between devices  62.2 us (55%)
  waiting for transfers between devices  26.7 us (24%)
  Pallas kernels  23.4 us (21%)
    ppermute x29, starting transfers between devices, shift(): return lax.ppermute(x, axis, [(i, (i - d) % size) for i in range(size)])  62.2 us
    ppermute x29, waiting for transfers between devices, shift(): return lax.ppermute(x, axis, [(i, (i - d) % size) for i in range(size)])  26.7 us
    pallas_call x2, Pallas kernels, backward(): pl.pallas_call(kernel, in_specs=[sspec()] + [vspec()] * (12 + n + len(sta...  9.68 us
    pallas_call x1, Pallas kernels, forward(): pl.pallas_call(kernel, in_specs=[sspec()] + [vspec()] * (4 + len(arrays))...  4.97 us
    pallas_call x1, Pallas kernels, stage(): pl.pallas_call(kernel, in_specs=[hspec()] * 2, out_specs=[vspec()] * 2, o...  3.4 us
  transfers between devices with their start and end apart: 29, of which 10 were waited for; matrix products, arithmetic and copies ran while one was open for 0% of the time, Pallas kernels for 15%

profile of v3, /device:TPU:2, one launch (start us, length us, event | category | flops | bytes accessed | tf_op | source)
XLA Modules:
  0.0 113.4 jit_solution(9878590735735480859)
XLA Ops:
  0.6 2.2 %collective-permute-start.11 = (bf16[128,1024]{1,0:T(8,128)(2,1)}, bf16[128,1024]{1,0:T(8,128)(2,1)S(1)}, u32[]{:S(2)}, u32[]{:S(2)}) collective-permute-start(bf16[128,1024]{1,0:T(8,128)(2,1)} %g_hbm.1), channel_id=1, source_target_pairs={{0,2},{2,0},{1,3},{3,1},{4,6},{6,4},{5,7},{7,5},{8,10},{10,8},{9,1... | collective-permute-start | bytes 786440 | tf_op jit(solution)/shard_map/ppermute | solution.py:529
  2.8 0.1 pad_add_fusion.sc
  2.9 1.6 %prepare.1 = (bf16[288,512]{1,0:T(8,128)(2,1)S(1)}, bf16[144,512]{1,0:T(8,128)(2,1)S(1)}, bf16[288,256]{1,0:T(8,128)(2,1)S(1)}, bf16[144,256]{1,0:T(8,128)(2,1)S(1)}) custom-call(s32[4]{0:T(128)S(1)} %pad_add_fusion.sc, bf16[128,1024]{1,0:T(8,128)(2,1)} %q_ref.1, bf16[128,256]{1,0:T(8,128)(2,1)} %k_ref.1, bf16[128,256]{1,0:T(8,128)(2,1)} %v_ref.1, ...), custom_call_target="tpu_custom_call" | custom-call | tf_op jit(solution)/shard_map/prepare/pallas_call | solution.py:85
  4.6 1.5 %collective-permute-start.4 = (bf16[144,256]{1,0:T(8,128)(2,1)S(1)}, bf16[144,256]{1,0:T(8,128)(2,1)S(1)}, u32[]{:S(2)}, u32[]{:S(2)}) collective-permute-start(bf16[144,256]{1,0:T(8,128)(2,1)S(1)} %get-tuple-element.39), channel_id=1, source_target_pairs={{0,128},{128,0},{1,129},{129,1},{2,130},{130,2},{3,131},{131,3},{4... | collective-permute-start | bytes 221192 | tf_op jit(solution)/shard_map/ppermute | solution.py:529
  6.1 0.6 collective-permute-start
  6.7 3.4 %stage.1 = (bf16[4096,1024]{1,0:T(8,128)(2,1)S(1)}, bf16[128,1024]{1,0:T(8,128)(2,1)S(1)}) custom-call(bf16[4096,1024]{1,0:T(8,128)(2,1)} %w_hbm.1, bf16[128,1024]{1,0:T(8,128)(2,1)} %g_hbm.1), custom_call_target="tpu_custom_call" | custom-call | bytes 16777216 | tf_op jit(solution)/shard_map/stage/pallas_call | solution.py:112
  10.1 3.2 %collective-permute-done.4 = bf16[144,256]{1,0:T(8,128)(2,1)S(1)} collective-permute-done((bf16[144,256]{1,0:T(8,128)(2,1)S(1)}, bf16[144,256]{1,0:T(8,128)(2,1)S(1)}, u32[]{:S(2)}, u32[]{:S(2)}) %collective-permute-start.4) | collective-permute-done | bytes 73760 | tf_op jit(solution)/shard_map/ppermute | solution.py:529
  13.2 0.1 collective-permute-start.12
  13.3 6.4 %collective-permute-start.5 = (bf16[288,256]{1,0:T(8,128)(2,1)S(1)}, bf16[288,256]{1,0:T(8,128)(2,1)S(1)}, u32[]{:S(2)}, u32[]{:S(2)}) collective-permute-start(bf16[288,256]{1,0:T(8,128)(2,1)S(1)} %constant_dynamic-update-slice_fusion.1.refs_4_.refs_12_), channel_id=1, source_target_pairs={{0,96},{16,112},{32,0},{48,16},{64,32},{80,48},{96,64},{112,80},{1... | collective-permute-start | bytes 442376 | tf_op jit(solution)/shard_map/ppermute | solution.py:529
  19.7 3.9 %collective-permute-start.9 = (bf16[288,256]{1,0:T(8,128)(2,1)S(1)}, bf16[288,256]{1,0:T(8,128)(2,1)S(1)}, u32[]{:S(2)}, u32[]{:S(2)}) collective-permute-start(bf16[288,256]{1,0:T(8,128)(2,1)S(1)} %constant_dynamic-update-slice_fusion.1.refs_4_.refs_12_), channel_id=1, source_target_pairs={{0,64},{16,80},{32,96},{48,112},{64,0},{80,16},{96,32},{112,48},{1... | collective-permute-start | bytes 442376 | tf_op jit(solution)/shard_map/ppermute | solution.py:529
  23.7 1.8 %upstream.1 = (bf16[256,512]{1,0:T(8,128)(2,1)S(1)}, bf16[128,512]{1,0:T(8,128)(2,1)S(1)}) custom-call(s32[4]{0:T(128)S(1)} %pad_add_fusion.sc, bf16[128,1024]{1,0:T(8,128)(2,1)S(1)} %get-tuple-element.40.refs_0_, bf16[128,1024]{1,0:T(8,128)(2,1)S(1)} %collective-permute-done.10.refs_1_, bf16[128,1024]{1,0:T(8,128)(2,1)S(1)} %collective-permute-done.11.refs_2_, ...), custom_call_target="tpu_custom_call" | custom-call | tf_op jit(solution)/shard_map/upstream/pallas_call | solution.py:142
  25.5 0.7 collective-permute-start.13
  26.2 3.0 %collective-permute-start.1 = (bf16[288,512]{1,0:T(8,128)(2,1)S(1)}, bf16[288,512]{1,0:T(8,128)(2,1)S(1)}, u32[]{:S(2)}, u32[]{:S(2)}) collective-permute-start(bf16[288,512]{1,0:T(8,128)(2,1)S(1)} %constant_dynamic-update-slice_fusion.2.refs_0_.refs_4_), channel_id=1, source_target_pairs={{0,12},{4,0},{8,4},{12,8},{1,13},{5,1},{9,5},{13,9},{2,14},{6,2},{... | collective-permute-start | bytes 884744 | tf_op jit(solution)/shard_map/ppermute | solution.py:529
  29.2 2.6 %collective-permute-done.5.refs_5_.refs_13_ = bf16[288,256]{1,0:T(8,128)(2,1)S(1)} collective-permute-done((bf16[288,256]{1,0:T(8,128)(2,1)S(1)}, bf16[288,256]{1,0:T(8,128)(2,1)S(1)}, u32[]{:S(2)}, u32[]{:S(2)}) %collective-permute-start.5) | collective-permute-done | bytes 147488 | tf_op jit(solution)/shard_map/ppermute | solution.py:529
  31.8 3.2 %collective-permute-start.2 = (bf16[288,512]{1,0:T(8,128)(2,1)S(1)}, bf16[288,512]{1,0:T(8,128)(2,1)S(1)}, u32[]{:S(2)}, u32[]{:S(2)}) collective-permute-start(bf16[288,512]{1,0:T(8,128)(2,1)S(1)} %constant_dynamic-update-slice_fusion.2.refs_0_.refs_4_), channel_id=1, source_target_pairs={{0,8},{4,12},{8,0},{12,4},{1,9},{5,13},{9,1},{13,5},{2,10},{6,14},... | collective-permute-start | bytes 884744 | tf_op jit(solution)/shard_map/ppermute | solution.py:529
  35.0 0.8 collective-permute-start.3
  35.9 1.3 %collective-permute-start.7 = (bf16[576,256]{1,0:T(8,128)(2,1)S(1)}, bf16[576,256]{1,0:T(8,128)(2,1)S(1)}, u32[]{:S(2)}, u32[]{:S(2)}) collective-permute-start(bf16[576,256]{1,0:T(8,128)(2,1)S(1)} %get-tuple-element.73), channel_id=1, source_target_pairs={{0,112},{16,0},{32,16},{48,32},{64,48},{80,64},{96,80},{112,96},{1... | collective-permute-start | bytes 884744 | tf_op jit(solution)/shard_map/ppermute | solution.py:529
  37.2 2.8 %collective-permute-start.8 = (bf16[576,256]{1,0:T(8,128)(2,1)S(1)}, bf16[576,256]{1,0:T(8,128)(2,1)S(1)}, u32[]{:S(2)}, u32[]{:S(2)}) collective-permute-start(bf16[576,256]{1,0:T(8,128)(2,1)S(1)} %get-tuple-element.72), channel_id=1, source_target_pairs={{0,16},{16,32},{32,48},{48,64},{64,80},{80,96},{96,112},{112,0},{1... | collective-permute-start | bytes 884744 | tf_op jit(solution)/shard_map/ppermute | solution.py:529
  40.1 3.5 %collective-permute-start.14 = (bf16[256,512]{1,0:T(8,128)(2,1)S(1)}, bf16[256,512]{1,0:T(8,128)(2,1)S(1)}, u32[]{:S(2)}, u32[]{:S(2)}) collective-permute-start(bf16[256,512]{1,0:T(8,128)(2,1)S(1)} %constant_dynamic-update-slice_fusion.refs_0_.refs_8_), channel_id=1, source_target_pairs={{0,12},{4,0},{8,4},{12,8},{1,13},{5,1},{9,5},{13,9},{2,14},{6,2},{... | collective-permute-start | bytes 786440 | tf_op jit(solution)/shard_map/ppermute | solution.py:529
  43.6 2.9 %collective-permute-start.15 = (bf16[256,512]{1,0:T(8,128)(2,1)S(1)}, bf16[256,512]{1,0:T(8,128)(2,1)S(1)}, u32[]{:S(2)}, u32[]{:S(2)}) collective-permute-start(bf16[256,512]{1,0:T(8,128)(2,1)S(1)} %constant_dynamic-update-slice_fusion.refs_0_.refs_8_), channel_id=1, source_target_pairs={{0,8},{4,12},{8,0},{12,4},{1,9},{5,13},{9,1},{13,5},{2,10},{6,14},... | collective-permute-start | bytes 786440 | tf_op jit(solution)/shard_map/ppermute | solution.py:529
  46.5 3.1 %collective-permute-done.3.refs_3_.refs_7_ = bf16[288,512]{1,0:T(8,128)(2,1)S(1)} collective-permute-done((bf16[288,512]{1,0:T(8,128)(2,1)S(1)}, bf16[288,512]{1,0:T(8,128)(2,1)S(1)}, u32[]{:S(2)}, u32[]{:S(2)}) %collective-permute-start.3) | collective-permute-done | bytes 294944 | tf_op jit(solution)/shard_map/ppermute | solution.py:529
  49.6 1.7 %collective-permute-start.16 = (bf16[256,512]{1,0:T(8,128)(2,1)S(1)}, bf16[256,512]{1,0:T(8,128)(2,1)S(1)}, u32[]{:S(2)}, u32[]{:S(2)}) collective-permute-start(bf16[256,512]{1,0:T(8,128)(2,1)S(1)} %constant_dynamic-update-slice_fusion.refs_0_.refs_8_), channel_id=1, source_target_pairs={{0,4},{4,8},{8,12},{12,0},{1,5},{5,9},{9,13},{13,1},{2,6},{6,10},{... | collective-permute-start | bytes 786440 | tf_op jit(solution)/shard_map/ppermute | solution.py:529
  51.3 5.0 %forward.1 = (f32[2,144,2048]{2,1,0:T(8,128)S(1)}, f32[4,2048]{1,0:T(4,128)S(1)}) custom-call(s32[4]{0:T(128)S(1)} %pad_add_fusion.sc, bf16[288,512]{1,0:T(8,128)(2,1)S(1)} %constant_dynamic-update-slice_fusion.2.refs_0_.refs_4_, bf16[288,512]{1,0:T(8,128)(2,1)S(1)} %collective-permute-done.1.refs_1_.refs_5_, ...), custom_call_target="tpu_custom_call" | custom-call | flops 8000000000 | bytes 4194304 | tf_op jit(solution)/shard_map/forward/pallas_call | solution.py:295
  56.3 3.6 %collective-permute-done.16.refs_3_.refs_11_ = bf16[256,512]{1,0:T(8,128)(2,1)S(1)} collective-permute-done((bf16[256,512]{1,0:T(8,128)(2,1)S(1)}, bf16[256,512]{1,0:T(8,128)(2,1)S(1)}, u32[]{:S(2)}, u32[]{:S(2)}) %collective-permute-start.16) | collective-permute-done | bytes 262176 | tf_op jit(solution)/shard_map/ppermute | solution.py:529
  59.9 0.4 weighted.1.refs_0_
  60.3 0.1 collective-permute-start.17
  60.4 3.2 %collective-permute-start.18 = (f32[6,2048]{1,0:T(8,128)S(1)}, f32[6,2048]{1,0:T(8,128)S(1)}, u32[]{:S(2)}, u32[]{:S(2)}) collective-permute-start(f32[6,2048]{1,0:T(8,128)S(1)} %weighted.1.refs_0_), channel_id=1, source_target_pairs={{0,8},{4,12},{8,0},{12,4},{1,9},{5,13},{9,1},{13,5},{2,10},{6,14},... | collective-permute-start | bytes 147464 | tf_op jit(solution)/shard_map/ppermute | solution.py:529
  63.6 0.5 collective-permute-start.19
  64.1 1.0 collective-permute-done.17.refs_1_
  65.2 1.2 %collective-permute-done.18.refs_2_ = f32[6,2048]{1,0:T(8,128)S(1)} collective-permute-done((f32[6,2048]{1,0:T(8,128)S(1)}, f32[6,2048]{1,0:T(8,128)S(1)}, u32[]{:S(2)}, u32[]{:S(2)}) %collective-permute-start.18) | collective-permute-done | bytes 49184 | tf_op jit(solution)/shard_map/ppermute | solution.py:529
  66.4 2.7 %collective-permute-done.19.refs_3_ = f32[6,2048]{1,0:T(8,128)S(1)} collective-permute-done((f32[6,2048]{1,0:T(8,128)S(1)}, f32[6,2048]{1,0:T(8,128)S(1)}, u32[]{:S(2)}, u32[]{:S(2)}) %collective-permute-start.19) | collective-permute-done | bytes 49184 | tf_op jit(solution)/shard_map/ppermute | solution.py:529
  69.1 4.5 %backward1.1 = (f32[2,128,2048]{2,1,0:T(8,128)S(1)}, bf16[512,256]{1,0:T(8,128)(2,1)S(1)}, bf16[512,256]{1,0:T(8,128)(2,1)S(1)}, bf16[256,256]{1,0:T(8,128)(2,1)S(1)}) custom-call(s32[4]{0:T(128)S(1)} %pad_add_fusion.sc, f32[6,2048]{1,0:T(8,128)S(1)} %weighted.1.refs_0_, f32[6,2048]{1,0:T(8,128)S(1)} %collective-permute-done.17.refs_1_, ...), custom_call_target="tpu_custom_call" | custom-call | flops 8000000000 | bytes 6291456 | tf_op jit(solution)/shard_map/backward1/pallas_call | solution.py:454
  73.6 0.1 collective-permute-start.20
  73.7 5.1 %collective-permute-start.21 = (bf16[512,256]{1,0:T(8,128)(2,1)S(1)}, bf16[512,256]{1,0:T(8,128)(2,1)S(1)}, u32[]{:S(2)}, u32[]{:S(2)}) collective-permute-start(bf16[512,256]{1,0:T(8,128)(2,1)S(1)} %get-tuple-element.57), channel_id=1, source_target_pairs={{0,112},{16,0},{32,16},{48,32},{64,48},{80,64},{96,80},{112,96},{1... | collective-permute-start | bytes 786440 | tf_op jit(solution)/shard_map/ppermute | solution.py:529
  78.8 5.2 %backward0.1 = (f32[256,512]{1,0:T(8,128)S(1)}, bf16[256,512]{1,0:T(8,128)(2,1)S(1)}, bf16[256,512]{1,0:T(8,128)(2,1)S(1)}, bf16[256,512]{1,0:T(8,128)(2,1)S(1)}...) custom-call(s32[4]{0:T(128)S(1)} %pad_add_fusion.sc, f32[6,2048]{1,0:T(8,128)S(1)} %weighted.1.refs_0_, ...), custom_call_target="tpu_custom_call" | custom-call | flops 8000000000 | bytes 6291456 | tf_op jit(solution)/shard_map/backward0/pallas_call | solution.py:454
  84.0 4.6 %collective-permute-start.25 = (bf16[256,256]{1,0:T(8,128)(2,1)S(1)}, bf16[256,256]{1,0:T(8,128)(2,1)S(1)}, u32[]{:S(2)}, u32[]{:S(2)}) collective-permute-start(bf16[256,256]{1,0:T(8,128)(2,1)S(1)} %get-tuple-element.64), channel_id=1, source_target_pairs={{0,64},{16,80},{32,96},{48,112},{64,0},{80,16},{96,32},{112,48},{1... | collective-permute-start | bytes 393224 | tf_op jit(solution)/shard_map/ppermute | solution.py:529
  88.6 0.1 convert_add_fusion
  88.7 0.1 collective-permute-start.22
  88.8 4.0 %collective-permute-start.23 = (bf16[256,512]{1,0:T(8,128)(2,1)S(1)}, bf16[256,512]{1,0:T(8,128)(2,1)S(1)}, u32[]{:S(2)}, u32[]{:S(2)}) collective-permute-start(bf16[256,512]{1,0:T(8,128)(2,1)S(1)} %get-tuple-element.60), channel_id=1, source_target_pairs={{0,8},{4,12},{8,0},{12,4},{1,9},{5,13},{9,1},{13,5},{2,10},{6,14},... | collective-permute-start | bytes 786440 | tf_op jit(solution)/shard_map/ppermute | solution.py:529
  92.9 0.2 collective-permute-start.24
  93.1 6.0 %collective-permute-start.26 = (bf16[256,256]{1,0:T(8,128)(2,1)S(1)}, bf16[256,256]{1,0:T(8,128)(2,1)S(1)}, u32[]{:S(2)}, u32[]{:S(2)}) collective-permute-start(bf16[256,256]{1,0:T(8,128)(2,1)S(1)} %get-tuple-element.65), channel_id=1, source_target_pairs={{0,32},{16,48},{32,64},{48,80},{64,96},{80,112},{96,0},{112,16},{1... | collective-permute-start | bytes 393224 | tf_op jit(solution)/shard_map/ppermute | solution.py:529
  99.0 2.8 %collective-permute-start.27 = (bf16[256,256]{1,0:T(8,128)(2,1)S(1)}, bf16[256,256]{1,0:T(8,128)(2,1)S(1)}, u32[]{:S(2)}, u32[]{:S(2)}) collective-permute-start(bf16[256,256]{1,0:T(8,128)(2,1)S(1)} %get-tuple-element.66), channel_id=1, source_target_pairs={{0,96},{16,112},{32,0},{48,16},{64,32},{80,48},{96,64},{112,80},{1... | collective-permute-start | bytes 393224 | tf_op jit(solution)/shard_map/ppermute | solution.py:529
  101.8 1.3 %collective-permute-done.26.refs_6_ = bf16[256,256]{1,0:T(8,128)(2,1)S(1)} collective-permute-done((bf16[256,256]{1,0:T(8,128)(2,1)S(1)}, bf16[256,256]{1,0:T(8,128)(2,1)S(1)}, u32[]{:S(2)}, u32[]{:S(2)}) %collective-permute-start.26) | collective-permute-done | bytes 131104 | tf_op jit(solution)/shard_map/ppermute | solution.py:529
  103.1 3.0 %collective-permute-done.27.refs_7_ = bf16[256,256]{1,0:T(8,128)(2,1)S(1)} collective-permute-done((bf16[256,256]{1,0:T(8,128)(2,1)S(1)}, bf16[256,256]{1,0:T(8,128)(2,1)S(1)}, u32[]{:S(2)}, u32[]{:S(2)}) %collective-permute-start.27) | collective-permute-done | bytes 131104 | tf_op jit(solution)/shard_map/ppermute | solution.py:529
  106.1 0.2 settle.1
  106.3 0.8 collective-permute-start.28
  107.1 5.0 %collective-permute-done.28.back_ref = bf16[128,768]{1,0:T(8,128)(2,1)S(1)} collective-permute-done((bf16[128,768]{1,0:T(8,128)(2,1)S(1)}, bf16[128,768]{1,0:T(8,128)(2,1)S(1)}, u32[]{:S(2)}, u32[]{:S(2)}) %collective-permute-start.28) | collective-permute-done | bytes 196640 | tf_op jit(solution)/shard_map/ppermute | solution.py:529
  112.0 1.3 %join.1 = (bf16[128,1024]{1,0:T(8,128)(2,1)}, bf16[128,256]{1,0:T(8,128)(2,1)}, bf16[128,256]{1,0:T(8,128)(2,1)}) custom-call(s32[4]{0:T(128)S(1)} %pad_add_fusion.sc, bf16[128,768]{1,0:T(8,128)(2,1)S(1)} %get-tuple-element.67.keep_ref, bf16[128,768]{1,0:T(8,128)(2,1)S(1)} %collective-permute-done.28.back_ref), custom_call_target="tpu_custom_call" | custom-call | tf_op jit(solution)/shard_map/join/pallas_call | solution.py:514
  (25 shorter events, 0.1 us)
Async XLA Ops:
  0.6 12.6 %collective-permute-start.11 = (bf16[128,1024]{1,0:T(8,128)(2,1)}, bf16[128,1024]{1,0:T(8,128)(2,1)S(1)}, u32[]{:S(2)}, u32[]{:S(2)}) collective-permute-start(bf16[128,1024]{1,0:T(8,128)(2,1)} %g_hbm.1), channel_id=1, source_target_pairs={{0,2},{2,0},{1,3},{3,1},{4,6},{6,4},{5,7},{7,5},{8,10},{10,8},{9,1... | collective-permute-start | bytes 786440 | tf_op jit(solution)/shard_map/ppermute | solution.py:529
  4.6 8.7 %collective-permute-start.4 = (bf16[144,256]{1,0:T(8,128)(2,1)S(1)}, bf16[144,256]{1,0:T(8,128)(2,1)S(1)}, u32[]{:S(2)}, u32[]{:S(2)}) collective-permute-start(bf16[144,256]{1,0:T(8,128)(2,1)S(1)} %get-tuple-element.39), channel_id=1, source_target_pairs={{0,128},{128,0},{1,129},{129,1},{2,130},{130,2},{3,131},{131,3},{4... | collective-permute-start | bytes 221192 | tf_op jit(solution)/shard_map/ppermute | solution.py:529
  6.1 17.6 %collective-permute-start.10 = (bf16[128,1024]{1,0:T(8,128)(2,1)}, bf16[128,1024]{1,0:T(8,128)(2,1)S(1)}, u32[]{:S(2)}, u32[]{:S(2)}) collective-permute-start(bf16[128,1024]{1,0:T(8,128)(2,1)} %g_hbm.1), channel_id=1, source_target_pairs={{0,1},{1,0},{2,3},{3,2},{4,5},{5,4},{6,7},{7,6},{8,9},{9,8},{10,11... | collective-permute-start | bytes 786440 | tf_op jit(solution)/shard_map/ppermute | solution.py:529
  6.1 13.7 %collective-permute-start = (bf16[144,512]{1,0:T(8,128)(2,1)S(1)}, bf16[144,512]{1,0:T(8,128)(2,1)S(1)}, u32[]{:S(2)}, u32[]{:S(2)}) collective-permute-start(bf16[144,512]{1,0:T(8,128)(2,1)S(1)} %get-tuple-element.37), channel_id=1, source_target_pairs={{0,128},{128,0},{1,129},{129,1},{2,130},{130,2},{3,131},{131,3},{4... | collective-permute-start | bytes 442376 | tf_op jit(solution)/shard_map/ppermute | solution.py:529
  13.2 10.4 %collective-permute-start.12 = (bf16[128,1024]{1,0:T(8,128)(2,1)S(1)}, bf16[128,1024]{1,0:T(8,128)(2,1)S(1)}, u32[]{:S(2)}, u32[]{:S(2)}) collective-permute-start(bf16[128,1024]{1,0:T(8,128)(2,1)S(1)} %collective-permute-done.11.refs_2_), channel_id=1, source_target_pairs={{0,1},{1,0},{2,3},{3,2},{4,5},{5,4},{6,7},{7,6},{8,9},{9,8},{10,11... | collective-permute-start | bytes 786440 | tf_op jit(solution)/shard_map/ppermute | solution.py:529
  13.3 18.5 %collective-permute-start.5 = (bf16[288,256]{1,0:T(8,128)(2,1)S(1)}, bf16[288,256]{1,0:T(8,128)(2,1)S(1)}, u32[]{:S(2)}, u32[]{:S(2)}) collective-permute-start(bf16[288,256]{1,0:T(8,128)(2,1)S(1)} %constant_dynamic-update-slice_fusion.1.refs_4_.refs_12_), channel_id=1, source_target_pairs={{0,96},{16,112},{32,0},{48,16},{64,32},{80,48},{96,64},{112,80},{1... | collective-permute-start | bytes 442376 | tf_op jit(solution)/shard_map/ppermute | solution.py:529
  19.7 15.3 %collective-permute-start.6 = (bf16[288,256]{1,0:T(8,128)(2,1)S(1)}, bf16[288,256]{1,0:T(8,128)(2,1)S(1)}, u32[]{:S(2)}, u32[]{:S(2)}) collective-permute-start(bf16[288,256]{1,0:T(8,128)(2,1)S(1)} %constant_dynamic-update-slice_fusion.1.refs_4_.refs_12_), channel_id=1, source_target_pairs={{0,32},{16,48},{32,64},{48,80},{64,96},{80,112},{96,0},{112,16},{1... | collective-permute-start | bytes 442376 | tf_op jit(solution)/shard_map/ppermute | solution.py:529
  19.7 16.1 %collective-permute-start.9 = (bf16[288,256]{1,0:T(8,128)(2,1)S(1)}, bf16[288,256]{1,0:T(8,128)(2,1)S(1)}, u32[]{:S(2)}, u32[]{:S(2)}) collective-permute-start(bf16[288,256]{1,0:T(8,128)(2,1)S(1)} %constant_dynamic-update-slice_fusion.1.refs_4_.refs_12_), channel_id=1, source_target_pairs={{0,64},{16,80},{32,96},{48,112},{64,0},{80,16},{96,32},{112,48},{1... | collective-permute-start | bytes 442376 | tf_op jit(solution)/shard_map/ppermute | solution.py:529
  25.5 11.7 %collective-permute-start.13 = (bf16[128,512]{1,0:T(8,128)(2,1)S(1)}, bf16[128,512]{1,0:T(8,128)(2,1)S(1)}, u32[]{:S(2)}, u32[]{:S(2)}) collective-permute-start(bf16[128,512]{1,0:T(8,128)(2,1)S(1)} %get-tuple-element.48), channel_id=1, source_target_pairs={{0,128},{128,0},{1,129},{129,1},{2,130},{130,2},{3,131},{131,3},{4... | collective-permute-start | bytes 393224 | tf_op jit(solution)/shard_map/ppermute | solution.py:529
  26.2 13.9 %collective-permute-start.1 = (bf16[288,512]{1,0:T(8,128)(2,1)S(1)}, bf16[288,512]{1,0:T(8,128)(2,1)S(1)}, u32[]{:S(2)}, u32[]{:S(2)}) collective-permute-start(bf16[288,512]{1,0:T(8,128)(2,1)S(1)} %constant_dynamic-update-slice_fusion.2.refs_0_.refs_4_), channel_id=1, source_target_pairs={{0,12},{4,0},{8,4},{12,8},{1,13},{5,1},{9,5},{13,9},{2,14},{6,2},{... | collective-permute-start | bytes 884744 | tf_op jit(solution)/shard_map/ppermute | solution.py:529
  31.8 11.8 %collective-permute-start.2 = (bf16[288,512]{1,0:T(8,128)(2,1)S(1)}, bf16[288,512]{1,0:T(8,128)(2,1)S(1)}, u32[]{:S(2)}, u32[]{:S(2)}) collective-permute-start(bf16[288,512]{1,0:T(8,128)(2,1)S(1)} %constant_dynamic-update-slice_fusion.2.refs_0_.refs_4_), channel_id=1, source_target_pairs={{0,8},{4,12},{8,0},{12,4},{1,9},{5,13},{9,1},{13,5},{2,10},{6,14},... | collective-permute-start | bytes 884744 | tf_op jit(solution)/shard_map/ppermute | solution.py:529
  35.0 14.5 %collective-permute-start.3 = (bf16[288,512]{1,0:T(8,128)(2,1)S(1)}, bf16[288,512]{1,0:T(8,128)(2,1)S(1)}, u32[]{:S(2)}, u32[]{:S(2)}) collective-permute-start(bf16[288,512]{1,0:T(8,128)(2,1)S(1)} %constant_dynamic-update-slice_fusion.2.refs_0_.refs_4_), channel_id=1, source_target_pairs={{0,4},{4,8},{8,12},{12,0},{1,5},{5,9},{9,13},{13,1},{2,6},{6,10},{... | collective-permute-start | bytes 884744 | tf_op jit(solution)/shard_map/ppermute | solution.py:529
  35.9 15.5 %collective-permute-start.7 = (bf16[576,256]{1,0:T(8,128)(2,1)S(1)}, bf16[576,256]{1,0:T(8,128)(2,1)S(1)}, u32[]{:S(2)}, u32[]{:S(2)}) collective-permute-start(bf16[576,256]{1,0:T(8,128)(2,1)S(1)} %get-tuple-element.73), channel_id=1, source_target_pairs={{0,112},{16,0},{32,16},{48,32},{64,48},{80,64},{96,80},{112,96},{1... | collective-permute-start | bytes 884744 | tf_op jit(solution)/shard_map/ppermute | solution.py:529
  37.2 14.1 %collective-permute-start.8 = (bf16[576,256]{1,0:T(8,128)(2,1)S(1)}, bf16[576,256]{1,0:T(8,128)(2,1)S(1)}, u32[]{:S(2)}, u32[]{:S(2)}) collective-permute-start(bf16[576,256]{1,0:T(8,128)(2,1)S(1)} %get-tuple-element.72), channel_id=1, source_target_pairs={{0,16},{16,32},{32,48},{48,64},{64,80},{80,96},{96,112},{112,0},{1... | collective-permute-start | bytes 884744 | tf_op jit(solution)/shard_map/ppermute | solution.py:529
  40.1 16.2 %collective-permute-start.14 = (bf16[256,512]{1,0:T(8,128)(2,1)S(1)}, bf16[256,512]{1,0:T(8,128)(2,1)S(1)}, u32[]{:S(2)}, u32[]{:S(2)}) collective-permute-start(bf16[256,512]{1,0:T(8,128)(2,1)S(1)} %constant_dynamic-update-slice_fusion.refs_0_.refs_8_), channel_id=1, source_target_pairs={{0,12},{4,0},{8,4},{12,8},{1,13},{5,1},{9,5},{13,9},{2,14},{6,2},{... | collective-permute-start | bytes 786440 | tf_op jit(solution)/shard_map/ppermute | solution.py:529
  43.6 12.7 %collective-permute-start.15 = (bf16[256,512]{1,0:T(8,128)(2,1)S(1)}, bf16[256,512]{1,0:T(8,128)(2,1)S(1)}, u32[]{:S(2)}, u32[]{:S(2)}) collective-permute-start(bf16[256,512]{1,0:T(8,128)(2,1)S(1)} %constant_dynamic-update-slice_fusion.refs_0_.refs_8_), channel_id=1, source_target_pairs={{0,8},{4,12},{8,0},{12,4},{1,9},{5,13},{9,1},{13,5},{2,10},{6,14},... | collective-permute-start | bytes 786440 | tf_op jit(solution)/shard_map/ppermute | solution.py:529
  49.6 10.3 %collective-permute-start.16 = (bf16[256,512]{1,0:T(8,128)(2,1)S(1)}, bf16[256,512]{1,0:T(8,128)(2,1)S(1)}, u32[]{:S(2)}, u32[]{:S(2)}) collective-permute-start(bf16[256,512]{1,0:T(8,128)(2,1)S(1)} %constant_dynamic-update-slice_fusion.refs_0_.refs_8_), channel_id=1, source_target_pairs={{0,4},{4,8},{8,12},{12,0},{1,5},{5,9},{9,13},{13,1},{2,6},{6,10},{... | collective-permute-start | bytes 786440 | tf_op jit(solution)/shard_map/ppermute | solution.py:529
  60.3 4.9 %collective-permute-start.17 = (f32[6,2048]{1,0:T(8,128)S(1)}, f32[6,2048]{1,0:T(8,128)S(1)}, u32[]{:S(2)}, u32[]{:S(2)}) collective-permute-start(f32[6,2048]{1,0:T(8,128)S(1)} %weighted.1.refs_0_), channel_id=1, source_target_pairs={{0,12},{4,0},{8,4},{12,8},{1,13},{5,1},{9,5},{13,9},{2,14},{6,2},{... | collective-permute-start | bytes 147464 | tf_op jit(solution)/shard_map/ppermute | solution.py:529
  60.4 6.0 %collective-permute-start.18 = (f32[6,2048]{1,0:T(8,128)S(1)}, f32[6,2048]{1,0:T(8,128)S(1)}, u32[]{:S(2)}, u32[]{:S(2)}) collective-permute-start(f32[6,2048]{1,0:T(8,128)S(1)} %weighted.1.refs_0_), channel_id=1, source_target_pairs={{0,8},{4,12},{8,0},{12,4},{1,9},{5,13},{9,1},{13,5},{2,10},{6,14},... | collective-permute-start | bytes 147464 | tf_op jit(solution)/shard_map/ppermute | solution.py:529
  63.6 5.5 %collective-permute-start.19 = (f32[6,2048]{1,0:T(8,128)S(1)}, f32[6,2048]{1,0:T(8,128)S(1)}, u32[]{:S(2)}, u32[]{:S(2)}) collective-permute-start(f32[6,2048]{1,0:T(8,128)S(1)} %weighted.1.refs_0_), channel_id=1, source_target_pairs={{0,4},{4,8},{8,12},{12,0},{1,5},{5,9},{9,13},{13,1},{2,6},{6,10},{... | collective-permute-start | bytes 147464 | tf_op jit(solution)/shard_map/ppermute | solution.py:529
  73.6 15.1 %collective-permute-start.20 = (bf16[512,256]{1,0:T(8,128)(2,1)S(1)}, bf16[512,256]{1,0:T(8,128)(2,1)S(1)}, u32[]{:S(2)}, u32[]{:S(2)}) collective-permute-start(bf16[512,256]{1,0:T(8,128)(2,1)S(1)} %get-tuple-element.55), channel_id=1, source_target_pairs={{0,16},{16,32},{32,48},{48,64},{64,80},{80,96},{96,112},{112,0},{1... | collective-permute-start | bytes 786440 | tf_op jit(solution)/shard_map/ppermute | solution.py:529
  73.7 15.0 %collective-permute-start.21 = (bf16[512,256]{1,0:T(8,128)(2,1)S(1)}, bf16[512,256]{1,0:T(8,128)(2,1)S(1)}, u32[]{:S(2)}, u32[]{:S(2)}) collective-permute-start(bf16[512,256]{1,0:T(8,128)(2,1)S(1)} %get-tuple-element.57), channel_id=1, source_target_pairs={{0,112},{16,0},{32,16},{48,32},{64,48},{80,64},{96,80},{112,96},{1... | collective-permute-start | bytes 786440 | tf_op jit(solution)/shard_map/ppermute | solution.py:529
  84.0 15.0 %collective-permute-start.25 = (bf16[256,256]{1,0:T(8,128)(2,1)S(1)}, bf16[256,256]{1,0:T(8,128)(2,1)S(1)}, u32[]{:S(2)}, u32[]{:S(2)}) collective-permute-start(bf16[256,256]{1,0:T(8,128)(2,1)S(1)} %get-tuple-element.64), channel_id=1, source_target_pairs={{0,64},{16,80},{32,96},{48,112},{64,0},{80,16},{96,32},{112,48},{1... | collective-permute-start | bytes 393224 | tf_op jit(solution)/shard_map/ppermute | solution.py:529
  88.7 17.3 %collective-permute-start.22 = (bf16[256,512]{1,0:T(8,128)(2,1)S(1)}, bf16[256,512]{1,0:T(8,128)(2,1)S(1)}, u32[]{:S(2)}, u32[]{:S(2)}) collective-permute-start(bf16[256,512]{1,0:T(8,128)(2,1)S(1)} %get-tuple-element.59), channel_id=1, source_target_pairs={{0,4},{4,8},{8,12},{12,0},{1,5},{5,9},{9,13},{13,1},{2,6},{6,10},{... | collective-permute-start | bytes 786440 | tf_op jit(solution)/shard_map/ppermute | solution.py:529
  88.8 17.2 %collective-permute-start.23 = (bf16[256,512]{1,0:T(8,128)(2,1)S(1)}, bf16[256,512]{1,0:T(8,128)(2,1)S(1)}, u32[]{:S(2)}, u32[]{:S(2)}) collective-permute-start(bf16[256,512]{1,0:T(8,128)(2,1)S(1)} %get-tuple-element.60), channel_id=1, source_target_pairs={{0,8},{4,12},{8,0},{12,4},{1,9},{5,13},{9,1},{13,5},{2,10},{6,14},... | collective-permute-start | bytes 786440 | tf_op jit(solution)/shard_map/ppermute | solution.py:529
  92.9 13.2 %collective-permute-start.24 = (bf16[256,512]{1,0:T(8,128)(2,1)S(1)}, bf16[256,512]{1,0:T(8,128)(2,1)S(1)}, u32[]{:S(2)}, u32[]{:S(2)}) collective-permute-start(bf16[256,512]{1,0:T(8,128)(2,1)S(1)} %get-tuple-element.61), channel_id=1, source_target_pairs={{0,12},{4,0},{8,4},{12,8},{1,13},{5,1},{9,5},{13,9},{2,14},{6,2},{... | collective-permute-start | bytes 786440 | tf_op jit(solution)/shard_map/ppermute | solution.py:529
  93.1 10.0 %collective-permute-start.26 = (bf16[256,256]{1,0:T(8,128)(2,1)S(1)}, bf16[256,256]{1,0:T(8,128)(2,1)S(1)}, u32[]{:S(2)}, u32[]{:S(2)}) collective-permute-start(bf16[256,256]{1,0:T(8,128)(2,1)S(1)} %get-tuple-element.65), channel_id=1, source_target_pairs={{0,32},{16,48},{32,64},{48,80},{64,96},{80,112},{96,0},{112,16},{1... | collective-permute-start | bytes 393224 | tf_op jit(solution)/shard_map/ppermute | solution.py:529
  99.0 7.0 %collective-permute-start.27 = (bf16[256,256]{1,0:T(8,128)(2,1)S(1)}, bf16[256,256]{1,0:T(8,128)(2,1)S(1)}, u32[]{:S(2)}, u32[]{:S(2)}) collective-permute-start(bf16[256,256]{1,0:T(8,128)(2,1)S(1)} %get-tuple-element.66), channel_id=1, source_target_pairs={{0,96},{16,112},{32,0},{48,16},{64,32},{80,48},{96,64},{112,80},{1... | collective-permute-start | bytes 393224 | tf_op jit(solution)/shard_map/ppermute | solution.py:529
  106.3 5.8 %collective-permute-start.28 = (bf16[128,768]{1,0:T(8,128)(2,1)S(1)}, bf16[128,768]{1,0:T(8,128)(2,1)S(1)}, u32[]{:S(2)}, u32[]{:S(2)}) collective-permute-start(bf16[128,768]{1,0:T(8,128)(2,1)S(1)} %get-tuple-element.68), channel_id=1, source_target_pairs={{0,128},{128,0},{1,129},{129,1},{2,130},{130,2},{3,131},{131,3},{4... | collective-permute-start | bytes 589832 | tf_op jit(solution)/shard_map/ppermute | solution.py:529
